TPU v7x, 32 devices: a whole 2x2x4 slice. The times are simulated.
32 devices in a mesh: wide: 8 (over y, x, core), blk: 4 (over z).
Axes of the slice: x: 2, y: 2, z: 4, core: 2. Of those that a mesh axis runs over, the one named last changes fastest.
Arguments:
- hidden: bfloat16 [4, 64, 8192], P('blk', 'wide'), may hold values from -400 to 400, as said below
- norm_gain: float32 [8192], replicated, may hold values from 0.1 to 1.9
- w_query: bfloat16 [8192, 8192], P('blk', 'wide'), may hold values from -0.0625 to 0.0625
- key_weight_matrix: bfloat16 [8192, 1024], P('blk'), may hold values from -0.0625 to 0.0625
- value_weight_matrix: bfloat16 [8192, 1024], P('blk'), may hold values from -0.0625 to 0.0625
- cache_key: bfloat16 [8192, 1024], P('blk'), may hold values from -90 to 90
- prefix_value_cache: bfloat16 [8192, 1024], P('blk'), may hold values from -5 to 5
- start: int32 [1], replicated, may hold values from 8192 to 130816
- reach: int32 [4, 64], P('blk'), may hold values from 0 to 8447
- passkey: int32 [16], replicated, may hold values from 0 to 8191
Outputs:
- attended: bfloat16 [4, 64, 8192], P('blk', 'wide')
Inputs may be any that keep to these rules, and one draw needn't show every extreme that they name: hidden states of order one up to row and feature scales.
All inputs are finite; a program needn't handle non-finite values.
Results may differ from a plain program's by a relative error of at most 0.017.
The roundings to bfloat16 on the way count: a program that leaves them out, or rounds other values in their place, can miss the bound.
Values may be sent and summed in bfloat16 or wider, within the bound.
No kernel may reach another device: no remote copies, remote signals or barrier semaphores. Data moves between devices by JAX's collectives and lax.ppermute only.
A program may use at most 128 MiB of HBM per device.

v0:
```python
import math

import jax
import jax.numpy as jnp
from jax import lax
from jax.sharding import PartitionSpec as P

QUERY_HEADS = 64
KEY_VALUE_HEADS = 8
HEAD_WIDTH = 128


rope_base = 500000.0
yarn_factor = 8.0
trained_context = 8192.0
fast_turns = 32.0
slow_turns = 1.0
masked_score = -1e30


def shifted(block, axis, distance):
    devices = range(lax.axis_size(axis))
    route = [((i - distance) % len(devices), i) for i in devices]
    return lax.ppermute(block, axis, route)


def yarn_tables(positions, head_size):
    half = head_size // 2
    log_base = math.log(rope_base)
    lowest = math.floor(
        head_size * math.log(trained_context / (fast_turns * 2.0 * math.pi)) / (2.0 * log_base)
    )
    highest = math.ceil(
        head_size * math.log(trained_context / (slow_turns * 2.0 * math.pi)) / (2.0 * log_base)
    )
    spread = max(highest - lowest, 1)
    counter = jnp.arange(half, dtype=jnp.float32)
    inverse = jnp.exp(-(2.0 * counter / head_size) * log_base)
    ramp = jnp.clip((counter - lowest) / spread, 0.0, 1.0)
    mixed = inverse / yarn_factor * ramp + inverse * (1.0 - ramp)
    angles = positions.astype(jnp.float32)[:, None] * mixed[None, :]
    mscale = 0.1 * math.log(yarn_factor) + 1.0
    return (jnp.cos(angles) * mscale, jnp.sin(angles) * mscale)


def apply_rotary(matrix, heads, cosine_table, sine_table):
    count = matrix.shape[0]
    shaped = matrix.reshape(count, heads, -1)
    half = shaped.shape[2] // 2
    front = shaped[:, :, :half]
    back = shaped[:, :, half:]
    cosine_table = cosine_table[:, None, :]
    sine_table = sine_table[:, None, :]
    turned = jnp.concatenate(
        [front * cosine_table - back * sine_table, back * cosine_table + front * sine_table], axis=2
    )
    return turned.reshape(count, heads * 2 * half)


def local(
    hidden,
    norm_gain,
    w_query,
    key_weight_matrix,
    value_weight_matrix,
    cache_key,
    prefix_value_cache,
    start,
    reach,
    passkey,
):
    blocks = lax.axis_size("blk")
    groups = lax.axis_size("wide")
    block_id = lax.axis_index("blk")
    group_number = lax.axis_index("wide")
    qcols = w_query.shape[1]
    query_head_rows = QUERY_HEADS // groups
    head_of_value = group_number * query_head_rows // (QUERY_HEADS // KEY_VALUE_HEADS)
    tokens = hidden[0].astype(jnp.float32)
    inv_rms = lax.rsqrt(jnp.mean(tokens * tokens, axis=1, keepdims=True) + 1e-05)
    normed = (tokens * inv_rms * norm_gain[None, :]).astype(jnp.bfloat16)[None]
    head_base = head_of_value * HEAD_WIDTH
    key_cols = lax.dynamic_slice_in_dim(key_weight_matrix, head_base, HEAD_WIDTH, 1)
    value_cols = lax.dynamic_slice_in_dim(value_weight_matrix, head_base, HEAD_WIDTH, 1)
    kv_width = key_cols.shape[1]
    sliced = lax.all_to_all(normed, "blk", split_axis=2, concat_axis=0, tiled=True)
    spread = lax.all_gather(sliced, "wide", axis=1, tiled=True)
    local_weights = jnp.concatenate([w_query, key_cols, value_cols], axis=1)
    summed = lax.psum_scatter(
        jnp.einsum("btd,dc->btc", spread, local_weights, preferred_element_type=jnp.float32),
        "blk",
        scatter_dimension=0,
        tiled=True,
    )[0]
    query_raw = summed[:, :qcols]
    unrotated_key = summed[:, qcols : qcols + kv_width]
    value_raw = summed[:, qcols + kv_width :]
    tokens_block = summed.shape[0]
    positions = start[0] + block_id * tokens_block + jnp.arange(tokens_block, dtype=jnp.int32)
    cosine_table, sine_table = yarn_tables(positions, HEAD_WIDTH)
    query = apply_rotary(query_raw, query_head_rows, cosine_table, sine_table).astype(jnp.bfloat16)
    window_key_rows = apply_rotary(unrotated_key, 1, cosine_table, sine_table).astype(jnp.bfloat16)
    value_new = value_raw.astype(jnp.bfloat16)
    queries = (
        query.reshape(tokens_block, query_head_rows, HEAD_WIDTH)
        .transpose(1, 0, 2)
        .reshape(query_head_rows * tokens_block, HEAD_WIDTH)
    )
    cache_rows = cache_key.shape[0]
    cache_total = cache_rows * blocks
    own_index = cache_total + block_id * tokens_block + jnp.arange(tokens_block, dtype=jnp.int32)
    query_index = jnp.tile(own_index, query_head_rows)
    query_reach = jnp.tile(reach[0], query_head_rows)
    cache_keys = lax.dynamic_slice_in_dim(cache_key, head_base, HEAD_WIDTH, 1)
    cache_values = lax.dynamic_slice_in_dim(prefix_value_cache, head_base, HEAD_WIDTH, 1)
    key_block = jnp.concatenate([cache_keys, window_key_rows], axis=0)
    value_block = jnp.concatenate([cache_values, value_new], axis=0)
    pair_block = jnp.stack([key_block, value_block], axis=0)[None]
    pair_len = cache_rows + tokens_block
    inv_sqrt = 1.0 / math.sqrt(HEAD_WIDTH)

    def attend(carry, pieces, first_operand):
        best, total, summed_values = carry
        count = pieces.shape[0]
        source = first_operand + jnp.arange(count, dtype=jnp.int32)[:, None]
        offset = jnp.arange(pair_len, dtype=jnp.int32)[None, :]
        in_cache = offset < cache_rows
        cache_index = source * cache_rows + offset
        key_index = jnp.where(
            in_cache, cache_index, cache_total + source * tokens_block + offset - cache_rows
        )
        pinned = in_cache & jnp.any(cache_index[:, :, None] == passkey[None, None, :], axis=2)
        key_index = key_index.reshape(count * pair_len)
        pinned = pinned.reshape(count * pair_len)
        keys_flat = pieces[:, 0].reshape(count * pair_len, HEAD_WIDTH)
        values_flat = pieces[:, 1].reshape(count * pair_len, HEAD_WIDTH)
        scores = (
            lax.dot_general(
                queries, keys_flat, (((1,), (1,)), ((), ())), preferred_element_type=jnp.float32
            )
            * inv_sqrt
        )
        visible = (key_index[None, :] <= query_index[:, None]) & (
            (key_index[None, :] >= query_index[:, None] - query_reach[:, None]) | pinned[None, :]
        )
        scores = jnp.where(visible, scores, masked_score)
        fresh = jnp.maximum(best, jnp.max(scores, axis=1))
        decay = jnp.exp(best - fresh)
        weights = jnp.where(visible, jnp.exp(scores - fresh[:, None]), 0.0)
        total = total * decay + jnp.sum(weights, axis=1)
        summed_values = summed_values * decay[:, None] + jnp.dot(
            weights.astype(jnp.bfloat16), values_flat, preferred_element_type=jnp.float32
        )
        return (fresh, total, summed_values)

    query_rows = query_head_rows * tokens_block
    initial_state = (
        jnp.full((query_rows,), masked_score, jnp.float32),
        jnp.zeros((query_rows,), jnp.float32),
        jnp.zeros((query_rows, HEAD_WIDTH), jnp.float32),
    )
    state = attend(initial_state, pair_block, block_id)

    def turn(step, loop_state):
        carry, travelling = loop_state
        travelling = shifted(travelling, "blk", 1)
        source_block = (block_id - step - 1) % blocks
        return (attend(carry, travelling, source_block), travelling)

    state, _ = lax.fori_loop(0, blocks - 1, turn, (state, pair_block))
    best, total, summed_values = state
    heads_out = (summed_values / total[:, None]).astype(jnp.bfloat16)
    heads_out = (
        heads_out.reshape(query_head_rows, tokens_block, HEAD_WIDTH)
        .transpose(1, 0, 2)
        .reshape(1, tokens_block, qcols)
    )
    return lax.all_to_all(heads_out, "wide", split_axis=1, concat_axis=2, tiled=True)


def solution(mesh):
    return jax.shard_map(
        local,
        mesh=mesh,
        in_specs=(
            P("blk", "wide", None),
            P(),
            P("blk", "wide"),
            P("blk", None),
            P("blk", None),
            P("blk", None),
            P("blk", None),
            P(),
            P("blk", None),
            P(),
        ),
        out_specs=P("blk", "wide", None),
        check_vma=False,
    )
```

profile of v0, /device:TPU:0, one launch (start us, length us, event | category | flops | bytes accessed | tf_op | source)
XLA Modules:
  0.0 274.0 jit_solution(11445664194508917927)
XLA Ops:
  6.5 1.1 fusion.32
  7.6 1.0 fusion.34
  8.6 6.7 %copy.39 = bf16[1,8,8192]{1,0,2:T(2,128)(2,1)} copy(bf16[1,8,8192]{2,1,0:T(8,128)(2,1)S(1)} %fusion.34) | data formatting | bytes 262144 | tf_op jit(solution)/shard_map/convert_element_type | solution.py:81
  15.4 0.5 broadcast.420
  15.9 45.2 %reduce.8 = bf16[8192,8]{1,0:T(8,128)(2,1)S(1)} reduce(bf16[8192,1,8]{2,1,0:T(2,128)(2,1)} %bitcast.67, bf16[]{:T(256)} %broadcast.420), dimensions={1}, to_apply=%bitcast.49.reduce_sub_computation | reduce | bytes 262146
  61.1 2.2 reshape.416
  63.3 12.2 %all_to_all.36 = bf16[4,2,8192]{2,1,0:T(2,128)(2,1)S(1)} all-to-all(bf16[4,2,8192]{2,1,0:T(2,128)(2,1)S(1)} %reshape.416), channel_id=1, replica_groups=mesh['wide'=8,'blk'=4] {'blk'}, dimensions={0} | all-to-all | bytes 262144 | tf_op jit(solution)/shard_map/all_to_all | solution.py:86
  75.5 5.9 %reshape.417 = bf16[8192,1,8]{2,1,0:T(2,128)(2,1)} reshape(bf16[4,2,8192]{2,1,0:T(2,128)(2,1)S(1)} %all_to_all.36) | data formatting | bytes 262144
  81.4 8.6 %copy.40 = bf16[1,8,8192]{2,1,0:T(8,128)(2,1)} copy(bf16[1,8,8192]{1,0,2:T(2,128)(2,1)} %bitcast.68) | data formatting | bytes 262144 | tf_op jit(solution)/shard_map/all_to_all | solution.py:86
  90.0 0.2 reduce-scatter.2.cloned.1.call-start
  90.2 1.3 constant_dynamic-slice_fusion.2
  91.6 21.2 %all-gather.3.cloned.1.call-done = bf16[4,1,64,2048]{3,2,0,1:T(8,128)(2,1)} async-done(((bf16[4,1,8,2048]{3,2,0,1:T(8,128)(2,1)}), bf16[4,1,64,2048]{3,2,0,1:T(8,128)(2,1)}) %all-gather.3.cloned.1.call-update) | async-done | bytes 1048592 | tf_op jit(solution)/shard_map/all_gather | solution.py:87
  112.7 5.1 %fusion.16 = f32[4,64,1280]{2,1,0:T(8,128)} fusion(bf16[2048,128]{1,0:T(8,128)(2,1)S(1)} %get-tuple-element.317, bf16[2048,128]{1,0:T(8,128)(2,1)S(1)} %get-tuple-element.318, bf16[2048,1024]{1,0:T(8,128)(2,1)} %param.14, bf16[4,1,64,2048]{3,2,0,1:T(8,128)(2,1)} %all-gather.3.cloned.1.call-done), kind=kOutput, calls=%fused_computation.23 | convolution fusion | flops 1357905920 | bytes 7602176 | tf_op jit(solution)/shard_map/btd,dc->btc/dot_general | solution.py:90
  118.8 0.1 compare_reduce_fusion.1
  118.9 0.2 fusion.35
  119.1 1.3 constant_dynamic-slice_fusion
  120.4 28.9 %reduce-scatter.2.cloned.1.call-done = f32[1,64,1280]{2,1,0:T(8,128)} async-done(((f32[4,64,1280]{2,1,0:T(8,128)}), f32[1,64,1280]{2,1,0:T(8,128)}) %reduce-scatter.2.cloned.1.call-update) | async-done | bytes 327696 | tf_op jit(solution)/shard_map/reduce_scatter | solution.py:89
  149.3 0.8 slice_bitcast_fusion.9
  150.0 0.8 slice.89
  150.8 1.0 slice_bitcast_fusion.8
  151.8 0.2 fusion.41
  152.0 0.2 subtract_convert_fusion
  152.2 0.1 maximum_bitcast_fusion.5
  152.5 0.1 maximum_bitcast_fusion.2
  152.6 1.6 fusion.57
  154.2 2.2 fusion.23
  156.4 2.0 fusion.28
  158.4 97.2 %while.22 = (s32[]{:T(128)}, f32[512]{0:T(512)S(1)}, f32[512]{0:T(512)S(1)}, f32[512,128]{1,0:T(8,128)S(1)}, bf16[1,2,2112,128]{3,2,1,0:T(8,128)(2,1)S(1)}, /*in...) while((s32[]{:T(128)}, f32[512]{0:T(512)S(1)}, ...), condition=%wide.region_9.10_spmd.clone, body=%wide.region_5.9_spmd.clone.sunk | while | flops 576570880 | bytes 21332160 | solution.py:170
  158.7 0.1 compare_reduce_fusion.3
  158.8 26.9 %collective-permute-done = bf16[1,2,2112,128]{3,2,1,0:T(8,128)(2,1)S(1)} collective-permute-done((bf16[1,2,2112,128]{3,2,1,0:T(8,128)(2,1)S(1)}, bf16[1,2,2112,128]{3,2,1,0:T(8,128)(2,1)S(1)}, u32[]{:S(2)}, u32[]{:S(2)}) %collective-permute-start) | collective-permute-done | bytes 1081376 | tf_op jit(solution)/shard_map/while/body/eval_jaxpr/ppermute | solution.py:24
  185.7 1.6 fusion.69
  187.3 2.2 fusion.70
  189.6 2.1 fusion.71
  192.0 0.1 compare_reduce_fusion.3
  192.1 26.0 %collective-permute-done = bf16[1,2,2112,128]{3,2,1,0:T(8,128)(2,1)S(1)} collective-permute-done((bf16[1,2,2112,128]{3,2,1,0:T(8,128)(2,1)S(1)}, bf16[1,2,2112,128]{3,2,1,0:T(8,128)(2,1)S(1)}, u32[]{:S(2)}, u32[]{:S(2)}) %collective-permute-start) | collective-permute-done | bytes 1081376 | tf_op jit(solution)/shard_map/while/body/eval_jaxpr/ppermute | solution.py:24
  218.1 1.6 fusion.69
  219.7 2.2 fusion.70
  222.0 2.1 fusion.71
  224.4 0.1 compare_reduce_fusion.3
  224.5 25.1 %collective-permute-done = bf16[1,2,2112,128]{3,2,1,0:T(8,128)(2,1)S(1)} collective-permute-done((bf16[1,2,2112,128]{3,2,1,0:T(8,128)(2,1)S(1)}, bf16[1,2,2112,128]{3,2,1,0:T(8,128)(2,1)S(1)}, u32[]{:S(2)}, u32[]{:S(2)}) %collective-permute-start) | collective-permute-done | bytes 1081376 | tf_op jit(solution)/shard_map/while/body/eval_jaxpr/ppermute | solution.py:24
  249.6 1.6 fusion.69
  251.2 2.2 fusion.70
  253.5 2.1 fusion.71
  255.6 0.1 divide_convert_fusion
  255.9 1.4 reduce.9
  257.4 9.0 %all_to_all.37 = bf16[8,2,4096]{2,1,0:T(2,128)(2,1)S(1)} all-to-all(bf16[8,2,4096]{2,1,0:T(2,128)(2,1)S(1)} %reshape.418), channel_id=1, replica_groups=mesh['wide'=8,'blk'=4] {'wide'}, dimensions={0} | all-to-all | bytes 262144 | tf_op jit(solution)/shard_map/all_to_all | solution.py:178
  266.3 0.1 reshape.419
  266.5 0.7 copy.45
  (64 shorter events, 1.7 us)
Async XLA Ops:
  6.5 106.2 %all-gather.3.cloned.1.call-start = ((), (), s32[]{:S(2)}) async-start(), calls=%async_computation.4 | async-start | bytes 1179648 | tf_op jit(solution)/shard_map/all_gather | solution.py:87
  90.0 59.3 %reduce-scatter.2.cloned.1.call-start = ((), (), s32[]{:S(2)}) async-start(), calls=%async_computation.3 | async-start | bytes 1638400 | tf_op jit(solution)/shard_map/reduce_scatter | solution.py:89
  112.7 5.8 %copy-start.1 = (s32[1,64]{1,0:T(1,128)S(1)}, s32[1,64]{1,0:T(1,128)}, u32[]{:S(2)}) copy-start(s32[1,64]{1,0:T(1,128)} %param.20) | copy-start | bytes 772
  112.7 6.0 %copy-start = (s32[16]{0:T(128)S(1)}, s32[16]{0:T(128)}, u32[]{:S(2)}) copy-start(s32[16]{0:T(128)} %param.21) | copy-start | bytes 196
  158.4 27.3 %collective-permute-start = (bf16[1,2,2112,128]{3,2,1,0:T(8,128)(2,1)S(1)}, bf16[1,2,2112,128]{3,2,1,0:T(8,128)(2,1)S(1)}, u32[]{:S(2)}, u32[]{:S(2)}) collective-permute-start(bf16[1,2,2112,128]{3,2,1,0:T(8,128)(2,1)S(1)} %get-tuple-element.414), channel_id=1, source_target_pairs={{3,0},{0,1},{1,2},{2,3},{7,4},{4,5},{5,6},{6,7},{11,8},{8,9},{9,10... | collective-permute-start | bytes 3244040 | tf_op jit(solution)/shard_map/while/body/eval_jaxpr/ppermute | solution.py:24
  191.7 26.4 %collective-permute-start = (bf16[1,2,2112,128]{3,2,1,0:T(8,128)(2,1)S(1)}, bf16[1,2,2112,128]{3,2,1,0:T(8,128)(2,1)S(1)}, u32[]{:S(2)}, u32[]{:S(2)}) collective-permute-start(bf16[1,2,2112,128]{3,2,1,0:T(8,128)(2,1)S(1)} %get-tuple-element.414), channel_id=1, source_target_pairs={{3,0},{0,1},{1,2},{2,3},{7,4},{4,5},{5,6},{6,7},{11,8},{8,9},{9,10... | collective-permute-start | bytes 3244040 | tf_op jit(solution)/shard_map/while/body/eval_jaxpr/ppermute | solution.py:24
  224.1 25.5 %collective-permute-start = (bf16[1,2,2112,128]{3,2,1,0:T(8,128)(2,1)S(1)}, bf16[1,2,2112,128]{3,2,1,0:T(8,128)(2,1)S(1)}, u32[]{:S(2)}, u32[]{:S(2)}) collective-permute-start(bf16[1,2,2112,128]{3,2,1,0:T(8,128)(2,1)S(1)} %get-tuple-element.414), channel_id=1, source_target_pairs={{3,0},{0,1},{1,2},{2,3},{7,4},{4,5},{5,6},{6,7},{11,8},{8,9},{9,10... | collective-permute-start | bytes 3244040 | tf_op jit(solution)/shard_map/while/body/eval_jaxpr/ppermute | solution.py:24
Sparse Core Ops, SparseCore 0:
  90.1 22.5 all-gather.2
  118.0 31.2 reduce-scatter.1
where the time goes:
time: 275 us; the launch traced here: 274 us
  waiting for transfers between devices  128 us (47%)
  other arithmetic  59 us (21%)
  local copies, waits for them, and re-layouts  31 us (11%)
  blocking collectives  21.2 us (8%)
  matrix products  19.8 us (7%)
  between operations  14.3 us (5%)
    ppermute x3, waiting for transfers between devices, shifted(): return lax.ppermute(block, axis, route)  78 us
    unnamed x2, other arithmetic  46.5 us
    reduce_scatter x1, waiting for transfers between devices, local(): lax.psum_scatter(jnp.einsum('btd,dc->btc', spread, local_weights, preferr...  28.9 us
    all_gather x1, waiting for transfers between devices, local(): spread = lax.all_gather(sliced, 'wide', axis=1, tiled=True)  21.2 us
    all_to_all x1, blocking collectives, local(): lax.all_to_all(normed, 'blk', split_axis=2, concat_axis=0, tiled=True)  12.2 us
    unnamed x12, local copies, waits for them, and re-layouts  10.5 us
    all_to_all x1, blocking collectives, local(): lax.all_to_all(heads_out, 'wide', split_axis=1, concat_axis=2, tiled=True)  8.97 us
    reduce_sum x4, other arithmetic, attend(): total = total * decay + jnp.sum(weights, axis=1)  8.72 us
  transfers between devices with their start and end apart: 5, of which 5 were waited for; matrix products, arithmetic and copies ran while one was open for 1% of the time, Pallas kernels for 0%

commit v1 on v0

v1 whole, which is shorter than its diff:
```python
import functools
import math

import jax
import jax.numpy as jnp
from jax import lax
from jax.experimental import pallas as pl
from jax.experimental.pallas import tpu as pltpu
from jax.sharding import PartitionSpec as P

QUERY_HEADS = 64
KEY_VALUE_HEADS = 8
HEAD_WIDTH = 128
MEBI = 1024 * 1024
CHUNKS = 2

rope_base = 500000.0
yarn_factor = 8.0
trained_context = 8192.0
fast_turns = 32.0
slow_turns = 1.0
masked_score = -1e30
lowest_max = -1e29
F32 = jnp.float32
BF16 = jnp.bfloat16


def yarn_tables(positions, head_size):
    half = head_size // 2
    log_base = math.log(rope_base)
    lowest = math.floor(
        head_size * math.log(trained_context / (fast_turns * 2.0 * math.pi)) / (2.0 * log_base)
    )
    highest = math.ceil(
        head_size * math.log(trained_context / (slow_turns * 2.0 * math.pi)) / (2.0 * log_base)
    )
    spread = max(highest - lowest, 1)
    counter = jnp.arange(half, dtype=jnp.float32)
    inverse = jnp.exp(-(2.0 * counter / head_size) * log_base)
    ramp = jnp.clip((counter - lowest) / spread, 0.0, 1.0)
    mixed = inverse / yarn_factor * ramp + inverse * (1.0 - ramp)
    angles = positions.astype(jnp.float32)[:, None] * mixed[None, :]
    mscale = 0.1 * math.log(yarn_factor) + 1.0
    return (jnp.cos(angles) * mscale, jnp.sin(angles) * mscale)


def swapped(block, axis, mask):
    return lax.ppermute(block, axis, [(i, i ^ mask) for i in range(lax.axis_size(axis))])


def params(*arrays):
    held = sum(math.prod(a.shape) * jnp.dtype(a.dtype).itemsize for a in arrays)
    return pltpu.CompilerParams(vmem_limit_bytes=min(56 * MEBI, 4 * MEBI + held))


def vmem(count=1):
    return [pl.BlockSpec(memory_space=pltpu.VMEM)] * count


def smem():
    return pl.BlockSpec(memory_space=pltpu.SMEM)


def norm_kernel(ids, hidden, gain, reach, *rest):
    outs, scratch = rest[:-1], rest[-1]
    rows, width = outs[0].shape
    x = hidden[0].astype(F32)
    inv_rms = lax.rsqrt(jnp.mean(x * x, axis=1, keepdims=True) + 1e-05)
    scratch[...] = x * inv_rms * gain[...]
    digits = jnp.concatenate([reach[...] >> 7, reach[...] & 127], axis=1).astype(F32)
    digits = jnp.broadcast_to(digits, (rows, digits.shape[1])).astype(BF16)
    for d, out in enumerate(outs):
        at = pl.multiple_of((ids[0] ^ d) * width, width)
        out[:, :width] = scratch[:, pl.ds(at, width)].astype(BF16)
        if out.shape[1] > width:
            out[:, width:] = digits


def norm(ids, hidden, gain, reach, blocks):
    _, rows, features = hidden.shape
    width = features // blocks
    longer = width + 2 * reach.shape[1]
    widths = [longer if d and d % 2 == 0 else width for d in range(blocks)]
    return pl.pallas_call(
        norm_kernel,
        out_shape=[jax.ShapeDtypeStruct((rows, size), BF16) for size in widths],
        in_specs=[smem()] + vmem(3),
        out_specs=vmem(blocks),
        scratch_shapes=[pltpu.VMEM((rows, features), F32)],
        compiler_params=params(hidden, gain),
        name="norm",
    )(ids, hidden, gain, reach)


def prepare_kernel(keys, values, out):
    out[0] = keys[...]
    for at in range(0, values.shape[0], HEAD_WIDTH):
        part = values[at : at + HEAD_WIDTH].astype(F32)
        out[1, at : at + HEAD_WIDTH] = part.T.astype(BF16)


def prepare(keys, values):
    return pl.pallas_call(
        prepare_kernel,
        in_specs=vmem(2),
        out_specs=vmem()[0],
        out_shape=jax.ShapeDtypeStruct((2, *keys.shape), BF16),
        compiler_params=pltpu.CompilerParams(vmem_limit_bytes=6 * MEBI),
        name="prepare",
    )(keys, values)


def mask_kernel(cached, groups, ids, passkey, low, bias):
    half, count = low.shape
    rows = count // groups
    total = 2 * cached
    lows = jnp.concatenate([low[j : j + 1] for j in range(half)], axis=1)
    lanes = half * count

    def index_of(slot, block):
        token = ((slot // rows) ^ ids[1]) * rows + slot % rows
        return ids[3] + block * count + token

    step = min(256, cached)
    ramp = lax.broadcasted_iota(jnp.int32, (step, lanes), 0)
    for side in range(2):
        first = (ids[0] ^ side) * cached
        for at in range(0, cached, step):
            here = side * cached + at
            bias[here : here + step] = jnp.where(ramp >= lows - (first + at), 0.0, masked_score)
        for n in range(passkey.shape[0]):
            row = passkey[n] - first

            @pl.when((row >= 0) & (row < cached))
            def _():
                bias[pl.ds(side * cached + row, 1), :] = jnp.zeros((1, lanes), F32)

    slots = lax.broadcasted_iota(jnp.int32, (1, count), 1)
    queries = jnp.concatenate([index_of(slots, ids[0] ^ (2 * j)) for j in range(half)], axis=1)
    slots = lax.broadcasted_iota(jnp.int32, (count, 1), 0)
    for d in range(2):
        index = index_of(slots, ids[0] ^ d)
        bias[total + d * count : total + (d + 1) * count] = jnp.where(
            (index <= queries) & (index >= lows), 0.0, masked_score
        )


def mask(ids, passkey, low, cached, groups):
    half, count = low.shape
    shape = jax.ShapeDtypeStruct((2 * cached + 2 * count, half * count), F32)
    return pl.pallas_call(
        functools.partial(mask_kernel, cached, groups),
        out_shape=shape,
        in_specs=[smem(), smem()] + vmem(),
        out_specs=vmem()[0],
        compiler_params=params(shape),
        name="mask",
    )(ids, passkey, low)


def gather_kernel(groups, part, *refs):
    pieces = refs[:groups]
    weights, tokens, keep, send = refs[groups:]
    blocks, rows, width = pieces[0].shape
    count = groups * rows
    pair = 2 * HEAD_WIDTH
    for d in range(blocks):
        block = jnp.concatenate([piece[d].astype(F32) for piece in pieces], axis=0)
        tokens[d * count : (d + 1) * count] = block.astype(BF16)
    raw = jnp.dot(tokens[...], weights[:, part:], preferred_element_type=F32)
    for d in range(blocks):
        block = raw[d * count : (d + 1) * count]
        first, other = (send, keep) if d % 2 else (keep, send)
        first[d // 2, :, part : part + pair] = block
        other[d // 2, :, part + pair :] = block
    tile = min(256, part)
    for at in range(0, part, tile):
        raw = jnp.dot(tokens[...], weights[:, at : at + tile], preferred_element_type=F32)
        for d in range(blocks):
            out = send if d % 2 else keep
            out[d // 2, :, at : at + tile] = raw[d * count : (d + 1) * count]


def gather(pieces, weights, part):
    groups = len(pieces)
    blocks, rows, width = pieces[0].shape
    count = groups * rows
    columns = part + 4 * HEAD_WIDTH
    tokens = jax.ShapeDtypeStruct((blocks * count, width), BF16)
    out = jax.ShapeDtypeStruct((blocks // 2, count, columns), F32)
    return pl.pallas_call(
        functools.partial(gather_kernel, groups, part),
        out_shape=[tokens, out, out],
        in_specs=vmem(groups + 1),
        out_specs=vmem(3),
        compiler_params=params(tokens, tokens, weights, out, out),
        cost_estimate=pl.CostEstimate(
            flops=2 * blocks * count * width * columns,
            bytes_accessed=4 * blocks * count * width,
            transcendentals=0,
        ),
        name="gather",
    )(*pieces, weights)


def project_kernel(tokens, weights, keep, send):
    half, count, _ = keep.shape
    raw = jnp.dot(tokens[...], weights[...], preferred_element_type=F32)
    for j in range(half):
        keep[j] = raw[2 * j * count : (2 * j + 1) * count]
        send[j] = raw[(2 * j + 1) * count : (2 * j + 2) * count]


def project(tokens, weights, blocks, at, columns):
    rows, width = tokens.shape
    tile = min(256, columns)
    half, count = blocks // 2, rows // blocks
    out = jax.ShapeDtypeStruct((half, count, columns), F32)
    out_spec = pl.BlockSpec((half, count, tile), lambda n: (0, 0, n))
    return pl.pallas_call(
        project_kernel,
        grid=(columns // tile,),
        in_specs=[
            pl.BlockSpec((rows, width), lambda n: (0, 0)),
            pl.BlockSpec((width, tile), lambda n: (0, n + at // tile)),
        ],
        out_specs=[out_spec, out_spec],
        out_shape=[out, out],
        compiler_params=params(tokens, tokens, out, out, out, out),
        cost_estimate=pl.CostEstimate(
            flops=2 * rows * width * columns,
            bytes_accessed=2 * width * columns,
            transcendentals=0,
        ),
        name="project",
    )(tokens, weights)


def turned(x, cosine, sine):
    return x * cosine + pltpu.roll(x, HEAD_WIDTH // 2, 1) * sine


def attend_kernel(together, q, kv, cosine, sine, bias, own, far, _, o_keep,
                   o_send, stats_keep, scores, k_new, v_new, pair, arrived):
    fetch = pltpu.make_async_copy(far, pair, arrived)
    fetch.start()
    half, count, columns = q.shape
    rows = half * count
    cached = own.shape[1]
    window = 2 * count
    heads = columns // HEAD_WIDTH
    for d in range(2):
        raw = kv[d]
        k_new[d * count : (d + 1) * count] = turned(
            raw[:, :HEAD_WIDTH], cosine[d], sine[d]
        ).astype(BF16)
    values = jnp.concatenate([kv[d, :, HEAD_WIDTH:] for d in range(2)], axis=0)
    for at in range(0, window, HEAD_WIDTH):
        v_new[at : at + HEAD_WIDTH] = values[at : at + HEAD_WIDTH].T.astype(BF16)
    scale = math.log2(math.e) / math.sqrt(HEAD_WIDTH)
    chunk = min(256, cached)
    spans = [
        (base + at, chunk, held.at[0], held.at[1], at)
        for held, base in ((own, 0), (pair, cached))
        for at in range(0, cached, chunk)
    ]
    spans += [
        (2 * cached + at, HEAD_WIDTH, k_new, v_new, at) for at in range(0, window, HEAD_WIDTH)
    ]
    width = together * rows
    tops, sums = [], []
    for first in range(0, heads, together):
        queries = []
        for h in range(first, first + together):
            lanes = slice(h * HEAD_WIDTH, (h + 1) * HEAD_WIDTH)
            for j in range(half):
                queries.append(turned(q[j, :, lanes], cosine[2 * j], sine[2 * j]).astype(BF16))
        queries = jnp.concatenate(queries, axis=0)
        top = jnp.full((8, width), lowest_max, F32)
        for at, size, keys, _, start in spans:
            if first == 0 and at == cached:
                fetch.wait()
            product = lax.dot_general(
                keys[start : start + size],
                queries,
                (((1,), (1,)), ((), ())),
                preferred_element_type=F32,
            )
            hidden_part = bias[at : at + size]
            product = product * scale + jnp.concatenate([hidden_part] * together, axis=1)
            scores[at : at + size] = product
            top = jnp.maximum(top, jnp.max(product.reshape(size // 8, 8, width), axis=0))
        top = jnp.max(top, axis=0, keepdims=True)
        total = jnp.zeros((8, width), F32)
        mixed = jnp.zeros((HEAD_WIDTH, width), F32)
        for at, size, _, held, start in spans:
            weights = jnp.exp2(scores[at : at + size] - top)
            total = total + jnp.sum(weights.reshape(size // 8, 8, width), axis=0)
            turned_values = jnp.concatenate(
                [held[start + c : start + c + HEAD_WIDTH] for c in range(0, size, HEAD_WIDTH)],
                axis=1,
            )
            mixed = mixed + jnp.dot(
                turned_values, weights.astype(BF16), preferred_element_type=F32
            )
        total = jnp.sum(total, axis=0, keepdims=True)
        mixed = mixed * (1.0 / jnp.maximum(total, 1e-30))
        for n in range(together):
            lanes = slice((first + n) * HEAD_WIDTH, (first + n + 1) * HEAD_WIDTH)
            tops.append(top[:, n * rows : (n + 1) * rows])
            sums.append(total[:, n * rows : (n + 1) * rows])
            upright = mixed[:, n * rows : (n + 1) * rows].T
            for j in range(half):
                part = upright[j * count : (j + 1) * count]
                if j < half // 2:
                    o_keep[j, :, lanes] = part
                else:
                    o_send[j - half // 2, :, lanes] = part.astype(BF16)
    stats = jnp.concatenate(tops + sums, axis=0)
    number = stats.shape[0]
    high = stats.astype(BF16).astype(F32)
    middle = (stats - high).astype(BF16).astype(F32)
    last = stats - high - middle
    stats = jnp.concatenate(
        [high, middle, last, jnp.zeros((HEAD_WIDTH - 3 * number, rows), F32)], axis=0
    ).T
    for j in range(half):
        part = stats[j * count : (j + 1) * count]
        if j < half // 2:
            stats_keep[j] = part
        else:
            o_send[j - half // 2, :, columns:] = part.astype(BF16)


def attend(q, kv, cosine, sine, bias, own, pair, before):
    half, count, columns = q.shape
    rows = half * count
    total = bias.shape[0]
    heads = columns // HEAD_WIDTH
    together = max(1, min(512 // rows, heads))
    out_half = half // 2
    outs = [
        jax.ShapeDtypeStruct((out_half, count, columns), F32),
        jax.ShapeDtypeStruct((out_half, count, columns + HEAD_WIDTH), BF16),
        jax.ShapeDtypeStruct((out_half, count, HEAD_WIDTH), F32),
    ]
    ins = (q, kv, cosine, sine, bias, own, pair, before)
    scores = jax.ShapeDtypeStruct((total, together * rows), F32)
    return pl.pallas_call(
        functools.partial(attend_kernel, together),
        out_shape=outs,
        in_specs=vmem(len(ins) - 2) + [pl.BlockSpec(memory_space=pl.ANY)] * 2,
        out_specs=vmem(3),
        scratch_shapes=[
            pltpu.VMEM(scores.shape, F32),
            pltpu.VMEM((2 * count, HEAD_WIDTH), BF16),
            pltpu.VMEM((2 * count, HEAD_WIDTH), BF16),
            pltpu.VMEM(pair.shape, BF16),
            pltpu.SemaphoreType.DMA(()),
        ],
        compiler_params=params(*ins, *outs, scores),
        cost_estimate=pl.CostEstimate(
            flops=16 * rows * columns * total,
            bytes_accessed=4 * rows * columns * 4,
            transcendentals=rows * heads * total,
        ),
        name="attend",
    )(*ins)


def merged(mine, other, mine_stats):
    columns = mine.shape[1]
    heads = columns // HEAD_WIDTH

    def read(stats):
        number = 2 * heads
        stats = (
            stats[:, :number] + stats[:, number : 2 * number] + stats[:, 2 * number : 3 * number]
        )
        return stats[:, :heads], stats[:, heads:]

    top_a, sum_a = read(mine_stats)
    top_b, sum_b = read(other[:, columns:].astype(F32))
    top = jnp.maximum(top_a, top_b)
    share_a = sum_a * jnp.exp2(top_a - top)
    share_b = sum_b * jnp.exp2(top_b - top)
    total = share_a + share_b
    scale = 1.0 / jnp.maximum(total, 1e-30)
    share_a = share_a * scale
    share_b = share_b * scale
    joined = [
        mine[:, h * HEAD_WIDTH : (h + 1) * HEAD_WIDTH] * share_a[:, h : h + 1]
        + other[:, h * HEAD_WIDTH : (h + 1) * HEAD_WIDTH].astype(F32) * share_b[:, h : h + 1]
        for h in range(heads)
    ]
    return joined, top, total


def merge_kernel(mine, other, mine_stats, keep, send, stats_keep):
    blocks, count, columns = mine.shape
    half = blocks // 2
    for n in range(blocks):
        joined, top, total = merged(mine[n], other[n], mine_stats[n])
        stats = jnp.concatenate([top, total], axis=1)
        high = stats.astype(BF16).astype(F32)
        middle = (stats - high).astype(BF16).astype(F32)
        number = stats.shape[1]
        stats = jnp.concatenate(
            [
                high,
                middle,
                stats - high - middle,
                jnp.zeros((count, HEAD_WIDTH - 3 * number), F32),
            ],
            axis=1,
        )
        for h, part in enumerate(joined):
            lanes = slice(h * HEAD_WIDTH, (h + 1) * HEAD_WIDTH)
            if n < half:
                keep[n, :, lanes] = part
            else:
                send[n - half, :, lanes] = part.astype(BF16)
        if n < half:
            stats_keep[n] = stats
        else:
            send[n - half, :, columns:] = stats.astype(BF16)


def merge(mine, other, mine_stats):
    blocks, count, columns = mine.shape
    half = blocks // 2
    return pl.pallas_call(
        merge_kernel,
        out_shape=[
            jax.ShapeDtypeStruct((half, count, columns), F32),
            jax.ShapeDtypeStruct((half, count, columns + HEAD_WIDTH), BF16),
            jax.ShapeDtypeStruct((half, count, HEAD_WIDTH), F32),
        ],
        in_specs=vmem(3),
        out_specs=vmem(3),
        compiler_params=params(mine, mine, other, mine_stats),
        name="merge",
    )(mine, other, mine_stats)


def finish_kernel(chunks, ids, *refs):
    out = refs[-1]
    groups, rows, _ = out.shape
    at = 0
    for c in range(chunks):
        mine, other, stats = refs[3 * c : 3 * c + 3]
        joined, _, _ = merged(mine[0], other[0], stats[0])
        for part in joined:
            for m in range(groups):
                out[ids[1] ^ m, :, at : at + HEAD_WIDTH] = part[m * rows : (m + 1) * rows].astype(
                    BF16
                )
            at += HEAD_WIDTH


def finish(ids, parts, groups):
    count = parts[0][0].shape[1]
    columns = sum(part[0].shape[2] for part in parts)
    flat = [array for part in parts for array in part]
    return pl.pallas_call(
        functools.partial(finish_kernel, len(parts)),
        out_shape=jax.ShapeDtypeStruct((groups, count // groups, columns), BF16),
        in_specs=[smem()] + vmem(len(flat)),
        out_specs=vmem()[0],
        compiler_params=params(*flat),
        name="finish",
    )(ids, *flat)


def reordered(array, flip):
    if not flip:
        return array
    return jnp.stack([array[j ^ flip] for j in range(array.shape[0])])


def local(
    hidden,
    norm_gain,
    w_query,
    key_weight_matrix,
    value_weight_matrix,
    cache_key,
    prefix_value_cache,
    start,
    reach,
    passkey,
):
    blocks = lax.axis_size("blk")
    groups = lax.axis_size("wide")
    b = lax.axis_index("blk").astype(jnp.int32)
    w = lax.axis_index("wide").astype(jnp.int32)
    rows, features = hidden.shape[1:]
    count = groups * rows
    half = blocks // 2
    heads = QUERY_HEADS // groups
    columns = w_query.shape[1]
    chunks = min(CHUNKS, heads)
    kv_head = w * heads // (QUERY_HEADS // KEY_VALUE_HEADS)
    cached = cache_key.shape[0]
    cache_total = cached * blocks
    ids = jnp.stack([b, w, kv_head, jnp.int32(cache_total)])
    largest = 1.9 * 0.0625 * features * 1.01
    fit = 2.0 ** math.floor(math.log2(65504.0 / largest))

    def narrow(array):
        return (array * fit).astype(jnp.float16)

    def widen(array):
        return array.astype(F32) * (1.0 / fit)

    slices = norm(ids, hidden, norm_gain[None, :], reach, blocks)
    sent = [swapped(slices[d], "blk", d) for d in range(1, blocks)]
    slices, cache_key, prefix_value_cache = lax.optimization_barrier(
        (slices, cache_key, prefix_value_cache)
    )
    base = kv_head * HEAD_WIDTH
    cache = prepare(
        lax.dynamic_slice_in_dim(cache_key, base, HEAD_WIDTH, 1),
        lax.dynamic_slice_in_dim(prefix_value_cache, base, HEAD_WIDTH, 1),
    )
    cache_pair = swapped(cache, "blk", 1)
    width = features // blocks
    own = jnp.stack([slices[0]] + [array[:, :width] for array in sent])
    own, first_weights, key_weight_matrix, value_weight_matrix = lax.optimization_barrier(
        (own, w_query, key_weight_matrix, value_weight_matrix)
    )

    pieces = [None] * groups
    for m in range(0, groups, 2):
        pieces[m] = swapped(own, "wide", m) if m else own
    for m in range(0, groups, 2):
        pieces[m + 1] = swapped(pieces[m], "wide", 1)

    weights = jnp.concatenate(
        [
            first_weights[:, : columns // chunks],
            lax.dynamic_slice_in_dim(key_weight_matrix, base, HEAD_WIDTH, 1),
            lax.dynamic_slice_in_dim(value_weight_matrix, base, HEAD_WIDTH, 1),
        ],
        axis=1,
    )

    token = (w ^ jnp.arange(groups, dtype=jnp.int32))[:, None] * rows + jnp.arange(
        rows, dtype=jnp.int32
    )
    token = token.reshape(count)
    block_of = b ^ jnp.arange(blocks, dtype=jnp.int32)
    place = block_of[:, None] * count + token[None, :]
    cosine, sine = yarn_tables(start[0] + place.reshape(-1), HEAD_WIDTH)
    cosine = jnp.concatenate([cosine, cosine], axis=1).reshape(blocks, count, HEAD_WIDTH)
    sine = jnp.concatenate([-sine, sine], axis=1).reshape(blocks, count, HEAD_WIDTH)
    digits = [array[0, width:].astype(jnp.int32) for array in sent[1::2]]
    reaches = jnp.stack(
        [reach[0]] + [array[:count] * 128 + array[count:] for array in digits]
    )
    natural = jnp.arange(count, dtype=jnp.int32)
    reaches = jnp.sum(
        jnp.where(token[None, :, None] == natural[None, None, :], reaches[:, None, :], 0), axis=2
    )
    bias = mask(ids, passkey, cache_total + place[::2] - reaches, cached, groups)

    part = columns // chunks
    tokens, *first = gather(pieces, weights, part)
    projected = [first] + [
        project(tokens, w_query, blocks, c * part, part) for c in range(1, chunks)
    ]
    pair = 2 * HEAD_WIDTH
    parts = []
    got = [swapped(narrow(send), "blk", 1) for _, send in projected]
    after = cosine
    for c, (keep, _) in enumerate(projected):
        keep = keep + widen(got[c])
        if c == 0:
            even = keep[:, :, part : part + pair]
            odd = keep[:, :, part + pair :]
            keep = keep[:, :, :part]
        bit = half // 2
        while bit >= 1:
            out = narrow(keep)
            if c == 0:
                extra = narrow(jnp.concatenate([even[bit:], odd[bit:]], axis=0))
                even, odd = even[:bit], odd[:bit]
                if 2 * bit == half:
                    out = jnp.concatenate([out, extra], axis=2)
                    other = swapped(out, "blk", 2 * bit)
                    other, extra = other[:, :, :part], other[:, :, part:]
                else:
                    other = swapped(out, "blk", 2 * bit)
                    extra = swapped(extra, "blk", 2 * bit)
                even = even + widen(extra[:bit])
                odd = odd + widen(extra[bit:])
            else:
                other = swapped(out, "blk", 2 * bit)
            keep = keep + reordered(widen(other), bit)
            bit //= 2
        if c == 0:
            kv = jnp.concatenate([even, odd], axis=0)
        keep, send, stats = attend(keep, kv, cosine, sine, bias, cache, cache_pair, after)
        after = stats
        bit = half // 2
        while bit > 1:
            keep, send, stats = merge(keep, swapped(send, "blk", 2 * bit), stats)
            bit //= 2
        parts.append((keep, swapped(send, "blk", 2), stats))
    ready = finish(ids, parts, groups)
    ready = lax.all_to_all(ready, "wide", split_axis=0, concat_axis=0, tiled=True)
    return ready.transpose(1, 0, 2).reshape(1, rows, groups * columns)


def solution(mesh):
    return jax.shard_map(
        local,
        mesh=mesh,
        in_specs=(
            P("blk", "wide", None),
            P(),
            P("blk", "wide"),
            P("blk", None),
            P("blk", None),
            P("blk", None),
            P("blk", None),
            P(),
            P("blk", None),
            P(),
        ),
        out_specs=P("blk", "wide", None),
        check_vma=False,
    )
```

time: 275 us -> 84.1 us (0.31)
  waiting for transfers between devices: 128 us -> 30 us
  other arithmetic: 59 us -> 4.12 us
  local copies, waits for them, and re-layouts: 31 us -> 7.72 us
  matrix products: 19.8 us -> 0 us
  starting transfers between devices: 0.4 us -> 18.3 us
  Pallas kernels: 0 us -> 13.5 us
  between operations: 14.3 us -> 0.98 us
  blocking collectives: 21.2 us -> 9.05 us
    ppermute x3 -> x17, waiting for transfers between devices: 78 us -> 30 us  [swapped(): lax.ppermute(block, axis, [(i, i ^ mask) for i in range(lax.axis_size(axi...]
    unnamed x2 -> x0, other arithmetic: 46.5 us -> none
    reduce_scatter x1 -> x0, waiting for transfers between devices: 28.9 us -> none  [local(): lax.psum_scatter(jnp.einsum('btd,dc->btc', spread, local_weights, preferr...]
    all_gather x1 -> x0, waiting for transfers between devices: 21.2 us -> none  [local(): spread = lax.all_gather(sliced, 'wide', axis=1, tiled=True)]
    dot_general x9 -> x0, matrix products: 19.8 us -> none  [the longest x4 8.45 us: attend(): jnp.dot(weights.astype(jnp.bfloat16), values_flat, preferred_element_type...]
    ppermute x3 -> x17, starting transfers between devices: 0.18 us -> 18.3 us  [swapped(): lax.ppermute(block, axis, [(i, i ^ mask) for i in range(lax.axis_size(axi...]
    pallas_call x0 -> x8, Pallas kernels: none -> 13.5 us  [the longest x2 7.99 us: attend(): pl.pallas_call(functools.partial(attend_kernel, together), out_shape=outs...]
    all_to_all x2 -> x1, blocking collectives: 21.2 us -> 9.05 us  [local(): lax.all_to_all(ready, 'wide', split_axis=0, concat_axis=0, tiled=True)]
  transfers between devices with their start and end apart: 5 -> 17, of which waited for: 5 -> 10; matrix products, arithmetic and copies ran while one was open for 1% -> 10% of each run, Pallas kernels for 0% -> 5%
where the time goes in v1:
time: 84.1 us; the launch traced here: 83.6 us
  waiting for transfers between devices  30 us (36%)
  starting transfers between devices  18.3 us (22%)
  Pallas kernels  13.5 us (16%)
  blocking collectives  9.05 us (11%)
  local copies, waits for them, and re-layouts  7.72 us (9%)
  other arithmetic  4.12 us (5%)
  between operations  0.98 us (1%)
    ppermute x17, waiting for transfers between devices, swapped(): lax.ppermute(block, axis, [(i, i ^ mask) for i in range(lax.axis_size(axi...  30 us
    ppermute x17, starting transfers between devices, swapped(): lax.ppermute(block, axis, [(i, i ^ mask) for i in range(lax.axis_size(axi...  18.3 us
    all_to_all x1, blocking collectives, local(): lax.all_to_all(ready, 'wide', split_axis=0, concat_axis=0, tiled=True)  9.05 us
    pallas_call x2, Pallas kernels, attend(): pl.pallas_call(functools.partial(attend_kernel, together), out_shape=outs...  7.99 us
    unnamed x15, local copies, waits for them, and re-layouts  2.99 us
  transfers between devices with their start and end apart: 17, of which 10 were waited for; matrix products, arithmetic and copies ran while one was open for 10% of the time, Pallas kernels for 5%

profile of v1, /device:TPU:0, one launch (start us, length us, event | category | flops | bytes accessed | tf_op | source)
XLA Modules:
  0.0 83.6 jit_solution(1624453307665465359)
XLA Ops:
  0.1 0.9 %copy-done.1 = bf16[1,8,8192]{2,1,0:T(8,128)(2,1)S(1)} copy-done((bf16[1,8,8192]{2,1,0:T(8,128)(2,1)S(1)}, bf16[1,8,8192]{2,1,0:T(8,128)(2,1)}, u32[]{:S(2)}) %copy-start.1) | copy-done | bytes 131096
  1.0 0.8 copy-done.2
  1.7 0.7 copy-done.3
  2.4 0.7 norm.1
  3.1 4.1 %collective-permute-start.1 = (bf16[8,2176]{1,0:T(8,128)(2,1)S(1)}, bf16[8,2176]{1,0:T(8,128)(2,1)}, u32[]{:S(2)}, u32[]{:S(2)}) collective-permute-start(bf16[8,2176]{1,0:T(8,128)(2,1)S(1)} %get-tuple-element.29), channel_id=1, source_target_pairs={{0,2},{1,3},{2,0},{3,1},{4,6},{5,7},{6,4},{7,5},{8,10},{9,11},{10,... | collective-permute-start | bytes 104456 | tf_op jit(solution)/shard_map/ppermute | solution.py:48
  7.2 1.6 %collective-permute-start = (bf16[8,2048]{1,0:T(8,128)(2,1)S(1)}, bf16[8,2048]{1,0:T(8,128)(2,1)}, u32[]{:S(2)}, u32[]{:S(2)}) collective-permute-start(bf16[8,2048]{1,0:T(8,128)(2,1)S(1)} %get-tuple-element.28), channel_id=1, source_target_pairs={{0,1},{1,0},{2,3},{3,2},{4,5},{5,4},{6,7},{7,6},{8,9},{9,8},{10,11... | collective-permute-start | bytes 98312 | tf_op jit(solution)/shard_map/ppermute | solution.py:48
  8.8 1.3 %constant_dynamic-slice_fusion = (bf16[2048,128]{1,0:T(8,128)(2,1)S(1)}, bf16[2048,128]{1,0:T(8,128)(2,1)S(1)}) fusion(bf16[2048,1024]{1,0:T(8,128)(2,1)} %param.16, s32[]{:T(128)S(6)} %select_n.16, bf16[2048,1024]{1,0:T(8,128)(2,1)} %param.15), kind=kLoop, calls=%fused_computation.33 | loop fusion | bytes 2097156 | tf_op jit(solution)/shard_map/dynamic_slice | solution.py:524
  10.1 0.2 prepare.1.own
  10.3 1.0 %collective-permute-start.12 = (bf16[2,2048,128]{2,1,0:T(8,128)(2,1)S(1)}, bf16[2,2048,128]{2,1,0:T(8,128)(2,1)}, u32[]{:S(2)}, u32[]{:S(2)}) collective-permute-start(bf16[2,2048,128]{2,1,0:T(8,128)(2,1)S(1)} %prepare.1.own), channel_id=1, source_target_pairs={{0,1},{1,0},{2,3},{3,2},{4,5},{5,4},{6,7},{7,6},{8,9},{9,8},{10,11... | collective-permute-start | bytes 3145736 | tf_op jit(solution)/shard_map/ppermute | solution.py:48
  11.4 0.1 add.109
  11.5 0.1 iota_compare_fusion
  12.2 0.6 broadcast_add_fusion
  12.9 0.5 fusion.3
  13.4 0.1 pad_maximum_fusion.4
  13.6 1.2 %slice.77 = s32[2,64]{1,0:T(2,128)} slice(s32[4,64]{1,0:T(4,128)} %get-tuple-element.60), slice={[0:4:2], [0:64:1]} | slice | bytes 1024 | tf_op jit(solution)/shard_map/slice | solution.py:565
  14.8 0.8 slice_bitcast_fusion
  15.6 0.8 pad_maximum_fusion.2.refs_0_
  16.4 1.6 %collective-permute-start.4 = (bf16[4,8,2048]{2,1,0:T(8,128)(2,1)S(1)}, bf16[4,8,2048]{2,1,0:T(8,128)(2,1)S(1)}, u32[]{:S(2)}, u32[]{:S(2)}) collective-permute-start(bf16[4,8,2048]{2,1,0:T(8,128)(2,1)S(1)} %pad_maximum_fusion.2.refs_0_), channel_id=1, source_target_pairs={{0,8},{4,12},{8,0},{12,4},{16,24},{20,28},{24,16},{28,20},{1,9},{5... | collective-permute-start | bytes 393224 | tf_op jit(solution)/shard_map/ppermute | solution.py:48
  17.9 1.5 %collective-permute-start.6 = (bf16[4,8,2048]{2,1,0:T(8,128)(2,1)S(1)}, bf16[4,8,2048]{2,1,0:T(8,128)(2,1)S(1)}, u32[]{:S(2)}, u32[]{:S(2)}) collective-permute-start(bf16[4,8,2048]{2,1,0:T(8,128)(2,1)S(1)} %pad_maximum_fusion.2.refs_0_), channel_id=1, source_target_pairs={{0,16},{4,20},{8,24},{12,28},{16,0},{20,4},{24,8},{28,12},{1,17},{... | collective-permute-start | bytes 393224 | tf_op jit(solution)/shard_map/ppermute | solution.py:48
  19.5 0.5 collective-permute-start.8
  19.9 1.3 %constant_dynamic-slice_fusion.2 = (bf16[2048,128]{1,0:T(8,128)(2,1)S(1)}, bf16[2048,128]{1,0:T(8,128)(2,1)S(1)}) fusion(bf16[2048,1024]{1,0:T(8,128)(2,1)} %param.14, s32[]{:T(128)S(6)} %select_n.16, bf16[2048,1024]{1,0:T(8,128)(2,1)} %param.13), kind=kLoop, calls=%fused_computation.35 | loop fusion | bytes 2097156 | tf_op jit(solution)/shard_map/dynamic_slice | solution.py:543
  21.3 0.3 pad_maximum_fusion.refs_8_
  21.5 0.8 slice_convert_fusion
  22.4 0.2 collective-permute-done.4.refs_2_
  22.6 0.3 collective-permute-start.5
  22.9 2.6 %collective-permute-done.6.refs_4_ = bf16[4,8,2048]{2,1,0:T(8,128)(2,1)S(1)} collective-permute-done((bf16[4,8,2048]{2,1,0:T(8,128)(2,1)S(1)}, bf16[4,8,2048]{2,1,0:T(8,128)(2,1)S(1)}, u32[]{:S(2)}, u32[]{:S(2)}) %collective-permute-start.6) | collective-permute-done | bytes 131104 | tf_op jit(solution)/shard_map/ppermute | solution.py:48
  25.5 0.5 collective-permute-start.9
  26.1 0.1 select_reduce_fusion
  26.2 0.7 collective-permute-done.7.refs_5_
  26.9 0.2 collective-permute-done.9.refs_7_
  27.1 1.0 %gather.1 = (bf16[256,2048]{1,0:T(8,128)(2,1)S(1)}, f32[2,64,1024]{2,1,0:T(8,128)S(1)}, f32[2,64,1024]{2,1,0:T(8,128)S(1)}) custom-call(bf16[4,8,2048]{2,1,0:T(8,128)(2,1)S(1)} %pad_maximum_fusion.2.refs_0_, bf16[4,8,2048]{2,1,0:T(8,128)(2,1)S(1)} %collective-permute-done.3.refs_1_, bf16[4,8,2048]{2,1,0:T(8,128)(2,1)S(1)} %collective-permute-done.4.refs_2_, ...), custom_call_target="tpu_custom_call" | custom-call | flops 1073741824 | bytes 2097152 | tf_op jit(solution)/shard_map/gather/pallas_call | solution.py:191
  28.1 1.2 %project.1 = (f32[2,64,512]{2,1,0:T(8,128)S(1)}, f32[2,64,512]{2,1,0:T(8,128)S(1)}) custom-call(bf16[256,2048]{1,0:T(8,128)(2,1)S(1)} %get-tuple-element.43.tokens, bf16[2048,1024]{1,0:T(8,128)(2,1)S(1)} %copy-done), custom_call_target="tpu_custom_call" | custom-call | flops 536870912 | bytes 2097152 | tf_op jit(solution)/shard_map/project/pallas_call | solution.py:220
  29.4 1.4 %collective-permute-start.14 = (f16[2,64,512]{2,1,0:T(8,128)(2,1)S(1)}, f16[2,64,512]{2,1,0:T(8,128)(2,1)S(1)}, u32[]{:S(2)}, u32[]{:S(2)}) collective-permute-start(f16[2,64,512]{2,1,0:T(8,128)(2,1)S(1)} %multiply_convert_fusion.2), channel_id=1, source_target_pairs={{0,1},{1,0},{2,3},{3,2},{4,5},{5,4},{6,7},{7,6},{8,9},{9,8},{10,11... | collective-permute-start | bytes 393224 | tf_op jit(solution)/shard_map/ppermute | solution.py:48
  30.8 0.7 collective-permute-start.10
  31.6 1.4 %mask.1.bias = f32[4224,128]{1,0:T(8,128)S(1)} custom-call(s32[4]{0:T(128)S(1)} %pad_add_fusion.1.ids, s32[16]{0:T(128)S(1)} %copy-done.5, s32[2,64]{1,0:T(2,128)S(1)} %add_subtract_fusion.low), custom_call_target="tpu_custom_call" | custom-call | tf_op jit(solution)/shard_map/mask/pallas_call | solution.py:151
  33.0 6.7 %collective-permute-done.14 = f16[2,64,512]{2,1,0:T(8,128)(2,1)S(1)} collective-permute-done((f16[2,64,512]{2,1,0:T(8,128)(2,1)S(1)}, f16[2,64,512]{2,1,0:T(8,128)(2,1)S(1)}, u32[]{:S(2)}, u32[]{:S(2)}) %collective-permute-start.14) | collective-permute-done | bytes 131104 | tf_op jit(solution)/shard_map/ppermute | solution.py:48
  39.7 2.1 %collective-permute-start.15 = (f16[2,64,512]{2,1,0:T(8,128)(2,1)S(1)}, f16[2,64,512]{2,1,0:T(8,128)(2,1)S(1)}, u32[]{:S(2)}, u32[]{:S(2)}) collective-permute-start(f16[2,64,512]{2,1,0:T(8,128)(2,1)S(1)} %multiply_convert_fusion.1), channel_id=1, source_target_pairs={{0,2},{1,3},{2,0},{3,1},{4,6},{5,7},{6,4},{7,5},{8,10},{9,11},{10,... | collective-permute-start | bytes 393224 | tf_op jit(solution)/shard_map/ppermute | solution.py:48
  41.8 4.5 %collective-permute-done.10 = f16[2,64,1024]{2,1,0:T(8,128)(2,1)S(1)} collective-permute-done((f16[2,64,1024]{2,1,0:T(8,128)(2,1)S(1)}, f16[2,64,1024]{2,1,0:T(8,128)(2,1)S(1)}, u32[]{:S(2)}, u32[]{:S(2)}) %collective-permute-start.10) | collective-permute-done | bytes 262176 | tf_op jit(solution)/shard_map/ppermute | solution.py:48
  46.4 1.9 %collective-permute-done.15 = f16[2,64,512]{2,1,0:T(8,128)(2,1)S(1)} collective-permute-done((f16[2,64,512]{2,1,0:T(8,128)(2,1)S(1)}, f16[2,64,512]{2,1,0:T(8,128)(2,1)S(1)}, u32[]{:S(2)}, u32[]{:S(2)}) %collective-permute-start.15) | collective-permute-done | bytes 131104 | tf_op jit(solution)/shard_map/ppermute | solution.py:48
  48.6 8.5 %collective-permute-done.11 = f16[2,64,768]{2,1,0:T(8,128)(2,1)S(1)} collective-permute-done((f16[2,64,768]{2,1,0:T(8,128)(2,1)S(1)}, f16[2,64,768]{2,1,0:T(8,128)(2,1)S(1)}, u32[]{:S(2)}, u32[]{:S(2)}) %collective-permute-start.11) | collective-permute-done | bytes 196640 | tf_op jit(solution)/shard_map/ppermute | solution.py:48
  57.3 4.0 %attend.2 = (f32[1,64,512]{2,1,0:T(8,128)S(1)}, bf16[1,64,640]{2,1,0:T(8,128)(2,1)S(1)}, f32[1,64,128]{2,1,0:T(8,128)S(1)}) custom-call(f32[2,64,512]{2,1,0:T(8,128)S(1)} %maximum_add_fusion.q, f32[2,64,256]{2,1,0:T(8,128)S(1)} %pad_maximum_fusion.3.kv, f32[4,64,128]{2,1,0:T(8,128)S(1)} %get-tuple-element.66.cosine._, ...), custom_call_target="tpu_custom_call" | custom-call | flops 4429185024 | bytes 1048576 | tf_op jit(solution)/shard_map/attend/pallas_call | solution.py:349
  61.3 4.0 %attend.3 = (f32[1,64,512]{2,1,0:T(8,128)S(1)}, bf16[1,64,640]{2,1,0:T(8,128)(2,1)S(1)}, f32[1,64,128]{2,1,0:T(8,128)S(1)}) custom-call(f32[2,64,512]{2,1,0:T(8,128)S(1)} %maximum_add_fusion.1.q, f32[2,64,256]{2,1,0:T(8,128)S(1)} %pad_maximum_fusion.3.kv, f32[4,64,128]{2,1,0:T(8,128)S(1)} %get-tuple-element.66.cosine._, ...), custom_call_target="tpu_custom_call" | custom-call | flops 4429185024 | bytes 1048576 | tf_op jit(solution)/shard_map/attend/pallas_call | solution.py:349
  65.4 2.9 %collective-permute-start.13 = (bf16[1,64,640]{2,1,0:T(8,128)(2,1)S(1)}, bf16[1,64,640]{2,1,0:T(8,128)(2,1)S(1)}, u32[]{:S(2)}, u32[]{:S(2)}) collective-permute-start(bf16[1,64,640]{2,1,0:T(8,128)(2,1)S(1)} %get-tuple-element.41), channel_id=1, source_target_pairs={{0,2},{1,3},{2,0},{3,1},{4,6},{5,7},{6,4},{7,5},{8,10},{9,11},{10,... | collective-permute-start | bytes 245768 | tf_op jit(solution)/shard_map/ppermute | solution.py:48
  68.3 2.9 %collective-permute-done.16.refs_4_ = bf16[1,64,640]{2,1,0:T(8,128)(2,1)S(1)} collective-permute-done((bf16[1,64,640]{2,1,0:T(8,128)(2,1)S(1)}, bf16[1,64,640]{2,1,0:T(8,128)(2,1)S(1)}, u32[]{:S(2)}, u32[]{:S(2)}) %collective-permute-start.16) | collective-permute-done | bytes 81952 | tf_op jit(solution)/shard_map/ppermute | solution.py:48
  71.2 1.8 %collective-permute-done.13.refs_1_ = bf16[1,64,640]{2,1,0:T(8,128)(2,1)S(1)} collective-permute-done((bf16[1,64,640]{2,1,0:T(8,128)(2,1)S(1)}, bf16[1,64,640]{2,1,0:T(8,128)(2,1)S(1)}, u32[]{:S(2)}, u32[]{:S(2)}) %collective-permute-start.13) | collective-permute-done | bytes 81952 | tf_op jit(solution)/shard_map/ppermute | solution.py:48
  72.9 0.9 %finish.1 = bf16[8,8,1024]{2,1,0:T(8,128)(2,1)S(1)} custom-call(s32[4]{0:T(128)S(1)} %pad_add_fusion.1.ids, f32[1,64,512]{2,1,0:T(8,128)S(1)} %get-tuple-element.40.refs_0_, bf16[1,64,640]{2,1,0:T(8,128)(2,1)S(1)} %collective-permute-done.13.refs_1_, f32[1,64,128]{2,1,0:T(8,128)S(1)} %get-tuple-element.42._.refs_2_, ...), custom_call_target="tpu_custom_call" | custom-call | tf_op jit(solution)/shard_map/finish/pallas_call | solution.py:465
  73.9 9.0 %all_to_all.5 = bf16[8,8,1024]{2,1,0:T(8,128)(2,1)S(1)} all-to-all(bf16[8,8,1024]{2,1,0:T(8,128)(2,1)S(1)} %finish.1), channel_id=1, replica_groups=mesh['wide'=8,'blk'=4] {'wide'}, dimensions={0} | all-to-all | bytes 262144 | tf_op jit(solution)/shard_map/all_to_all | solution.py:611
  82.9 0.7 copy.13
  (49 shorter events, 1.0 us)
Async XLA Ops:
  0.1 0.9 %copy-start.1 = (bf16[1,8,8192]{2,1,0:T(8,128)(2,1)S(1)}, bf16[1,8,8192]{2,1,0:T(8,128)(2,1)}, u32[]{:S(2)}) copy-start(bf16[1,8,8192]{2,1,0:T(8,128)(2,1)} %hidden.1) | copy-start | bytes 393220
  1.0 0.8 copy-start.2
  1.7 0.7 copy-start.3
  3.1 11.7 %collective-permute-start.1 = (bf16[8,2176]{1,0:T(8,128)(2,1)S(1)}, bf16[8,2176]{1,0:T(8,128)(2,1)}, u32[]{:S(2)}, u32[]{:S(2)}) collective-permute-start(bf16[8,2176]{1,0:T(8,128)(2,1)S(1)} %get-tuple-element.29), channel_id=1, source_target_pairs={{0,2},{1,3},{2,0},{3,1},{4,6},{5,7},{6,4},{7,5},{8,10},{9,11},{10,... | collective-permute-start | bytes 104456 | tf_op jit(solution)/shard_map/ppermute | solution.py:48
  7.2 8.3 %collective-permute-start = (bf16[8,2048]{1,0:T(8,128)(2,1)S(1)}, bf16[8,2048]{1,0:T(8,128)(2,1)}, u32[]{:S(2)}, u32[]{:S(2)}) collective-permute-start(bf16[8,2048]{1,0:T(8,128)(2,1)S(1)} %get-tuple-element.28), channel_id=1, source_target_pairs={{0,1},{1,0},{2,3},{3,2},{4,5},{5,4},{6,7},{7,6},{8,9},{9,8},{10,11... | collective-permute-start | bytes 98312 | tf_op jit(solution)/shard_map/ppermute | solution.py:48
  8.8 6.7 %collective-permute-start.2 = (bf16[8,2048]{1,0:T(8,128)(2,1)S(1)}, bf16[8,2048]{1,0:T(8,128)(2,1)}, u32[]{:S(2)}, u32[]{:S(2)}) collective-permute-start(bf16[8,2048]{1,0:T(8,128)(2,1)S(1)} %get-tuple-element.30), channel_id=1, source_target_pairs={{0,3},{1,2},{2,1},{3,0},{4,7},{5,6},{6,5},{7,4},{8,11},{9,10},{10,... | collective-permute-start | bytes 98312 | tf_op jit(solution)/shard_map/ppermute | solution.py:48
  10.3 10.9 %slice-start = ((bf16[2048,1024]{1,0:T(8,128)(2,1)}), bf16[2048,512]{1,0:T(8,128)(2,1)S(1)}, s32[]{:S(2)}) async-start(bf16[2048,1024]{1,0:T(8,128)(2,1)} %weights.1), calls=%async_computation.1 | async-start | bytes 4194304 | tf_op jit(solution)/shard_map/slice | solution.py:541
  10.3 46.9 %collective-permute-start.12 = (bf16[2,2048,128]{2,1,0:T(8,128)(2,1)S(1)}, bf16[2,2048,128]{2,1,0:T(8,128)(2,1)}, u32[]{:S(2)}, u32[]{:S(2)}) collective-permute-start(bf16[2,2048,128]{2,1,0:T(8,128)(2,1)S(1)} %prepare.1.own), channel_id=1, source_target_pairs={{0,1},{1,0},{2,3},{3,2},{4,5},{5,4},{6,7},{7,6},{8,9},{9,8},{10,11... | collective-permute-start | bytes 3145736 | tf_op jit(solution)/shard_map/ppermute | solution.py:48
  16.4 6.3 %collective-permute-start.4 = (bf16[4,8,2048]{2,1,0:T(8,128)(2,1)S(1)}, bf16[4,8,2048]{2,1,0:T(8,128)(2,1)S(1)}, u32[]{:S(2)}, u32[]{:S(2)}) collective-permute-start(bf16[4,8,2048]{2,1,0:T(8,128)(2,1)S(1)} %pad_maximum_fusion.2.refs_0_), channel_id=1, source_target_pairs={{0,8},{4,12},{8,0},{12,4},{16,24},{20,28},{24,16},{28,20},{1,9},{5... | collective-permute-start | bytes 393224 | tf_op jit(solution)/shard_map/ppermute | solution.py:48
  17.9 7.6 %collective-permute-start.6 = (bf16[4,8,2048]{2,1,0:T(8,128)(2,1)S(1)}, bf16[4,8,2048]{2,1,0:T(8,128)(2,1)S(1)}, u32[]{:S(2)}, u32[]{:S(2)}) collective-permute-start(bf16[4,8,2048]{2,1,0:T(8,128)(2,1)S(1)} %pad_maximum_fusion.2.refs_0_), channel_id=1, source_target_pairs={{0,16},{4,20},{8,24},{12,28},{16,0},{20,4},{24,8},{28,12},{1,17},{... | collective-permute-start | bytes 393224 | tf_op jit(solution)/shard_map/ppermute | solution.py:48
  19.5 6.1 %collective-permute-start.8 = (bf16[4,8,2048]{2,1,0:T(8,128)(2,1)S(1)}, bf16[4,8,2048]{2,1,0:T(8,128)(2,1)S(1)}, u32[]{:S(2)}, u32[]{:S(2)}) collective-permute-start(bf16[4,8,2048]{2,1,0:T(8,128)(2,1)S(1)} %pad_maximum_fusion.2.refs_0_), channel_id=1, source_target_pairs={{0,24},{4,28},{8,16},{12,20},{16,8},{20,12},{24,0},{28,4},{1,25},{... | collective-permute-start | bytes 393224 | tf_op jit(solution)/shard_map/ppermute | solution.py:48
  19.9 6.2 %collective-permute-start.3 = (bf16[4,8,2048]{2,1,0:T(8,128)(2,1)S(1)}, bf16[4,8,2048]{2,1,0:T(8,128)(2,1)S(1)}, u32[]{:S(2)}, u32[]{:S(2)}) collective-permute-start(bf16[4,8,2048]{2,1,0:T(8,128)(2,1)S(1)} %pad_maximum_fusion.2.refs_0_), channel_id=1, source_target_pairs={{0,4},{4,0},{8,12},{12,8},{16,20},{20,16},{24,28},{28,24},{1,5},{5... | collective-permute-start | bytes 393224 | tf_op jit(solution)/shard_map/ppermute | solution.py:48
  19.9 6.1 %copy-start.4 = (s32[1,64]{1,0:T(1,128)S(1)}, s32[1,64]{1,0:T(1,128)}, u32[]{:S(2)}) copy-start(s32[1,64]{1,0:T(1,128)} %reach.1) | copy-start | bytes 772
  21.2 6.8 %copy-start = (bf16[2048,1024]{1,0:T(8,128)(2,1)S(1)}, bf16[2048,1024]{1,0:T(8,128)(2,1)}, u32[]{:S(2)}) copy-start(bf16[2048,1024]{1,0:T(8,128)(2,1)} %weights.1) | copy-start | bytes 12582916
  22.6 3.5 %collective-permute-start.5 = (bf16[4,8,2048]{2,1,0:T(8,128)(2,1)S(1)}, bf16[4,8,2048]{2,1,0:T(8,128)(2,1)S(1)}, u32[]{:S(2)}, u32[]{:S(2)}) collective-permute-start(bf16[4,8,2048]{2,1,0:T(8,128)(2,1)S(1)} %collective-permute-done.4.refs_2_), channel_id=1, source_target_pairs={{0,4},{4,0},{8,12},{12,8},{16,20},{20,16},{24,28},{28,24},{1,5},{5... | collective-permute-start | bytes 393224 | tf_op jit(solution)/shard_map/ppermute | solution.py:48
  25.5 1.3 %collective-permute-start.7 = (bf16[4,8,2048]{2,1,0:T(8,128)(2,1)S(1)}, bf16[4,8,2048]{2,1,0:T(8,128)(2,1)S(1)}, u32[]{:S(2)}, u32[]{:S(2)}) collective-permute-start(bf16[4,8,2048]{2,1,0:T(8,128)(2,1)S(1)} %collective-permute-done.6.refs_4_), channel_id=1, source_target_pairs={{0,4},{4,0},{8,12},{12,8},{16,20},{20,16},{24,28},{28,24},{1,5},{5... | collective-permute-start | bytes 393224 | tf_op jit(solution)/shard_map/ppermute | solution.py:48
  25.5 1.5 %collective-permute-start.9 = (bf16[4,8,2048]{2,1,0:T(8,128)(2,1)S(1)}, bf16[4,8,2048]{2,1,0:T(8,128)(2,1)S(1)}, u32[]{:S(2)}, u32[]{:S(2)}) collective-permute-start(bf16[4,8,2048]{2,1,0:T(8,128)(2,1)S(1)} %collective-permute-done.8.refs_6_), channel_id=1, source_target_pairs={{0,4},{4,0},{8,12},{12,8},{16,20},{20,16},{24,28},{28,24},{1,5},{5... | collective-permute-start | bytes 393224 | tf_op jit(solution)/shard_map/ppermute | solution.py:48
  28.0 3.5 %copy-start.6 = (s32[2,64]{1,0:T(2,128)S(1)}, s32[2,64]{1,0:T(2,128)}, u32[]{:S(2)}) copy-start(s32[2,64]{1,0:T(2,128)} %slice.77) | copy-start | bytes 1540
  28.1 3.5 %copy-start.5 = (s32[16]{0:T(128)S(1)}, s32[16]{0:T(128)}, u32[]{:S(2)}) copy-start(s32[16]{0:T(128)} %passkey.1) | copy-start | bytes 196
  29.4 10.3 %collective-permute-start.14 = (f16[2,64,512]{2,1,0:T(8,128)(2,1)S(1)}, f16[2,64,512]{2,1,0:T(8,128)(2,1)S(1)}, u32[]{:S(2)}, u32[]{:S(2)}) collective-permute-start(f16[2,64,512]{2,1,0:T(8,128)(2,1)S(1)} %multiply_convert_fusion.2), channel_id=1, source_target_pairs={{0,1},{1,0},{2,3},{3,2},{4,5},{5,4},{6,7},{7,6},{8,9},{9,8},{10,11... | collective-permute-start | bytes 393224 | tf_op jit(solution)/shard_map/ppermute | solution.py:48
  30.8 15.4 %collective-permute-start.10 = (f16[2,64,1024]{2,1,0:T(8,128)(2,1)S(1)}, f16[2,64,1024]{2,1,0:T(8,128)(2,1)S(1)}, u32[]{:S(2)}, u32[]{:S(2)}) collective-permute-start(f16[2,64,1024]{2,1,0:T(8,128)(2,1)S(1)} %multiply_convert_fusion), channel_id=1, source_target_pairs={{0,1},{1,0},{2,3},{3,2},{4,5},{5,4},{6,7},{7,6},{8,9},{9,8},{10,11... | collective-permute-start | bytes 786440 | tf_op jit(solution)/shard_map/ppermute | solution.py:48
  39.7 8.6 %collective-permute-start.15 = (f16[2,64,512]{2,1,0:T(8,128)(2,1)S(1)}, f16[2,64,512]{2,1,0:T(8,128)(2,1)S(1)}, u32[]{:S(2)}, u32[]{:S(2)}) collective-permute-start(f16[2,64,512]{2,1,0:T(8,128)(2,1)S(1)} %multiply_convert_fusion.1), channel_id=1, source_target_pairs={{0,2},{1,3},{2,0},{3,1},{4,6},{5,7},{6,4},{7,5},{8,10},{9,11},{10,... | collective-permute-start | bytes 393224 | tf_op jit(solution)/shard_map/ppermute | solution.py:48
  48.4 8.7 %collective-permute-start.11 = (f16[2,64,768]{2,1,0:T(8,128)(2,1)S(1)}, f16[2,64,768]{2,1,0:T(8,128)(2,1)S(1)}, u32[]{:S(2)}, u32[]{:S(2)}) collective-permute-start(f16[2,64,768]{2,1,0:T(8,128)(2,1)S(1)} %pad_maximum_fusion.1), channel_id=1, source_target_pairs={{0,2},{1,3},{2,0},{3,1},{4,6},{5,7},{6,4},{7,5},{8,10},{9,11},{10,... | collective-permute-start | bytes 589832 | tf_op jit(solution)/shard_map/ppermute | solution.py:48
  65.3 5.9 %collective-permute-start.16 = (bf16[1,64,640]{2,1,0:T(8,128)(2,1)S(1)}, bf16[1,64,640]{2,1,0:T(8,128)(2,1)S(1)}, u32[]{:S(2)}, u32[]{:S(2)}) collective-permute-start(bf16[1,64,640]{2,1,0:T(8,128)(2,1)S(1)} %get-tuple-element.47), channel_id=1, source_target_pairs={{0,2},{1,3},{2,0},{3,1},{4,6},{5,7},{6,4},{7,5},{8,10},{9,11},{10,... | collective-permute-start | bytes 245768 | tf_op jit(solution)/shard_map/ppermute | solution.py:48
  65.4 7.6 %collective-permute-start.13 = (bf16[1,64,640]{2,1,0:T(8,128)(2,1)S(1)}, bf16[1,64,640]{2,1,0:T(8,128)(2,1)S(1)}, u32[]{:S(2)}, u32[]{:S(2)}) collective-permute-start(bf16[1,64,640]{2,1,0:T(8,128)(2,1)S(1)} %get-tuple-element.41), channel_id=1, source_target_pairs={{0,2},{1,3},{2,0},{3,1},{4,6},{5,7},{6,4},{7,5},{8,10},{9,11},{10,... | collective-permute-start | bytes 245768 | tf_op jit(solution)/shard_map/ppermute | solution.py:48

commit v2 on v1

--- a/solution.py
+++ b/solution.py
@@ -35,13 +35,15 @@
         head_size * math.log(trained_context / (slow_turns * 2.0 * math.pi)) / (2.0 * log_base)
     )
     spread = max(highest - lowest, 1)
-    counter = jnp.arange(half, dtype=jnp.float32)
+    lane = jnp.arange(head_size, dtype=jnp.int32)
+    counter = (lane % half).astype(jnp.float32)
     inverse = jnp.exp(-(2.0 * counter / head_size) * log_base)
     ramp = jnp.clip((counter - lowest) / spread, 0.0, 1.0)
     mixed = inverse / yarn_factor * ramp + inverse * (1.0 - ramp)
-    angles = positions.astype(jnp.float32)[:, None] * mixed[None, :]
+    angles = positions.astype(jnp.float32) * mixed
     mscale = 0.1 * math.log(yarn_factor) + 1.0
-    return (jnp.cos(angles) * mscale, jnp.sin(angles) * mscale)
+    signed = jnp.where(lane < half, -mscale, mscale)
+    return (jnp.cos(angles) * mscale, jnp.sin(angles) * signed)
 
 
 def swapped(block, axis, mask):
@@ -61,22 +63,23 @@
     return pl.BlockSpec(memory_space=pltpu.SMEM)
 
 
-def norm_kernel(ids, hidden, gain, reach, *rest):
+def norm_kernel(hidden, gain, reach, *rest):
     outs, scratch = rest[:-1], rest[-1]
     rows, width = outs[0].shape
+    me = lax.axis_index("blk")
     x = hidden[0].astype(F32)
     inv_rms = lax.rsqrt(jnp.mean(x * x, axis=1, keepdims=True) + 1e-05)
     scratch[...] = x * inv_rms * gain[...]
     digits = jnp.concatenate([reach[...] >> 7, reach[...] & 127], axis=1).astype(F32)
     digits = jnp.broadcast_to(digits, (rows, digits.shape[1])).astype(BF16)
     for d, out in enumerate(outs):
-        at = pl.multiple_of((ids[0] ^ d) * width, width)
+        at = pl.multiple_of((me ^ d) * width, width)
         out[:, :width] = scratch[:, pl.ds(at, width)].astype(BF16)
         if out.shape[1] > width:
             out[:, width:] = digits
 
 
-def norm(ids, hidden, gain, reach, blocks):
+def norm(hidden, gain, reach, blocks):
     _, rows, features = hidden.shape
     width = features // blocks
     longer = width + 2 * reach.shape[1]
@@ -84,12 +87,12 @@
     return pl.pallas_call(
         norm_kernel,
         out_shape=[jax.ShapeDtypeStruct((rows, size), BF16) for size in widths],
-        in_specs=[smem()] + vmem(3),
+        in_specs=vmem(3),
         out_specs=vmem(blocks),
         scratch_shapes=[pltpu.VMEM((rows, features), F32)],
-        compiler_params=params(hidden, gain),
+        compiler_params=pltpu.CompilerParams(vmem_limit_bytes=56 * MEBI),
         name="norm",
-    )(ids, hidden, gain, reach)
+    )(hidden, gain, reach)
 
 
 def prepare_kernel(keys, values, out):
@@ -110,16 +113,34 @@
     )(keys, values)
 
 
-def mask_kernel(cached, groups, ids, passkey, low, bias):
-    half, count = low.shape
+def mask_kernel(cached, groups, ids, passkey, reach, *refs):
+    digits, bias = refs[:-1], refs[-1]
+    half = len(digits) + 1
+    count = reach.shape[1]
     rows = count // groups
     total = 2 * cached
-    lows = jnp.concatenate([low[j : j + 1] for j in range(half)], axis=1)
     lanes = half * count
 
-    def index_of(slot, block):
-        token = ((slot // rows) ^ ids[1]) * rows + slot % rows
-        return ids[3] + block * count + token
+    def token_of(slot):
+        return ((slot // rows) ^ ids[1]) * rows + slot % rows
+
+    slots = lax.broadcasted_iota(jnp.int32, (1, count), 1)
+    tokens = token_of(slots)
+    down = lax.broadcasted_iota(jnp.int32, (count, count), 0)
+    across = lax.broadcasted_iota(jnp.int32, (count, count), 1)
+    reaches = [reach[...].astype(F32)]
+    for array in digits:
+        pair = array[:1].astype(F32)
+        reaches.append(pair[:, :count] * 128.0 + pair[:, count:])
+    lows, queries = [], []
+    for j, natural in enumerate(reaches):
+        column = jnp.sum(jnp.where(down == across, natural, 0.0), axis=1, keepdims=True)
+        slotted = jnp.sum(jnp.where(down == tokens, column, 0.0), axis=0, keepdims=True)
+        index = ids[3] + (ids[0] ^ (2 * j)) * count + tokens
+        queries.append(index)
+        lows.append(index - slotted.astype(jnp.int32))
+    lows = jnp.concatenate(lows, axis=1)
+    queries = jnp.concatenate(queries, axis=1)
 
     step = min(256, cached)
     ramp = lax.broadcasted_iota(jnp.int32, (step, lanes), 0)
@@ -135,27 +156,26 @@
             def _():
                 bias[pl.ds(side * cached + row, 1), :] = jnp.zeros((1, lanes), F32)
 
-    slots = lax.broadcasted_iota(jnp.int32, (1, count), 1)
-    queries = jnp.concatenate([index_of(slots, ids[0] ^ (2 * j)) for j in range(half)], axis=1)
     slots = lax.broadcasted_iota(jnp.int32, (count, 1), 0)
     for d in range(2):
-        index = index_of(slots, ids[0] ^ d)
+        index = ids[3] + (ids[0] ^ d) * count + token_of(slots)
         bias[total + d * count : total + (d + 1) * count] = jnp.where(
             (index <= queries) & (index >= lows), 0.0, masked_score
         )
 
 
-def mask(ids, passkey, low, cached, groups):
-    half, count = low.shape
+def mask(ids, passkey, reach, digits, cached, groups):
+    count = reach.shape[1]
+    half = len(digits) + 1
     shape = jax.ShapeDtypeStruct((2 * cached + 2 * count, half * count), F32)
     return pl.pallas_call(
         functools.partial(mask_kernel, cached, groups),
         out_shape=shape,
-        in_specs=[smem(), smem()] + vmem(),
+        in_specs=[smem(), smem()] + vmem(half),
         out_specs=vmem()[0],
         compiler_params=params(shape),
         name="mask",
-    )(ids, passkey, low)
+    )(ids, passkey, reach, *digits)
 
 
 def gather_kernel(groups, part, *refs):
@@ -240,7 +260,7 @@
     return x * cosine + pltpu.roll(x, HEAD_WIDTH // 2, 1) * sine
 
 
-def attend_kernel(together, q, kv, cosine, sine, bias, own, far, _, o_keep,
+def attend_kernel(together, q, kv, cosine, sine, bias, own, far, o_keep,
                    o_send, stats_keep, scores, k_new, v_new, pair, arrived):
     fetch = pltpu.make_async_copy(far, pair, arrived)
     fetch.start()
@@ -332,7 +352,7 @@
             o_send[j - half // 2, :, columns:] = part.astype(BF16)
 
 
-def attend(q, kv, cosine, sine, bias, own, pair, before):
+def attend(q, kv, cosine, sine, bias, own, pair):
     half, count, columns = q.shape
     rows = half * count
     total = bias.shape[0]
@@ -344,12 +364,12 @@
         jax.ShapeDtypeStruct((out_half, count, columns + HEAD_WIDTH), BF16),
         jax.ShapeDtypeStruct((out_half, count, HEAD_WIDTH), F32),
     ]
-    ins = (q, kv, cosine, sine, bias, own, pair, before)
+    ins = (q, kv, cosine, sine, bias, own, pair)
     scores = jax.ShapeDtypeStruct((total, together * rows), F32)
     return pl.pallas_call(
         functools.partial(attend_kernel, together),
         out_shape=outs,
-        in_specs=vmem(len(ins) - 2) + [pl.BlockSpec(memory_space=pl.ANY)] * 2,
+        in_specs=vmem(len(ins) - 1) + [pl.BlockSpec(memory_space=pl.ANY)],
         out_specs=vmem(3),
         scratch_shapes=[
             pltpu.VMEM(scores.shape, F32),
@@ -513,7 +533,7 @@
     def widen(array):
         return array.astype(F32) * (1.0 / fit)
 
-    slices = norm(ids, hidden, norm_gain[None, :], reach, blocks)
+    slices = norm(hidden, norm_gain[None, :], reach, blocks)
     sent = [swapped(slices[d], "blk", d) for d in range(1, blocks)]
     slices, cache_key, prefix_value_cache = lax.optimization_barrier(
         (slices, cache_key, prefix_value_cache)
@@ -545,24 +565,13 @@
         axis=1,
     )
 
-    token = (w ^ jnp.arange(groups, dtype=jnp.int32))[:, None] * rows + jnp.arange(
-        rows, dtype=jnp.int32
-    )
-    token = token.reshape(count)
-    block_of = b ^ jnp.arange(blocks, dtype=jnp.int32)
-    place = block_of[:, None] * count + token[None, :]
-    cosine, sine = yarn_tables(start[0] + place.reshape(-1), HEAD_WIDTH)
-    cosine = jnp.concatenate([cosine, cosine], axis=1).reshape(blocks, count, HEAD_WIDTH)
-    sine = jnp.concatenate([-sine, sine], axis=1).reshape(blocks, count, HEAD_WIDTH)
-    digits = [array[0, width:].astype(jnp.int32) for array in sent[1::2]]
-    reaches = jnp.stack(
-        [reach[0]] + [array[:count] * 128 + array[count:] for array in digits]
-    )
-    natural = jnp.arange(count, dtype=jnp.int32)
-    reaches = jnp.sum(
-        jnp.where(token[None, :, None] == natural[None, None, :], reaches[:, None, :], 0), axis=2
-    )
-    bias = mask(ids, passkey, cache_total + place[::2] - reaches, cached, groups)
+    shape = (blocks, count, HEAD_WIDTH)
+    slot = lax.broadcasted_iota(jnp.int32, shape, 1)
+    block = b ^ lax.broadcasted_iota(jnp.int32, shape, 0)
+    token = ((slot // rows) ^ w) * rows + slot % rows
+    cosine, sine = yarn_tables(start[0] + block * count + token, HEAD_WIDTH)
+    digits = [array[:, width:] for array in sent[1::2]]
+    bias = mask(ids, passkey, reach, digits, cached, groups)
 
     part = columns // chunks
     tokens, *first = gather(pieces, weights, part)
@@ -570,11 +579,11 @@
         project(tokens, w_query, blocks, c * part, part) for c in range(1, chunks)
     ]
     pair = 2 * HEAD_WIDTH
-    parts = []
-    got = [swapped(narrow(send), "blk", 1) for _, send in projected]
-    after = cosine
-    for c, (keep, _) in enumerate(projected):
-        keep = keep + widen(got[c])
+    order = list(range(chunks))
+    got = {c: swapped(narrow(projected[c][1]), "blk", 1) for c in order}
+    queries = {}
+    for c in order:
+        keep = projected[c][0] + widen(got[c])
         if c == 0:
             even = keep[:, :, part : part + pair]
             odd = keep[:, :, part + pair :]
@@ -600,13 +609,16 @@
             bit //= 2
         if c == 0:
             kv = jnp.concatenate([even, odd], axis=0)
-        keep, send, stats = attend(keep, kv, cosine, sine, bias, cache, cache_pair, after)
-        after = stats
+        queries[c] = keep
+    parts = {}
+    for c in range(chunks):
+        keep, send, stats = attend(queries[c], kv, cosine, sine, bias, cache, cache_pair)
         bit = half // 2
         while bit > 1:
             keep, send, stats = merge(keep, swapped(send, "blk", 2 * bit), stats)
             bit //= 2
-        parts.append((keep, swapped(send, "blk", 2), stats))
+        parts[c] = (keep, swapped(send, "blk", 2), stats)
+    parts = [parts[c] for c in range(chunks)]
     ready = finish(ids, parts, groups)
     ready = lax.all_to_all(ready, "wide", split_axis=0, concat_axis=0, tiled=True)
     return ready.transpose(1, 0, 2).reshape(1, rows, groups * columns)

time: 84.1 us -> 80.3 us (0.955)
  local copies, waits for them, and re-layouts: 7.72 us -> 3.31 us
  waiting for transfers between devices: 30 us -> 33.2 us
  other arithmetic: 4.12 us -> 1.48 us
  Pallas kernels: 13.5 us -> 14.6 us
    ppermute x17, waiting for transfers between devices: 30 us -> 33.2 us  [swapped(): lax.ppermute(block, axis, [(i, i ^ mask) for i in range(lax.axis_size(axi...]
    unnamed x15 -> x9, local copies, waits for them, and re-layouts: 2.99 us -> 0.68 us
    slice x1, local copies, waits for them, and re-layouts: 1.24 us -> 0.01 us  [local(): digits = [array[:, width:] for array in sent[1::2]]]
    pallas_call x1, Pallas kernels: 0.74 us -> 1.77 us  [norm(): pl.pallas_call(norm_kernel, out_shape=[jax.ShapeDtypeStruct((rows, size),...]
  transfers between devices with their start and end apart: 17 -> 17, of which waited for: 10 -> 10; matrix products, arithmetic and copies ran while one was open for 10% -> 5% of each run, Pallas kernels for 5% -> 10%
where the time goes in v2:
time: 80.3 us; the launch traced here: 80 us
  waiting for transfers between devices  33.2 us (41%)
  starting transfers between devices  17.5 us (22%)
  Pallas kernels  14.6 us (18%)
  blocking collectives  8.89 us (11%)
  local copies, waits for them, and re-layouts  3.31 us (4%)
  other arithmetic  1.48 us (2%)
  between operations  0.98 us (1%)
    ppermute x17, waiting for transfers between devices, swapped(): lax.ppermute(block, axis, [(i, i ^ mask) for i in range(lax.axis_size(axi...  33.2 us
    ppermute x17, starting transfers between devices, swapped(): lax.ppermute(block, axis, [(i, i ^ mask) for i in range(lax.axis_size(axi...  17.5 us
    all_to_all x1, blocking collectives, local(): lax.all_to_all(ready, 'wide', split_axis=0, concat_axis=0, tiled=True)  8.89 us
    pallas_call x2, Pallas kernels, attend(): pl.pallas_call(functools.partial(attend_kernel, together), out_shape=outs...  7.99 us
    pallas_call x1, Pallas kernels, norm(): pl.pallas_call(norm_kernel, out_shape=[jax.ShapeDtypeStruct((rows, size),...  1.77 us
  transfers between devices with their start and end apart: 17, of which 10 were waited for; matrix products, arithmetic and copies ran while one was open for 5% of the time, Pallas kernels for 10%

profile of v2, /device:TPU:0, one launch (start us, length us, event | category | flops | bytes accessed | tf_op | source)
XLA Modules:
  0.0 80.0 jit_solution(12788647434131356483)
XLA Ops:
  0.0 1.8 %norm.1 = (bf16[8,2048]{1,0:T(8,128)(2,1)}, bf16[8,2048]{1,0:T(8,128)(2,1)}, bf16[8,2176]{1,0:T(8,128)(2,1)}, bf16[8,2048]{1,0:T(8,128)(2,1)}) custom-call(bf16[1,8,8192]{2,1,0:T(8,128)(2,1)} %hidden.1, f32[1,8192]{1,0:T(1,128)} %bitcast.15, s32[1,64]{1,0:T(1,128)} %reach.3), custom_call_target="tpu_custom_call" | custom-call | tf_op jit(solution)/shard_map/norm/pallas_call | solution.py:87
  1.8 4.0 %collective-permute-start.1 = (bf16[8,2176]{1,0:T(8,128)(2,1)}, bf16[8,2176]{1,0:T(8,128)(2,1)S(1)}, u32[]{:S(2)}, u32[]{:S(2)}) collective-permute-start(bf16[8,2176]{1,0:T(8,128)(2,1)} %get-tuple-element.29), channel_id=1, source_target_pairs={{0,2},{1,3},{2,0},{3,1},{4,6},{5,7},{6,4},{7,5},{8,10},{9,11},{10,... | collective-permute-start | bytes 104456 | tf_op jit(solution)/shard_map/ppermute | solution.py:50
  5.8 1.6 %collective-permute-start = (bf16[8,2048]{1,0:T(8,128)(2,1)}, bf16[8,2048]{1,0:T(8,128)(2,1)S(1)}, u32[]{:S(2)}, u32[]{:S(2)}) collective-permute-start(bf16[8,2048]{1,0:T(8,128)(2,1)} %get-tuple-element.28), channel_id=1, source_target_pairs={{0,1},{1,0},{2,3},{3,2},{4,5},{5,4},{6,7},{7,6},{8,9},{9,8},{10,11... | collective-permute-start | bytes 98312 | tf_op jit(solution)/shard_map/ppermute | solution.py:50
  7.4 1.3 %constant_dynamic-slice_fusion = (bf16[2048,128]{1,0:T(8,128)(2,1)S(1)}, bf16[2048,128]{1,0:T(8,128)(2,1)S(1)}) fusion(bf16[2048,1024]{1,0:T(8,128)(2,1)} %param.16, s32[]{:T(128)S(6)} %select_n.41, bf16[2048,1024]{1,0:T(8,128)(2,1)} %param.15), kind=kLoop, calls=%fused_computation.29 | loop fusion | bytes 2097156 | tf_op jit(solution)/shard_map/dynamic_slice | solution.py:544
  8.7 0.0 slice-start
  8.7 0.2 prepare.1.own
  8.9 1.0 %collective-permute-start.12 = (bf16[2,2048,128]{2,1,0:T(8,128)(2,1)S(1)}, bf16[2,2048,128]{2,1,0:T(8,128)(2,1)}, u32[]{:S(2)}, u32[]{:S(2)}) collective-permute-start(bf16[2,2048,128]{2,1,0:T(8,128)(2,1)S(1)} %prepare.1.own), channel_id=1, source_target_pairs={{0,1},{1,0},{2,3},{3,2},{4,5},{5,4},{6,7},{7,6},{8,9},{9,8},{10,11... | collective-permute-start | bytes 3145736 | tf_op jit(solution)/shard_map/ppermute | solution.py:50
  10.6 0.6 sine_multiply_fusion
  11.2 0.0 collective-permute-done.1
  11.2 2.5 %collective-permute-done.2 = bf16[8,2048]{1,0:T(8,128)(2,1)S(1)} collective-permute-done((bf16[8,2048]{1,0:T(8,128)(2,1)}, bf16[8,2048]{1,0:T(8,128)(2,1)S(1)}, u32[]{:S(2)}, u32[]{:S(2)}) %collective-permute-start.2) | collective-permute-done | bytes 32800 | tf_op jit(solution)/shard_map/ppermute | solution.py:50
  13.7 1.6 %collective-permute-start.4 = (bf16[4,8,2048]{2,1,0:T(8,128)(2,1)S(1)}, bf16[4,8,2048]{2,1,0:T(8,128)(2,1)S(1)}, u32[]{:S(2)}, u32[]{:S(2)}) collective-permute-start(bf16[4,8,2048]{2,1,0:T(8,128)(2,1)S(1)} %pad_maximum_fusion.2.refs_0_), channel_id=1, source_target_pairs={{0,8},{4,12},{8,0},{12,4},{16,24},{20,28},{24,16},{28,20},{1,9},{5... | collective-permute-start | bytes 393224 | tf_op jit(solution)/shard_map/ppermute | solution.py:50
  15.2 1.5 %collective-permute-start.6 = (bf16[4,8,2048]{2,1,0:T(8,128)(2,1)S(1)}, bf16[4,8,2048]{2,1,0:T(8,128)(2,1)S(1)}, u32[]{:S(2)}, u32[]{:S(2)}) collective-permute-start(bf16[4,8,2048]{2,1,0:T(8,128)(2,1)S(1)} %pad_maximum_fusion.2.refs_0_), channel_id=1, source_target_pairs={{0,16},{4,20},{8,24},{12,28},{16,0},{20,4},{24,8},{28,12},{1,17},{... | collective-permute-start | bytes 393224 | tf_op jit(solution)/shard_map/ppermute | solution.py:50
  16.8 0.5 collective-permute-start.8
  17.2 0.0 collective-permute-start.3
  17.2 1.3 %constant_dynamic-slice_fusion.2 = (bf16[2048,128]{1,0:T(8,128)(2,1)S(1)}, bf16[2048,128]{1,0:T(8,128)(2,1)S(1)}) fusion(bf16[2048,1024]{1,0:T(8,128)(2,1)} %param.14, s32[]{:T(128)S(6)} %select_n.41, bf16[2048,1024]{1,0:T(8,128)(2,1)} %param.13), kind=kLoop, calls=%fused_computation.31 | loop fusion | bytes 2097156 | tf_op jit(solution)/shard_map/dynamic_slice | solution.py:563
  18.5 0.9 %collective-permute-done.4.refs_2_ = bf16[4,8,2048]{2,1,0:T(8,128)(2,1)S(1)} collective-permute-done((bf16[4,8,2048]{2,1,0:T(8,128)(2,1)S(1)}, bf16[4,8,2048]{2,1,0:T(8,128)(2,1)S(1)}, u32[]{:S(2)}, u32[]{:S(2)}) %collective-permute-start.4) | collective-permute-done | bytes 131104 | tf_op jit(solution)/shard_map/ppermute | solution.py:50
  19.5 0.0 collective-permute-start.5
  19.5 1.2 %collective-permute-done.6.refs_4_ = bf16[4,8,2048]{2,1,0:T(8,128)(2,1)S(1)} collective-permute-done((bf16[4,8,2048]{2,1,0:T(8,128)(2,1)S(1)}, bf16[4,8,2048]{2,1,0:T(8,128)(2,1)S(1)}, u32[]{:S(2)}, u32[]{:S(2)}) %collective-permute-start.6) | collective-permute-done | bytes 131104 | tf_op jit(solution)/shard_map/ppermute | solution.py:50
  20.7 0.0 collective-permute-start.7
  20.7 1.9 %collective-permute-done.8.refs_6_ = bf16[4,8,2048]{2,1,0:T(8,128)(2,1)S(1)} collective-permute-done((bf16[4,8,2048]{2,1,0:T(8,128)(2,1)S(1)}, bf16[4,8,2048]{2,1,0:T(8,128)(2,1)S(1)}, u32[]{:S(2)}, u32[]{:S(2)}) %collective-permute-start.8) | collective-permute-done | bytes 131104 | tf_op jit(solution)/shard_map/ppermute | solution.py:50
  22.6 0.3 pad_maximum_fusion.refs_8_
  22.9 1.0 %collective-permute-done.9.refs_7_ = bf16[4,8,2048]{2,1,0:T(8,128)(2,1)S(1)} collective-permute-done((bf16[4,8,2048]{2,1,0:T(8,128)(2,1)S(1)}, bf16[4,8,2048]{2,1,0:T(8,128)(2,1)S(1)}, u32[]{:S(2)}, u32[]{:S(2)}) %collective-permute-start.9) | collective-permute-done | bytes 131104 | tf_op jit(solution)/shard_map/ppermute | solution.py:50
  24.0 1.0 %gather.1 = (bf16[256,2048]{1,0:T(8,128)(2,1)S(1)}, f32[2,64,1024]{2,1,0:T(8,128)S(1)}, f32[2,64,1024]{2,1,0:T(8,128)S(1)}) custom-call(bf16[4,8,2048]{2,1,0:T(8,128)(2,1)S(1)} %pad_maximum_fusion.2.refs_0_, bf16[4,8,2048]{2,1,0:T(8,128)(2,1)S(1)} %collective-permute-done.3.refs_1_, bf16[4,8,2048]{2,1,0:T(8,128)(2,1)S(1)} %collective-permute-done.4.refs_2_, ...), custom_call_target="tpu_custom_call" | custom-call | flops 1073741824 | bytes 2097152 | tf_op jit(solution)/shard_map/gather/pallas_call | solution.py:211
  25.0 0.0 copy-start.1
  25.0 0.0 copy-start.2
  25.0 1.2 %project.1 = (f32[2,64,512]{2,1,0:T(8,128)S(1)}, f32[2,64,512]{2,1,0:T(8,128)S(1)}) custom-call(bf16[256,2048]{1,0:T(8,128)(2,1)S(1)} %get-tuple-element.43.tokens, bf16[2048,1024]{1,0:T(8,128)(2,1)S(1)} %copy-done), custom_call_target="tpu_custom_call" | custom-call | flops 536870912 | bytes 2097152 | tf_op jit(solution)/shard_map/project/pallas_call | solution.py:240
  26.3 0.1 collective-permute-start.14
  26.4 2.1 %collective-permute-start.10 = (f16[2,64,1024]{2,1,0:T(8,128)(2,1)S(1)}, f16[2,64,1024]{2,1,0:T(8,128)(2,1)S(1)}, u32[]{:S(2)}, u32[]{:S(2)}) collective-permute-start(f16[2,64,1024]{2,1,0:T(8,128)(2,1)S(1)} %multiply_convert_fusion), channel_id=1, source_target_pairs={{0,1},{1,0},{2,3},{3,2},{4,5},{5,4},{6,7},{7,6},{8,9},{9,8},{10,11... | collective-permute-start | bytes 786440 | tf_op jit(solution)/shard_map/ppermute | solution.py:50
  28.5 0.1 pad_add_fusion.ids
  28.6 1.5 %mask.1.bias = f32[4224,128]{1,0:T(8,128)S(1)} custom-call(s32[4]{0:T(128)S(1)} %pad_add_fusion.ids, s32[16]{0:T(128)S(1)} %copy-done.2, s32[1,64]{1,0:T(1,128)S(1)} %copy-done.1, bf16[8,128]{1,0:T(8,128)(2,1)S(1)} %slice.80.refs_0_), custom_call_target="tpu_custom_call" | custom-call | tf_op jit(solution)/shard_map/mask/pallas_call | solution.py:171
  30.1 8.2 %collective-permute-done.14 = f16[2,64,512]{2,1,0:T(8,128)(2,1)S(1)} collective-permute-done((f16[2,64,512]{2,1,0:T(8,128)(2,1)S(1)}, f16[2,64,512]{2,1,0:T(8,128)(2,1)S(1)}, u32[]{:S(2)}, u32[]{:S(2)}) %collective-permute-start.14) | collective-permute-done | bytes 131104 | tf_op jit(solution)/shard_map/ppermute | solution.py:50
  38.2 0.1 multiply_convert_fusion.1
  38.3 2.1 %collective-permute-start.15 = (f16[2,64,512]{2,1,0:T(8,128)(2,1)S(1)}, f16[2,64,512]{2,1,0:T(8,128)(2,1)S(1)}, u32[]{:S(2)}, u32[]{:S(2)}) collective-permute-start(f16[2,64,512]{2,1,0:T(8,128)(2,1)S(1)} %multiply_convert_fusion.1), channel_id=1, source_target_pairs={{0,2},{1,3},{2,0},{3,1},{4,6},{5,7},{6,4},{7,5},{8,10},{9,11},{10,... | collective-permute-start | bytes 393224 | tf_op jit(solution)/shard_map/ppermute | solution.py:50
  40.4 4.5 %collective-permute-done.10 = f16[2,64,1024]{2,1,0:T(8,128)(2,1)S(1)} collective-permute-done((f16[2,64,1024]{2,1,0:T(8,128)(2,1)S(1)}, f16[2,64,1024]{2,1,0:T(8,128)(2,1)S(1)}, u32[]{:S(2)}, u32[]{:S(2)}) %collective-permute-start.10) | collective-permute-done | bytes 262176 | tf_op jit(solution)/shard_map/ppermute | solution.py:50
  44.9 0.1 multiply_add_fusion
  45.0 1.8 %collective-permute-done.15 = f16[2,64,512]{2,1,0:T(8,128)(2,1)S(1)} collective-permute-done((f16[2,64,512]{2,1,0:T(8,128)(2,1)S(1)}, f16[2,64,512]{2,1,0:T(8,128)(2,1)S(1)}, u32[]{:S(2)}, u32[]{:S(2)}) %collective-permute-start.15) | collective-permute-done | bytes 131104 | tf_op jit(solution)/shard_map/ppermute | solution.py:50
  46.9 0.1 pad_maximum_fusion.1
  47.0 0.1 collective-permute-start.11
  47.1 0.1 maximum_add_fusion.1.q
  47.1 8.5 %collective-permute-done.11 = f16[2,64,768]{2,1,0:T(8,128)(2,1)S(1)} collective-permute-done((f16[2,64,768]{2,1,0:T(8,128)(2,1)S(1)}, f16[2,64,768]{2,1,0:T(8,128)(2,1)S(1)}, u32[]{:S(2)}, u32[]{:S(2)}) %collective-permute-start.11) | collective-permute-done | bytes 196640 | tf_op jit(solution)/shard_map/ppermute | solution.py:50
  55.8 4.0 %attend.3 = (f32[1,64,512]{2,1,0:T(8,128)S(1)}, bf16[1,64,640]{2,1,0:T(8,128)(2,1)S(1)}, f32[1,64,128]{2,1,0:T(8,128)S(1)}) custom-call(f32[2,64,512]{2,1,0:T(8,128)S(1)} %maximum_add_fusion.1.q, f32[2,64,256]{2,1,0:T(8,128)S(1)} %pad_maximum_fusion.3.kv, f32[4,64,128]{2,1,0:T(8,128)S(1)} %get-tuple-element.58.cosine, ...), custom_call_target="tpu_custom_call" | custom-call | flops 4429185024 | bytes 1048576 | tf_op jit(solution)/shard_map/attend/pallas_call | solution.py:369
  59.8 0.1 collective-permute-start.16
  59.9 4.0 %attend.2 = (f32[1,64,512]{2,1,0:T(8,128)S(1)}, bf16[1,64,640]{2,1,0:T(8,128)(2,1)S(1)}, f32[1,64,128]{2,1,0:T(8,128)S(1)}) custom-call(f32[2,64,512]{2,1,0:T(8,128)S(1)} %maximum_add_fusion.q, f32[2,64,256]{2,1,0:T(8,128)S(1)} %pad_maximum_fusion.3.kv, f32[4,64,128]{2,1,0:T(8,128)S(1)} %get-tuple-element.58.cosine, ...), custom_call_target="tpu_custom_call" | custom-call | flops 4429185024 | bytes 1048576 | tf_op jit(solution)/shard_map/attend/pallas_call | solution.py:369
  63.9 3.0 %collective-permute-start.13 = (bf16[1,64,640]{2,1,0:T(8,128)(2,1)S(1)}, bf16[1,64,640]{2,1,0:T(8,128)(2,1)S(1)}, u32[]{:S(2)}, u32[]{:S(2)}) collective-permute-start(bf16[1,64,640]{2,1,0:T(8,128)(2,1)S(1)} %get-tuple-element.41), channel_id=1, source_target_pairs={{0,2},{1,3},{2,0},{3,1},{4,6},{5,7},{6,4},{7,5},{8,10},{9,11},{10,... | collective-permute-start | bytes 245768 | tf_op jit(solution)/shard_map/ppermute | solution.py:50
  66.9 2.6 %collective-permute-done.13.refs_1_ = bf16[1,64,640]{2,1,0:T(8,128)(2,1)S(1)} collective-permute-done((bf16[1,64,640]{2,1,0:T(8,128)(2,1)S(1)}, bf16[1,64,640]{2,1,0:T(8,128)(2,1)S(1)}, u32[]{:S(2)}, u32[]{:S(2)}) %collective-permute-start.13) | collective-permute-done | bytes 81952 | tf_op jit(solution)/shard_map/ppermute | solution.py:50
  69.5 0.9 %finish.1 = bf16[8,8,1024]{2,1,0:T(8,128)(2,1)S(1)} custom-call(s32[4]{0:T(128)S(1)} %pad_add_fusion.ids, f32[1,64,512]{2,1,0:T(8,128)S(1)} %get-tuple-element.40.refs_0_, bf16[1,64,640]{2,1,0:T(8,128)(2,1)S(1)} %collective-permute-done.13.refs_1_, f32[1,64,128]{2,1,0:T(8,128)S(1)} %get-tuple-element.42.refs_2_, ...), custom_call_target="tpu_custom_call" | custom-call | tf_op jit(solution)/shard_map/finish/pallas_call | solution.py:485
  70.4 8.9 %all_to_all.5 = bf16[8,8,1024]{2,1,0:T(8,128)(2,1)S(1)} all-to-all(bf16[8,8,1024]{2,1,0:T(8,128)(2,1)S(1)} %finish.1), channel_id=1, replica_groups=mesh['wide'=8,'blk'=4] {'wide'}, dimensions={0} | all-to-all | bytes 262144 | tf_op jit(solution)/shard_map/all_to_all | solution.py:623
  79.3 0.7 copy.13
  (35 shorter events, 0.4 us)
Async XLA Ops:
  1.8 11.9 %copy-start.3 = (bf16[8,2048]{1,0:T(8,128)(2,1)S(1)}, bf16[8,2048]{1,0:T(8,128)(2,1)}, u32[]{:S(2)}) copy-start(bf16[8,2048]{1,0:T(8,128)(2,1)} %get-tuple-element.31) | copy-start | bytes 98308
  1.8 9.4 %collective-permute-start.1 = (bf16[8,2176]{1,0:T(8,128)(2,1)}, bf16[8,2176]{1,0:T(8,128)(2,1)S(1)}, u32[]{:S(2)}, u32[]{:S(2)}) collective-permute-start(bf16[8,2176]{1,0:T(8,128)(2,1)} %get-tuple-element.29), channel_id=1, source_target_pairs={{0,2},{1,3},{2,0},{3,1},{4,6},{5,7},{6,4},{7,5},{8,10},{9,11},{10,... | collective-permute-start | bytes 104456 | tf_op jit(solution)/shard_map/ppermute | solution.py:50
  5.8 5.4 %collective-permute-start = (bf16[8,2048]{1,0:T(8,128)(2,1)}, bf16[8,2048]{1,0:T(8,128)(2,1)S(1)}, u32[]{:S(2)}, u32[]{:S(2)}) collective-permute-start(bf16[8,2048]{1,0:T(8,128)(2,1)} %get-tuple-element.28), channel_id=1, source_target_pairs={{0,1},{1,0},{2,3},{3,2},{4,5},{5,4},{6,7},{7,6},{8,9},{9,8},{10,11... | collective-permute-start | bytes 98312 | tf_op jit(solution)/shard_map/ppermute | solution.py:50
  7.4 6.3 %collective-permute-start.2 = (bf16[8,2048]{1,0:T(8,128)(2,1)}, bf16[8,2048]{1,0:T(8,128)(2,1)S(1)}, u32[]{:S(2)}, u32[]{:S(2)}) collective-permute-start(bf16[8,2048]{1,0:T(8,128)(2,1)} %get-tuple-element.30), channel_id=1, source_target_pairs={{0,3},{1,2},{2,1},{3,0},{4,7},{5,6},{6,5},{7,4},{8,11},{9,10},{10,... | collective-permute-start | bytes 98312 | tf_op jit(solution)/shard_map/ppermute | solution.py:50
  8.7 14.0 %slice-start = ((bf16[2048,1024]{1,0:T(8,128)(2,1)}), bf16[2048,512]{1,0:T(8,128)(2,1)S(1)}, s32[]{:S(2)}) async-start(bf16[2048,1024]{1,0:T(8,128)(2,1)} %weights.1), calls=%async_computation.1 | async-start | bytes 4194304 | tf_op jit(solution)/shard_map/slice | solution.py:561
  8.9 46.9 %collective-permute-start.12 = (bf16[2,2048,128]{2,1,0:T(8,128)(2,1)S(1)}, bf16[2,2048,128]{2,1,0:T(8,128)(2,1)}, u32[]{:S(2)}, u32[]{:S(2)}) collective-permute-start(bf16[2,2048,128]{2,1,0:T(8,128)(2,1)S(1)} %prepare.1.own), channel_id=1, source_target_pairs={{0,1},{1,0},{2,3},{3,2},{4,5},{5,4},{6,7},{7,6},{8,9},{9,8},{10,11... | collective-permute-start | bytes 3145736 | tf_op jit(solution)/shard_map/ppermute | solution.py:50
  13.7 5.8 %collective-permute-start.4 = (bf16[4,8,2048]{2,1,0:T(8,128)(2,1)S(1)}, bf16[4,8,2048]{2,1,0:T(8,128)(2,1)S(1)}, u32[]{:S(2)}, u32[]{:S(2)}) collective-permute-start(bf16[4,8,2048]{2,1,0:T(8,128)(2,1)S(1)} %pad_maximum_fusion.2.refs_0_), channel_id=1, source_target_pairs={{0,8},{4,12},{8,0},{12,4},{16,24},{20,28},{24,16},{28,20},{1,9},{5... | collective-permute-start | bytes 393224 | tf_op jit(solution)/shard_map/ppermute | solution.py:50
  15.2 5.5 %collective-permute-start.6 = (bf16[4,8,2048]{2,1,0:T(8,128)(2,1)S(1)}, bf16[4,8,2048]{2,1,0:T(8,128)(2,1)S(1)}, u32[]{:S(2)}, u32[]{:S(2)}) collective-permute-start(bf16[4,8,2048]{2,1,0:T(8,128)(2,1)S(1)} %pad_maximum_fusion.2.refs_0_), channel_id=1, source_target_pairs={{0,16},{4,20},{8,24},{12,28},{16,0},{20,4},{24,8},{28,12},{1,17},{... | collective-permute-start | bytes 393224 | tf_op jit(solution)/shard_map/ppermute | solution.py:50
  16.8 5.9 %collective-permute-start.8 = (bf16[4,8,2048]{2,1,0:T(8,128)(2,1)S(1)}, bf16[4,8,2048]{2,1,0:T(8,128)(2,1)S(1)}, u32[]{:S(2)}, u32[]{:S(2)}) collective-permute-start(bf16[4,8,2048]{2,1,0:T(8,128)(2,1)S(1)} %pad_maximum_fusion.2.refs_0_), channel_id=1, source_target_pairs={{0,24},{4,28},{8,16},{12,20},{16,8},{20,12},{24,0},{28,4},{1,25},{... | collective-permute-start | bytes 393224 | tf_op jit(solution)/shard_map/ppermute | solution.py:50
  17.2 5.7 %collective-permute-start.3 = (bf16[4,8,2048]{2,1,0:T(8,128)(2,1)S(1)}, bf16[4,8,2048]{2,1,0:T(8,128)(2,1)S(1)}, u32[]{:S(2)}, u32[]{:S(2)}) collective-permute-start(bf16[4,8,2048]{2,1,0:T(8,128)(2,1)S(1)} %pad_maximum_fusion.2.refs_0_), channel_id=1, source_target_pairs={{0,4},{4,0},{8,12},{12,8},{16,20},{20,16},{24,28},{28,24},{1,5},{5... | collective-permute-start | bytes 393224 | tf_op jit(solution)/shard_map/ppermute | solution.py:50
  19.5 3.5 %collective-permute-start.5 = (bf16[4,8,2048]{2,1,0:T(8,128)(2,1)S(1)}, bf16[4,8,2048]{2,1,0:T(8,128)(2,1)S(1)}, u32[]{:S(2)}, u32[]{:S(2)}) collective-permute-start(bf16[4,8,2048]{2,1,0:T(8,128)(2,1)S(1)} %collective-permute-done.4.refs_2_), channel_id=1, source_target_pairs={{0,4},{4,0},{8,12},{12,8},{16,20},{20,16},{24,28},{28,24},{1,5},{5... | collective-permute-start | bytes 393224 | tf_op jit(solution)/shard_map/ppermute | solution.py:50
  20.7 2.2 %collective-permute-start.7 = (bf16[4,8,2048]{2,1,0:T(8,128)(2,1)S(1)}, bf16[4,8,2048]{2,1,0:T(8,128)(2,1)S(1)}, u32[]{:S(2)}, u32[]{:S(2)}) collective-permute-start(bf16[4,8,2048]{2,1,0:T(8,128)(2,1)S(1)} %collective-permute-done.6.refs_4_), channel_id=1, source_target_pairs={{0,4},{4,0},{8,12},{12,8},{16,20},{20,16},{24,28},{28,24},{1,5},{5... | collective-permute-start | bytes 393224 | tf_op jit(solution)/shard_map/ppermute | solution.py:50
  22.6 1.3 %collective-permute-start.9 = (bf16[4,8,2048]{2,1,0:T(8,128)(2,1)S(1)}, bf16[4,8,2048]{2,1,0:T(8,128)(2,1)S(1)}, u32[]{:S(2)}, u32[]{:S(2)}) collective-permute-start(bf16[4,8,2048]{2,1,0:T(8,128)(2,1)S(1)} %collective-permute-done.8.refs_6_), channel_id=1, source_target_pairs={{0,4},{4,0},{8,12},{12,8},{16,20},{20,16},{24,28},{28,24},{1,5},{5... | collective-permute-start | bytes 393224 | tf_op jit(solution)/shard_map/ppermute | solution.py:50
  22.6 2.4 %copy-start = (bf16[2048,1024]{1,0:T(8,128)(2,1)S(1)}, bf16[2048,1024]{1,0:T(8,128)(2,1)}, u32[]{:S(2)}) copy-start(bf16[2048,1024]{1,0:T(8,128)(2,1)} %weights.1) | copy-start | bytes 12582916
  25.0 3.6 %copy-start.1 = (s32[1,64]{1,0:T(1,128)S(1)}, s32[1,64]{1,0:T(1,128)}, u32[]{:S(2)}) copy-start(s32[1,64]{1,0:T(1,128)} %reach.3) | copy-start | bytes 772
  25.0 3.6 %copy-start.2 = (s32[16]{0:T(128)S(1)}, s32[16]{0:T(128)}, u32[]{:S(2)}) copy-start(s32[16]{0:T(128)} %passkey.1) | copy-start | bytes 196
  26.3 11.9 %collective-permute-start.14 = (f16[2,64,512]{2,1,0:T(8,128)(2,1)S(1)}, f16[2,64,512]{2,1,0:T(8,128)(2,1)S(1)}, u32[]{:S(2)}, u32[]{:S(2)}) collective-permute-start(f16[2,64,512]{2,1,0:T(8,128)(2,1)S(1)} %multiply_convert_fusion.2), channel_id=1, source_target_pairs={{0,1},{1,0},{2,3},{3,2},{4,5},{5,4},{6,7},{7,6},{8,9},{9,8},{10,11... | collective-permute-start | bytes 393224 | tf_op jit(solution)/shard_map/ppermute | solution.py:50
  26.4 18.4 %collective-permute-start.10 = (f16[2,64,1024]{2,1,0:T(8,128)(2,1)S(1)}, f16[2,64,1024]{2,1,0:T(8,128)(2,1)S(1)}, u32[]{:S(2)}, u32[]{:S(2)}) collective-permute-start(f16[2,64,1024]{2,1,0:T(8,128)(2,1)S(1)} %multiply_convert_fusion), channel_id=1, source_target_pairs={{0,1},{1,0},{2,3},{3,2},{4,5},{5,4},{6,7},{7,6},{8,9},{9,8},{10,11... | collective-permute-start | bytes 786440 | tf_op jit(solution)/shard_map/ppermute | solution.py:50
  38.3 8.6 %collective-permute-start.15 = (f16[2,64,512]{2,1,0:T(8,128)(2,1)S(1)}, f16[2,64,512]{2,1,0:T(8,128)(2,1)S(1)}, u32[]{:S(2)}, u32[]{:S(2)}) collective-permute-start(f16[2,64,512]{2,1,0:T(8,128)(2,1)S(1)} %multiply_convert_fusion.1), channel_id=1, source_target_pairs={{0,2},{1,3},{2,0},{3,1},{4,6},{5,7},{6,4},{7,5},{8,10},{9,11},{10,... | collective-permute-start | bytes 393224 | tf_op jit(solution)/shard_map/ppermute | solution.py:50
  47.0 8.7 %collective-permute-start.11 = (f16[2,64,768]{2,1,0:T(8,128)(2,1)S(1)}, f16[2,64,768]{2,1,0:T(8,128)(2,1)S(1)}, u32[]{:S(2)}, u32[]{:S(2)}) collective-permute-start(f16[2,64,768]{2,1,0:T(8,128)(2,1)S(1)} %pad_maximum_fusion.1), channel_id=1, source_target_pairs={{0,2},{1,3},{2,0},{3,1},{4,6},{5,7},{6,4},{7,5},{8,10},{9,11},{10,... | collective-permute-start | bytes 589832 | tf_op jit(solution)/shard_map/ppermute | solution.py:50
  59.8 7.1 %collective-permute-start.16 = (bf16[1,64,640]{2,1,0:T(8,128)(2,1)S(1)}, bf16[1,64,640]{2,1,0:T(8,128)(2,1)S(1)}, u32[]{:S(2)}, u32[]{:S(2)}) collective-permute-start(bf16[1,64,640]{2,1,0:T(8,128)(2,1)S(1)} %get-tuple-element.47), channel_id=1, source_target_pairs={{0,2},{1,3},{2,0},{3,1},{4,6},{5,7},{6,4},{7,5},{8,10},{9,11},{10,... | collective-permute-start | bytes 245768 | tf_op jit(solution)/shard_map/ppermute | solution.py:50
  63.9 5.6 %collective-permute-start.13 = (bf16[1,64,640]{2,1,0:T(8,128)(2,1)S(1)}, bf16[1,64,640]{2,1,0:T(8,128)(2,1)S(1)}, u32[]{:S(2)}, u32[]{:S(2)}) collective-permute-start(bf16[1,64,640]{2,1,0:T(8,128)(2,1)S(1)} %get-tuple-element.41), channel_id=1, source_target_pairs={{0,2},{1,3},{2,0},{3,1},{4,6},{5,7},{6,4},{7,5},{8,10},{9,11},{10,... | collective-permute-start | bytes 245768 | tf_op jit(solution)/shard_map/ppermute | solution.py:50

commit v3 on v2

--- a/solution.py
+++ b/solution.py
@@ -95,22 +95,46 @@
     )(hidden, gain, reach)
 
 
-def prepare_kernel(keys, values, out):
+def prepare_kernel(keys, values, out, first):
+    size = first.shape[1]
     out[0] = keys[...]
+    first[0] = keys[:size]
     for at in range(0, values.shape[0], HEAD_WIDTH):
-        part = values[at : at + HEAD_WIDTH].astype(F32)
-        out[1, at : at + HEAD_WIDTH] = part.T.astype(BF16)
-
-
-def prepare(keys, values):
+        part = values[at : at + HEAD_WIDTH].astype(F32).T.astype(BF16)
+        out[1, at : at + HEAD_WIDTH] = part
+        if at < size:
+            first[1, at : at + HEAD_WIDTH] = part
+
+
+def prepare(keys, values, size):
     return pl.pallas_call(
         prepare_kernel,
         in_specs=vmem(2),
-        out_specs=vmem()[0],
-        out_shape=jax.ShapeDtypeStruct((2, *keys.shape), BF16),
+        out_specs=vmem(2),
+        out_shape=[
+            jax.ShapeDtypeStruct((2, *keys.shape), BF16),
+            jax.ShapeDtypeStruct((2, size, keys.shape[1]), BF16),
+        ],
         compiler_params=pltpu.CompilerParams(vmem_limit_bytes=6 * MEBI),
         name="prepare",
     )(keys, values)
+
+
+def rest_kernel(held, *refs):
+    out = refs[-1]
+    size = out.shape[1]
+    out[...] = held[:, held.shape[1] - size :]
+
+
+def rest(held, size, earlier):
+    return pl.pallas_call(
+        rest_kernel,
+        in_specs=vmem(1) + [pl.BlockSpec(memory_space=pl.ANY)] * len(earlier),
+        out_specs=vmem()[0],
+        out_shape=jax.ShapeDtypeStruct((2, size, held.shape[2]), BF16),
+        compiler_params=pltpu.CompilerParams(vmem_limit_bytes=6 * MEBI),
+        name="rest",
+    )(held, *earlier)
 
 
 def mask_kernel(cached, groups, ids, passkey, reach, *refs):
@@ -260,10 +284,17 @@
     return x * cosine + pltpu.roll(x, HEAD_WIDTH // 2, 1) * sine
 
 
-def attend_kernel(together, q, kv, cosine, sine, bias, own, far, o_keep,
+def attend_kernel(together, q, kv, cosine, sine, bias, own, far_first, far_last, o_keep,
                    o_send, stats_keep, scores, k_new, v_new, pair, arrived):
-    fetch = pltpu.make_async_copy(far, pair, arrived)
-    fetch.start()
+    early = far_first.shape[1]
+    fetches = {}
+    for n, (far, at) in enumerate(((far_first, 0), (far_last, early))):
+        for side in range(2):
+            fetch = pltpu.make_async_copy(
+                far.at[side], pair.at[side, pl.ds(at, far.shape[1])], arrived.at[2 * n + side]
+            )
+            fetch.start()
+            fetches.setdefault(own.shape[1] + at, []).append(fetch)
     half, count, columns = q.shape
     rows = half * count
     cached = own.shape[1]
@@ -278,7 +309,7 @@
     for at in range(0, window, HEAD_WIDTH):
         v_new[at : at + HEAD_WIDTH] = values[at : at + HEAD_WIDTH].T.astype(BF16)
     scale = math.log2(math.e) / math.sqrt(HEAD_WIDTH)
-    chunk = min(256, cached)
+    chunk = min(256, cached // 2)
     spans = [
         (base + at, chunk, held.at[0], held.at[1], at)
         for held, base in ((own, 0), (pair, cached))
@@ -298,8 +329,9 @@
         queries = jnp.concatenate(queries, axis=0)
         top = jnp.full((8, width), lowest_max, F32)
         for at, size, keys, _, start in spans:
-            if first == 0 and at == cached:
-                fetch.wait()
+            if first == 0:
+                for fetch in fetches.get(at, ()):
+                    fetch.wait()
             product = lax.dot_general(
                 keys[start : start + size],
                 queries,
@@ -352,7 +384,7 @@
             o_send[j - half // 2, :, columns:] = part.astype(BF16)
 
 
-def attend(q, kv, cosine, sine, bias, own, pair):
+def attend(q, kv, cosine, sine, bias, own, first, last):
     half, count, columns = q.shape
     rows = half * count
     total = bias.shape[0]
@@ -364,19 +396,19 @@
         jax.ShapeDtypeStruct((out_half, count, columns + HEAD_WIDTH), BF16),
         jax.ShapeDtypeStruct((out_half, count, HEAD_WIDTH), F32),
     ]
-    ins = (q, kv, cosine, sine, bias, own, pair)
+    ins = (q, kv, cosine, sine, bias, own, first, last)
     scores = jax.ShapeDtypeStruct((total, together * rows), F32)
     return pl.pallas_call(
         functools.partial(attend_kernel, together),
         out_shape=outs,
-        in_specs=vmem(len(ins) - 1) + [pl.BlockSpec(memory_space=pl.ANY)],
+        in_specs=vmem(len(ins) - 2) + [pl.BlockSpec(memory_space=pl.ANY)] * 2,
         out_specs=vmem(3),
         scratch_shapes=[
             pltpu.VMEM(scores.shape, F32),
             pltpu.VMEM((2 * count, HEAD_WIDTH), BF16),
             pltpu.VMEM((2 * count, HEAD_WIDTH), BF16),
-            pltpu.VMEM(pair.shape, BF16),
-            pltpu.SemaphoreType.DMA(()),
+            pltpu.VMEM(own.shape, BF16),
+            pltpu.SemaphoreType.DMA((4,)),
         ],
         compiler_params=params(*ins, *outs, scores),
         cost_estimate=pl.CostEstimate(
@@ -539,11 +571,14 @@
         (slices, cache_key, prefix_value_cache)
     )
     base = kv_head * HEAD_WIDTH
-    cache = prepare(
+    chunk = min(256, cached // 2)
+    early = cached * 3 // 4 // chunk * chunk
+    cache, first_rows = prepare(
         lax.dynamic_slice_in_dim(cache_key, base, HEAD_WIDTH, 1),
         lax.dynamic_slice_in_dim(prefix_value_cache, base, HEAD_WIDTH, 1),
+        early,
     )
-    cache_pair = swapped(cache, "blk", 1)
+    first_rows = swapped(first_rows, "blk", 1)
     width = features // blocks
     own = jnp.stack([slices[0]] + [array[:, :width] for array in sent])
     own, first_weights, key_weight_matrix, value_weight_matrix = lax.optimization_barrier(
@@ -581,9 +616,10 @@
     pair = 2 * HEAD_WIDTH
     order = list(range(chunks))
     got = {c: swapped(narrow(projected[c][1]), "blk", 1) for c in order}
-    queries = {}
+    queries, sums = {}, []
     for c in order:
         keep = projected[c][0] + widen(got[c])
+        sums.append(keep)
         if c == 0:
             even = keep[:, :, part : part + pair]
             odd = keep[:, :, part + pair :]
@@ -610,9 +646,10 @@
         if c == 0:
             kv = jnp.concatenate([even, odd], axis=0)
         queries[c] = keep
+    last_rows = swapped(rest(cache, cached - early, sums[-1:]), "blk", 1)
     parts = {}
     for c in range(chunks):
-        keep, send, stats = attend(queries[c], kv, cosine, sine, bias, cache, cache_pair)
+        keep, send, stats = attend(queries[c], kv, cosine, sine, bias, cache, first_rows, last_rows)
         bit = half // 2
         while bit > 1:
             keep, send, stats = merge(keep, swapped(send, "blk", 2 * bit), stats)

time: 80.3 us -> 77.2 us (0.961)
  waiting for transfers between devices: 33.2 us -> 25.6 us
  starting transfers between devices: 17.5 us -> 20 us
    ppermute x17 -> x18, waiting for transfers between devices: 33.2 us -> 25.6 us  [swapped(): lax.ppermute(block, axis, [(i, i ^ mask) for i in range(lax.axis_size(axi...]
    ppermute x17 -> x18, starting transfers between devices: 17.5 us -> 20 us  [swapped(): lax.ppermute(block, axis, [(i, i ^ mask) for i in range(lax.axis_size(axi...]
    pallas_call x1 -> x2, Pallas kernels: 0.21 us -> 1.18 us  [the longest x1 1.16 us: prepare(): pl.pallas_call(prepare_kernel, in_specs=vmem(2), out_specs=vmem(2), out_s...]
  transfers between devices with their start and end apart: 17 -> 18, of which waited for: 10 -> 10; matrix products, arithmetic and copies ran while one was open for 5% -> 6% of each run, Pallas kernels for 10% -> 11%
where the time goes in v3:
time: 77.2 us; the launch traced here: 76.9 us
  waiting for transfers between devices  25.6 us (33%)
  starting transfers between devices  20 us (26%)
  Pallas kernels  15.3 us (20%)
  blocking collectives  9.51 us (12%)
  local copies, waits for them, and re-layouts  3.31 us (4%)
  other arithmetic  2.19 us (3%)
  between operations  0.96 us (1%)
    ppermute x18, waiting for transfers between devices, swapped(): lax.ppermute(block, axis, [(i, i ^ mask) for i in range(lax.axis_size(axi...  25.6 us
    ppermute x18, starting transfers between devices, swapped(): lax.ppermute(block, axis, [(i, i ^ mask) for i in range(lax.axis_size(axi...  20 us
    all_to_all x1, blocking collectives, local(): lax.all_to_all(ready, 'wide', split_axis=0, concat_axis=0, tiled=True)  9.51 us
    pallas_call x2, Pallas kernels, attend(): pl.pallas_call(functools.partial(attend_kernel, together), out_shape=outs...  7.77 us
    pallas_call x1, Pallas kernels, norm(): pl.pallas_call(norm_kernel, out_shape=[jax.ShapeDtypeStruct((rows, size),...  1.76 us
  transfers between devices with their start and end apart: 18, of which 10 were waited for; matrix products, arithmetic and copies ran while one was open for 6% of the time, Pallas kernels for 11%

profile of v3, /device:TPU:0, one launch (start us, length us, event | category | flops | bytes accessed | tf_op | source)
XLA Modules:
  0.0 76.9 jit_solution(5572483668124799706)
XLA Ops:
  0.0 1.8 %norm.1 = (bf16[8,2048]{1,0:T(8,128)(2,1)}, bf16[8,2048]{1,0:T(8,128)(2,1)}, bf16[8,2176]{1,0:T(8,128)(2,1)}, bf16[8,2048]{1,0:T(8,128)(2,1)}) custom-call(bf16[1,8,8192]{2,1,0:T(8,128)(2,1)} %hidden.1, f32[1,8192]{1,0:T(1,128)} %bitcast.15, s32[1,64]{1,0:T(1,128)} %reach.3), custom_call_target="tpu_custom_call" | custom-call | tf_op jit(solution)/shard_map/norm/pallas_call | solution.py:87
  1.8 4.0 %collective-permute-start.1 = (bf16[8,2176]{1,0:T(8,128)(2,1)}, bf16[8,2176]{1,0:T(8,128)(2,1)S(1)}, u32[]{:S(2)}, u32[]{:S(2)}) collective-permute-start(bf16[8,2176]{1,0:T(8,128)(2,1)} %get-tuple-element.31), channel_id=1, source_target_pairs={{0,2},{1,3},{2,0},{3,1},{4,6},{5,7},{6,4},{7,5},{8,10},{9,11},{10,... | collective-permute-start | bytes 104456 | tf_op jit(solution)/shard_map/ppermute | solution.py:50
  5.8 1.6 %collective-permute-start = (bf16[8,2048]{1,0:T(8,128)(2,1)}, bf16[8,2048]{1,0:T(8,128)(2,1)S(1)}, u32[]{:S(2)}, u32[]{:S(2)}) collective-permute-start(bf16[8,2048]{1,0:T(8,128)(2,1)} %get-tuple-element.30), channel_id=1, source_target_pairs={{0,1},{1,0},{2,3},{3,2},{4,5},{5,4},{6,7},{7,6},{8,9},{9,8},{10,11... | collective-permute-start | bytes 98312 | tf_op jit(solution)/shard_map/ppermute | solution.py:50
  7.4 0.0 collective-permute-start.2
  7.4 1.3 %constant_dynamic-slice_fusion = (bf16[2048,128]{1,0:T(8,128)(2,1)S(1)}, bf16[2048,128]{1,0:T(8,128)(2,1)S(1)}) fusion(bf16[2048,1024]{1,0:T(8,128)(2,1)} %param.16, s32[]{:T(128)S(6)} %select_n.41, bf16[2048,1024]{1,0:T(8,128)(2,1)} %param.15), kind=kLoop, calls=%fused_computation.29 | loop fusion | bytes 2097156 | tf_op jit(solution)/shard_map/dynamic_slice | solution.py:578
  8.7 0.0 slice-start
  8.7 1.2 %prepare.1 = (bf16[2,2048,128]{2,1,0:T(8,128)(2,1)S(1)}, bf16[2,1536,128]{2,1,0:T(8,128)(2,1)}) custom-call(bf16[2048,128]{1,0:T(8,128)(2,1)S(1)} %get-tuple-element.68.keys, bf16[2048,128]{1,0:T(8,128)(2,1)S(1)} %get-tuple-element.67.values), custom_call_target="tpu_custom_call" | custom-call | tf_op jit(solution)/shard_map/prepare/pallas_call | solution.py:110
  9.8 0.9 %collective-permute-start.12 = (bf16[2,1536,128]{2,1,0:T(8,128)(2,1)}, bf16[2,1536,128]{2,1,0:T(8,128)(2,1)}, u32[]{:S(2)}, u32[]{:S(2)}) collective-permute-start(bf16[2,1536,128]{2,1,0:T(8,128)(2,1)} %get-tuple-element.43), channel_id=1, source_target_pairs={{0,1},{1,0},{2,3},{3,2},{4,5},{5,4},{6,7},{7,6},{8,9},{9,8},{10,11... | collective-permute-start | bytes 2359304 | tf_op jit(solution)/shard_map/ppermute | solution.py:50
  11.4 0.6 sine_multiply_fusion
  12.1 0.0 collective-permute-done
  12.1 1.3 %collective-permute-done.2 = bf16[8,2048]{1,0:T(8,128)(2,1)S(1)} collective-permute-done((bf16[8,2048]{1,0:T(8,128)(2,1)}, bf16[8,2048]{1,0:T(8,128)(2,1)S(1)}, u32[]{:S(2)}, u32[]{:S(2)}) %collective-permute-start.2) | collective-permute-done | bytes 32800 | tf_op jit(solution)/shard_map/ppermute | solution.py:50
  13.4 0.8 %pad_maximum_fusion.2.refs_0_ = bf16[4,8,2048]{2,1,0:T(8,128)(2,1)S(1)} fusion(bf16[1,8,2048]{2,1,0:T(8,128)(2,1)S(1)} %bitcast.18, bf16[1,8,2048]{2,1,0:T(8,128)(2,1)S(1)} %slice_bitcast_fusion, bf16[1,8,2048]{2,1,0:T(8,128)(2,1)S(1)} %bitcast.17, bf16[1,8,2048]{2,1,0:T(8,128)(2,1)} %bitcast.16), kind=kLoop, calls=%fused_computation.12 | loop fusion | flops 196608 | bytes 262144 | tf_op jit(solution)/shard_map/stack | solution.py:583
  14.2 1.6 %collective-permute-start.4 = (bf16[4,8,2048]{2,1,0:T(8,128)(2,1)S(1)}, bf16[4,8,2048]{2,1,0:T(8,128)(2,1)S(1)}, u32[]{:S(2)}, u32[]{:S(2)}) collective-permute-start(bf16[4,8,2048]{2,1,0:T(8,128)(2,1)S(1)} %pad_maximum_fusion.2.refs_0_), channel_id=1, source_target_pairs={{0,8},{4,12},{8,0},{12,4},{16,24},{20,28},{24,16},{28,20},{1,9},{5... | collective-permute-start | bytes 393224 | tf_op jit(solution)/shard_map/ppermute | solution.py:50
  15.7 1.5 %collective-permute-start.6 = (bf16[4,8,2048]{2,1,0:T(8,128)(2,1)S(1)}, bf16[4,8,2048]{2,1,0:T(8,128)(2,1)S(1)}, u32[]{:S(2)}, u32[]{:S(2)}) collective-permute-start(bf16[4,8,2048]{2,1,0:T(8,128)(2,1)S(1)} %pad_maximum_fusion.2.refs_0_), channel_id=1, source_target_pairs={{0,16},{4,20},{8,24},{12,28},{16,0},{20,4},{24,8},{28,12},{1,17},{... | collective-permute-start | bytes 393224 | tf_op jit(solution)/shard_map/ppermute | solution.py:50
  17.3 0.5 collective-permute-start.8
  17.7 1.3 %constant_dynamic-slice_fusion.2 = (bf16[2048,128]{1,0:T(8,128)(2,1)S(1)}, bf16[2048,128]{1,0:T(8,128)(2,1)S(1)}) fusion(bf16[2048,1024]{1,0:T(8,128)(2,1)} %param.14, s32[]{:T(128)S(6)} %select_n.41, bf16[2048,1024]{1,0:T(8,128)(2,1)} %param.13), kind=kLoop, calls=%fused_computation.31 | loop fusion | bytes 2097156 | tf_op jit(solution)/shard_map/dynamic_slice | solution.py:598
  19.0 1.1 %collective-permute-done.4.refs_2_ = bf16[4,8,2048]{2,1,0:T(8,128)(2,1)S(1)} collective-permute-done((bf16[4,8,2048]{2,1,0:T(8,128)(2,1)S(1)}, bf16[4,8,2048]{2,1,0:T(8,128)(2,1)S(1)}, u32[]{:S(2)}, u32[]{:S(2)}) %collective-permute-start.4) | collective-permute-done | bytes 131104 | tf_op jit(solution)/shard_map/ppermute | solution.py:50
  20.2 0.0 collective-permute-start.5
  20.2 1.3 %collective-permute-done.6.refs_4_ = bf16[4,8,2048]{2,1,0:T(8,128)(2,1)S(1)} collective-permute-done((bf16[4,8,2048]{2,1,0:T(8,128)(2,1)S(1)}, bf16[4,8,2048]{2,1,0:T(8,128)(2,1)S(1)}, u32[]{:S(2)}, u32[]{:S(2)}) %collective-permute-start.6) | collective-permute-done | bytes 131104 | tf_op jit(solution)/shard_map/ppermute | solution.py:50
  21.4 1.7 %collective-permute-done.8.refs_6_ = bf16[4,8,2048]{2,1,0:T(8,128)(2,1)S(1)} collective-permute-done((bf16[4,8,2048]{2,1,0:T(8,128)(2,1)S(1)}, bf16[4,8,2048]{2,1,0:T(8,128)(2,1)S(1)}, u32[]{:S(2)}, u32[]{:S(2)}) %collective-permute-start.8) | collective-permute-done | bytes 131104 | tf_op jit(solution)/shard_map/ppermute | solution.py:50
  23.1 0.3 pad_maximum_fusion.refs_8_
  23.4 1.0 %collective-permute-done.9.refs_7_ = bf16[4,8,2048]{2,1,0:T(8,128)(2,1)S(1)} collective-permute-done((bf16[4,8,2048]{2,1,0:T(8,128)(2,1)S(1)}, bf16[4,8,2048]{2,1,0:T(8,128)(2,1)S(1)}, u32[]{:S(2)}, u32[]{:S(2)}) %collective-permute-start.9) | collective-permute-done | bytes 131104 | tf_op jit(solution)/shard_map/ppermute | solution.py:50
  24.5 1.0 %gather.1 = (bf16[256,2048]{1,0:T(8,128)(2,1)S(1)}, f32[2,64,1024]{2,1,0:T(8,128)S(1)}, f32[2,64,1024]{2,1,0:T(8,128)S(1)}) custom-call(bf16[4,8,2048]{2,1,0:T(8,128)(2,1)S(1)} %pad_maximum_fusion.2.refs_0_, bf16[4,8,2048]{2,1,0:T(8,128)(2,1)S(1)} %collective-permute-done.3.refs_1_, bf16[4,8,2048]{2,1,0:T(8,128)(2,1)S(1)} %collective-permute-done.4.refs_2_, ...), custom_call_target="tpu_custom_call" | custom-call | flops 1073741824 | bytes 2097152 | tf_op jit(solution)/shard_map/gather/pallas_call | solution.py:235
  25.5 0.0 copy-start.1
  25.5 0.0 copy-start.2
  25.5 1.2 %project.1 = (f32[2,64,512]{2,1,0:T(8,128)S(1)}, f32[2,64,512]{2,1,0:T(8,128)S(1)}) custom-call(bf16[256,2048]{1,0:T(8,128)(2,1)S(1)} %get-tuple-element.44.tokens, bf16[2048,1024]{1,0:T(8,128)(2,1)S(1)} %copy-done), custom_call_target="tpu_custom_call" | custom-call | flops 536870912 | bytes 2097152 | tf_op jit(solution)/shard_map/project/pallas_call | solution.py:264
  26.8 0.7 collective-permute-start.13
  27.5 1.5 %collective-permute-start.10 = (f16[2,64,1024]{2,1,0:T(8,128)(2,1)S(1)}, f16[2,64,1024]{2,1,0:T(8,128)(2,1)S(1)}, u32[]{:S(2)}, u32[]{:S(2)}) collective-permute-start(f16[2,64,1024]{2,1,0:T(8,128)(2,1)S(1)} %multiply_convert_fusion), channel_id=1, source_target_pairs={{0,1},{1,0},{2,3},{3,2},{4,5},{5,4},{6,7},{7,6},{8,9},{9,8},{10,11... | collective-permute-start | bytes 786440 | tf_op jit(solution)/shard_map/ppermute | solution.py:50
  29.0 0.1 pad_add_fusion.ids
  29.1 1.5 %mask.1.bias = f32[4224,128]{1,0:T(8,128)S(1)} custom-call(s32[4]{0:T(128)S(1)} %pad_add_fusion.ids, s32[16]{0:T(128)S(1)} %copy-done.2, s32[1,64]{1,0:T(1,128)S(1)} %copy-done.1, bf16[8,128]{1,0:T(8,128)(2,1)S(1)} %slice.80.refs_0_), custom_call_target="tpu_custom_call" | custom-call | tf_op jit(solution)/shard_map/mask/pallas_call | solution.py:195
  30.6 2.6 %collective-permute-done.13 = f16[2,64,512]{2,1,0:T(8,128)(2,1)S(1)} collective-permute-done((f16[2,64,512]{2,1,0:T(8,128)(2,1)S(1)}, f16[2,64,512]{2,1,0:T(8,128)(2,1)S(1)}, u32[]{:S(2)}, u32[]{:S(2)}) %collective-permute-start.13) | collective-permute-done | bytes 131104 | tf_op jit(solution)/shard_map/ppermute | solution.py:50
  33.2 0.1 multiply_convert_fusion.1
  33.2 2.8 %collective-permute-start.16 = (f16[2,64,512]{2,1,0:T(8,128)(2,1)S(1)}, f16[2,64,512]{2,1,0:T(8,128)(2,1)S(1)}, u32[]{:S(2)}, u32[]{:S(2)}) collective-permute-start(f16[2,64,512]{2,1,0:T(8,128)(2,1)S(1)} %get-tuple-element.53), channel_id=1, source_target_pairs={{0,2},{1,3},{2,0},{3,1},{4,6},{5,7},{6,4},{7,5},{8,10},{9,11},{10,... | collective-permute-start | bytes 393224 | tf_op jit(solution)/shard_map/ppermute | solution.py:50
  36.0 0.2 collective-permute-start.14
  36.2 5.3 %collective-permute-done.10 = f16[2,64,1024]{2,1,0:T(8,128)(2,1)S(1)} collective-permute-done((f16[2,64,1024]{2,1,0:T(8,128)(2,1)S(1)}, f16[2,64,1024]{2,1,0:T(8,128)(2,1)S(1)}, u32[]{:S(2)}, u32[]{:S(2)}) %collective-permute-start.10) | collective-permute-done | bytes 262176 | tf_op jit(solution)/shard_map/ppermute | solution.py:50
  41.6 0.1 multiply_add_fusion
  41.8 0.1 pad_maximum_fusion.1
  41.9 1.7 %collective-permute-start.11 = (f16[2,64,768]{2,1,0:T(8,128)(2,1)S(1)}, f16[2,64,768]{2,1,0:T(8,128)(2,1)S(1)}, u32[]{:S(2)}, u32[]{:S(2)}) collective-permute-start(f16[2,64,768]{2,1,0:T(8,128)(2,1)S(1)} %pad_maximum_fusion.1), channel_id=1, source_target_pairs={{0,2},{1,3},{2,0},{3,1},{4,6},{5,7},{6,4},{7,5},{8,10},{9,11},{10,... | collective-permute-start | bytes 589832 | tf_op jit(solution)/shard_map/ppermute | solution.py:50
  43.6 5.8 %collective-permute-done.11 = f16[2,64,768]{2,1,0:T(8,128)(2,1)S(1)} collective-permute-done((f16[2,64,768]{2,1,0:T(8,128)(2,1)S(1)}, f16[2,64,768]{2,1,0:T(8,128)(2,1)S(1)}, u32[]{:S(2)}, u32[]{:S(2)}) %collective-permute-start.11) | collective-permute-done | bytes 196640 | tf_op jit(solution)/shard_map/ppermute | solution.py:50
  49.5 1.3 %collective-permute-done.14.far_last = bf16[2,512,128]{2,1,0:T(8,128)(2,1)S(1)} collective-permute-done((bf16[2,512,128]{2,1,0:T(8,128)(2,1)S(1)}, bf16[2,512,128]{2,1,0:T(8,128)(2,1)S(1)}, u32[]{:S(2)}, u32[]{:S(2)}) %collective-permute-start.14) | collective-permute-done | bytes 262176 | tf_op jit(solution)/shard_map/ppermute | solution.py:50
  50.8 3.9 %attend.3 = (f32[1,64,512]{2,1,0:T(8,128)S(1)}, bf16[1,64,640]{2,1,0:T(8,128)(2,1)S(1)}, f32[1,64,128]{2,1,0:T(8,128)S(1)}) custom-call(f32[2,64,512]{2,1,0:T(8,128)S(1)} %maximum_add_fusion.1.q, f32[2,64,256]{2,1,0:T(8,128)S(1)} %pad_maximum_fusion.3.kv, f32[4,64,128]{2,1,0:T(8,128)S(1)} %get-tuple-element.64.cosine, ...), custom_call_target="tpu_custom_call" | custom-call | flops 4429185024 | bytes 1048576 | tf_op jit(solution)/shard_map/attend/pallas_call | solution.py:401
  54.7 1.8 %collective-permute-start.17 = (bf16[1,64,640]{2,1,0:T(8,128)(2,1)S(1)}, bf16[1,64,640]{2,1,0:T(8,128)(2,1)S(1)}, u32[]{:S(2)}, u32[]{:S(2)}) collective-permute-start(bf16[1,64,640]{2,1,0:T(8,128)(2,1)S(1)} %get-tuple-element.51), channel_id=1, source_target_pairs={{0,2},{1,3},{2,0},{3,1},{4,6},{5,7},{6,4},{7,5},{8,10},{9,11},{10,... | collective-permute-start | bytes 245768 | tf_op jit(solution)/shard_map/ppermute | solution.py:50
  56.5 3.9 %attend.2 = (f32[1,64,512]{2,1,0:T(8,128)S(1)}, bf16[1,64,640]{2,1,0:T(8,128)(2,1)S(1)}, f32[1,64,128]{2,1,0:T(8,128)S(1)}) custom-call(f32[2,64,512]{2,1,0:T(8,128)S(1)} %maximum_add_fusion.q, f32[2,64,256]{2,1,0:T(8,128)S(1)} %pad_maximum_fusion.3.kv, f32[4,64,128]{2,1,0:T(8,128)S(1)} %get-tuple-element.64.cosine, ...), custom_call_target="tpu_custom_call" | custom-call | flops 4429185024 | bytes 1048576 | tf_op jit(solution)/shard_map/attend/pallas_call | solution.py:401
  60.4 1.3 %collective-permute-start.15 = (bf16[1,64,640]{2,1,0:T(8,128)(2,1)S(1)}, bf16[1,64,640]{2,1,0:T(8,128)(2,1)S(1)}, u32[]{:S(2)}, u32[]{:S(2)}) collective-permute-start(bf16[1,64,640]{2,1,0:T(8,128)(2,1)S(1)} %get-tuple-element.48), channel_id=1, source_target_pairs={{0,2},{1,3},{2,0},{3,1},{4,6},{5,7},{6,4},{7,5},{8,10},{9,11},{10,... | collective-permute-start | bytes 245768 | tf_op jit(solution)/shard_map/ppermute | solution.py:50
  61.7 4.1 %collective-permute-done.15.refs_1_ = bf16[1,64,640]{2,1,0:T(8,128)(2,1)S(1)} collective-permute-done((bf16[1,64,640]{2,1,0:T(8,128)(2,1)S(1)}, bf16[1,64,640]{2,1,0:T(8,128)(2,1)S(1)}, u32[]{:S(2)}, u32[]{:S(2)}) %collective-permute-start.15) | collective-permute-done | bytes 81952 | tf_op jit(solution)/shard_map/ppermute | solution.py:50
  65.8 0.9 %finish.1 = bf16[8,8,1024]{2,1,0:T(8,128)(2,1)S(1)} custom-call(s32[4]{0:T(128)S(1)} %pad_add_fusion.ids, f32[1,64,512]{2,1,0:T(8,128)S(1)} %get-tuple-element.47.refs_0_, bf16[1,64,640]{2,1,0:T(8,128)(2,1)S(1)} %collective-permute-done.15.refs_1_, f32[1,64,128]{2,1,0:T(8,128)S(1)} %get-tuple-element.49.refs_2_, ...), custom_call_target="tpu_custom_call" | custom-call | tf_op jit(solution)/shard_map/finish/pallas_call | solution.py:517
  66.7 9.5 %all_to_all.5 = bf16[8,8,1024]{2,1,0:T(8,128)(2,1)S(1)} all-to-all(bf16[8,8,1024]{2,1,0:T(8,128)(2,1)S(1)} %finish.1), channel_id=1, replica_groups=mesh['wide'=8,'blk'=4] {'wide'}, dimensions={0} | all-to-all | bytes 262144 | tf_op jit(solution)/shard_map/all_to_all | solution.py:660
  76.2 0.7 copy.13
  (36 shorter events, 0.4 us)
Async XLA Ops:
  1.8 10.3 %collective-permute-start.1 = (bf16[8,2176]{1,0:T(8,128)(2,1)}, bf16[8,2176]{1,0:T(8,128)(2,1)S(1)}, u32[]{:S(2)}, u32[]{:S(2)}) collective-permute-start(bf16[8,2176]{1,0:T(8,128)(2,1)} %get-tuple-element.31), channel_id=1, source_target_pairs={{0,2},{1,3},{2,0},{3,1},{4,6},{5,7},{6,4},{7,5},{8,10},{9,11},{10,... | collective-permute-start | bytes 104456 | tf_op jit(solution)/shard_map/ppermute | solution.py:50
  5.8 6.3 %collective-permute-start = (bf16[8,2048]{1,0:T(8,128)(2,1)}, bf16[8,2048]{1,0:T(8,128)(2,1)S(1)}, u32[]{:S(2)}, u32[]{:S(2)}) collective-permute-start(bf16[8,2048]{1,0:T(8,128)(2,1)} %get-tuple-element.30), channel_id=1, source_target_pairs={{0,1},{1,0},{2,3},{3,2},{4,5},{5,4},{6,7},{7,6},{8,9},{9,8},{10,11... | collective-permute-start | bytes 98312 | tf_op jit(solution)/shard_map/ppermute | solution.py:50
  7.4 6.0 %collective-permute-start.2 = (bf16[8,2048]{1,0:T(8,128)(2,1)}, bf16[8,2048]{1,0:T(8,128)(2,1)S(1)}, u32[]{:S(2)}, u32[]{:S(2)}) collective-permute-start(bf16[8,2048]{1,0:T(8,128)(2,1)} %get-tuple-element.32), channel_id=1, source_target_pairs={{0,3},{1,2},{2,1},{3,0},{4,7},{5,6},{6,5},{7,4},{8,11},{9,10},{10,... | collective-permute-start | bytes 98312 | tf_op jit(solution)/shard_map/ppermute | solution.py:50
  8.7 14.5 %slice-start = ((bf16[2048,1024]{1,0:T(8,128)(2,1)}), bf16[2048,512]{1,0:T(8,128)(2,1)S(1)}, s32[]{:S(2)}) async-start(bf16[2048,1024]{1,0:T(8,128)(2,1)} %weights.1), calls=%async_computation.1 | async-start | bytes 4194304 | tf_op jit(solution)/shard_map/slice | solution.py:596
  9.8 41.0 %collective-permute-start.12 = (bf16[2,1536,128]{2,1,0:T(8,128)(2,1)}, bf16[2,1536,128]{2,1,0:T(8,128)(2,1)}, u32[]{:S(2)}, u32[]{:S(2)}) collective-permute-start(bf16[2,1536,128]{2,1,0:T(8,128)(2,1)} %get-tuple-element.43), channel_id=1, source_target_pairs={{0,1},{1,0},{2,3},{3,2},{4,5},{5,4},{6,7},{7,6},{8,9},{9,8},{10,11... | collective-permute-start | bytes 2359304 | tf_op jit(solution)/shard_map/ppermute | solution.py:50
  14.2 6.0 %collective-permute-start.4 = (bf16[4,8,2048]{2,1,0:T(8,128)(2,1)S(1)}, bf16[4,8,2048]{2,1,0:T(8,128)(2,1)S(1)}, u32[]{:S(2)}, u32[]{:S(2)}) collective-permute-start(bf16[4,8,2048]{2,1,0:T(8,128)(2,1)S(1)} %pad_maximum_fusion.2.refs_0_), channel_id=1, source_target_pairs={{0,8},{4,12},{8,0},{12,4},{16,24},{20,28},{24,16},{28,20},{1,9},{5... | collective-permute-start | bytes 393224 | tf_op jit(solution)/shard_map/ppermute | solution.py:50
  15.7 5.7 %collective-permute-start.6 = (bf16[4,8,2048]{2,1,0:T(8,128)(2,1)S(1)}, bf16[4,8,2048]{2,1,0:T(8,128)(2,1)S(1)}, u32[]{:S(2)}, u32[]{:S(2)}) collective-permute-start(bf16[4,8,2048]{2,1,0:T(8,128)(2,1)S(1)} %pad_maximum_fusion.2.refs_0_), channel_id=1, source_target_pairs={{0,16},{4,20},{8,24},{12,28},{16,0},{20,4},{24,8},{28,12},{1,17},{... | collective-permute-start | bytes 393224 | tf_op jit(solution)/shard_map/ppermute | solution.py:50
  17.3 5.9 %collective-permute-start.8 = (bf16[4,8,2048]{2,1,0:T(8,128)(2,1)S(1)}, bf16[4,8,2048]{2,1,0:T(8,128)(2,1)S(1)}, u32[]{:S(2)}, u32[]{:S(2)}) collective-permute-start(bf16[4,8,2048]{2,1,0:T(8,128)(2,1)S(1)} %pad_maximum_fusion.2.refs_0_), channel_id=1, source_target_pairs={{0,24},{4,28},{8,16},{12,20},{16,8},{20,12},{24,0},{28,4},{1,25},{... | collective-permute-start | bytes 393224 | tf_op jit(solution)/shard_map/ppermute | solution.py:50
  17.7 5.7 %collective-permute-start.3 = (bf16[4,8,2048]{2,1,0:T(8,128)(2,1)S(1)}, bf16[4,8,2048]{2,1,0:T(8,128)(2,1)S(1)}, u32[]{:S(2)}, u32[]{:S(2)}) collective-permute-start(bf16[4,8,2048]{2,1,0:T(8,128)(2,1)S(1)} %pad_maximum_fusion.2.refs_0_), channel_id=1, source_target_pairs={{0,4},{4,0},{8,12},{12,8},{16,20},{20,16},{24,28},{28,24},{1,5},{5... | collective-permute-start | bytes 393224 | tf_op jit(solution)/shard_map/ppermute | solution.py:50
  20.2 3.2 %collective-permute-start.5 = (bf16[4,8,2048]{2,1,0:T(8,128)(2,1)S(1)}, bf16[4,8,2048]{2,1,0:T(8,128)(2,1)S(1)}, u32[]{:S(2)}, u32[]{:S(2)}) collective-permute-start(bf16[4,8,2048]{2,1,0:T(8,128)(2,1)S(1)} %collective-permute-done.4.refs_2_), channel_id=1, source_target_pairs={{0,4},{4,0},{8,12},{12,8},{16,20},{20,16},{24,28},{28,24},{1,5},{5... | collective-permute-start | bytes 393224 | tf_op jit(solution)/shard_map/ppermute | solution.py:50
  21.4 2.0 %collective-permute-start.7 = (bf16[4,8,2048]{2,1,0:T(8,128)(2,1)S(1)}, bf16[4,8,2048]{2,1,0:T(8,128)(2,1)S(1)}, u32[]{:S(2)}, u32[]{:S(2)}) collective-permute-start(bf16[4,8,2048]{2,1,0:T(8,128)(2,1)S(1)} %collective-permute-done.6.refs_4_), channel_id=1, source_target_pairs={{0,4},{4,0},{8,12},{12,8},{16,20},{20,16},{24,28},{28,24},{1,5},{5... | collective-permute-start | bytes 393224 | tf_op jit(solution)/shard_map/ppermute | solution.py:50
  23.1 1.3 %collective-permute-start.9 = (bf16[4,8,2048]{2,1,0:T(8,128)(2,1)S(1)}, bf16[4,8,2048]{2,1,0:T(8,128)(2,1)S(1)}, u32[]{:S(2)}, u32[]{:S(2)}) collective-permute-start(bf16[4,8,2048]{2,1,0:T(8,128)(2,1)S(1)} %collective-permute-done.8.refs_6_), channel_id=1, source_target_pairs={{0,4},{4,0},{8,12},{12,8},{16,20},{20,16},{24,28},{28,24},{1,5},{5... | collective-permute-start | bytes 393224 | tf_op jit(solution)/shard_map/ppermute | solution.py:50
  23.1 2.4 %copy-start = (bf16[2048,1024]{1,0:T(8,128)(2,1)S(1)}, bf16[2048,1024]{1,0:T(8,128)(2,1)}, u32[]{:S(2)}) copy-start(bf16[2048,1024]{1,0:T(8,128)(2,1)} %weights.1) | copy-start | bytes 12582916
  25.5 3.6 %copy-start.1 = (s32[1,64]{1,0:T(1,128)S(1)}, s32[1,64]{1,0:T(1,128)}, u32[]{:S(2)}) copy-start(s32[1,64]{1,0:T(1,128)} %reach.3) | copy-start | bytes 772
  25.5 3.6 %copy-start.2 = (s32[16]{0:T(128)S(1)}, s32[16]{0:T(128)}, u32[]{:S(2)}) copy-start(s32[16]{0:T(128)} %passkey.1) | copy-start | bytes 196
  26.8 6.4 %collective-permute-start.13 = (f16[2,64,512]{2,1,0:T(8,128)(2,1)S(1)}, f16[2,64,512]{2,1,0:T(8,128)(2,1)S(1)}, u32[]{:S(2)}, u32[]{:S(2)}) collective-permute-start(f16[2,64,512]{2,1,0:T(8,128)(2,1)S(1)} %multiply_convert_fusion.2), channel_id=1, source_target_pairs={{0,1},{1,0},{2,3},{3,2},{4,5},{5,4},{6,7},{7,6},{8,9},{9,8},{10,11... | collective-permute-start | bytes 393224 | tf_op jit(solution)/shard_map/ppermute | solution.py:50
  27.5 14.1 %collective-permute-start.10 = (f16[2,64,1024]{2,1,0:T(8,128)(2,1)S(1)}, f16[2,64,1024]{2,1,0:T(8,128)(2,1)S(1)}, u32[]{:S(2)}, u32[]{:S(2)}) collective-permute-start(f16[2,64,1024]{2,1,0:T(8,128)(2,1)S(1)} %multiply_convert_fusion), channel_id=1, source_target_pairs={{0,1},{1,0},{2,3},{3,2},{4,5},{5,4},{6,7},{7,6},{8,9},{9,8},{10,11... | collective-permute-start | bytes 786440 | tf_op jit(solution)/shard_map/ppermute | solution.py:50
  33.2 8.5 %collective-permute-start.16 = (f16[2,64,512]{2,1,0:T(8,128)(2,1)S(1)}, f16[2,64,512]{2,1,0:T(8,128)(2,1)S(1)}, u32[]{:S(2)}, u32[]{:S(2)}) collective-permute-start(f16[2,64,512]{2,1,0:T(8,128)(2,1)S(1)} %get-tuple-element.53), channel_id=1, source_target_pairs={{0,2},{1,3},{2,0},{3,1},{4,6},{5,7},{6,4},{7,5},{8,10},{9,11},{10,... | collective-permute-start | bytes 393224 | tf_op jit(solution)/shard_map/ppermute | solution.py:50
  36.0 14.8 %collective-permute-start.14 = (bf16[2,512,128]{2,1,0:T(8,128)(2,1)S(1)}, bf16[2,512,128]{2,1,0:T(8,128)(2,1)S(1)}, u32[]{:S(2)}, u32[]{:S(2)}) collective-permute-start(bf16[2,512,128]{2,1,0:T(8,128)(2,1)S(1)} %rest.1), channel_id=1, source_target_pairs={{0,1},{1,0},{2,3},{3,2},{4,5},{5,4},{6,7},{7,6},{8,9},{9,8},{10,11... | collective-permute-start | bytes 786440 | tf_op jit(solution)/shard_map/ppermute | solution.py:50
  41.9 7.5 %collective-permute-start.11 = (f16[2,64,768]{2,1,0:T(8,128)(2,1)S(1)}, f16[2,64,768]{2,1,0:T(8,128)(2,1)S(1)}, u32[]{:S(2)}, u32[]{:S(2)}) collective-permute-start(f16[2,64,768]{2,1,0:T(8,128)(2,1)S(1)} %pad_maximum_fusion.1), channel_id=1, source_target_pairs={{0,2},{1,3},{2,0},{3,1},{4,6},{5,7},{6,4},{7,5},{8,10},{9,11},{10,... | collective-permute-start | bytes 589832 | tf_op jit(solution)/shard_map/ppermute | solution.py:50
  54.7 6.9 %collective-permute-start.17 = (bf16[1,64,640]{2,1,0:T(8,128)(2,1)S(1)}, bf16[1,64,640]{2,1,0:T(8,128)(2,1)S(1)}, u32[]{:S(2)}, u32[]{:S(2)}) collective-permute-start(bf16[1,64,640]{2,1,0:T(8,128)(2,1)S(1)} %get-tuple-element.51), channel_id=1, source_target_pairs={{0,2},{1,3},{2,0},{3,1},{4,6},{5,7},{6,4},{7,5},{8,10},{9,11},{10,... | collective-permute-start | bytes 245768 | tf_op jit(solution)/shard_map/ppermute | solution.py:50
  60.4 5.4 %collective-permute-start.15 = (bf16[1,64,640]{2,1,0:T(8,128)(2,1)S(1)}, bf16[1,64,640]{2,1,0:T(8,128)(2,1)S(1)}, u32[]{:S(2)}, u32[]{:S(2)}) collective-permute-start(bf16[1,64,640]{2,1,0:T(8,128)(2,1)S(1)} %get-tuple-element.48), channel_id=1, source_target_pairs={{0,2},{1,3},{2,0},{3,1},{4,6},{5,7},{6,4},{7,5},{8,10},{9,11},{10,... | collective-permute-start | bytes 245768 | tf_op jit(solution)/shard_map/ppermute | solution.py:50

commit v4 on v3

--- a/solution.py
+++ b/solution.py
@@ -495,33 +495,32 @@
     )(mine, other, mine_stats)
 
 
-def finish_kernel(chunks, ids, *refs):
+def finish_kernel(chunks, *refs):
+    me = lax.axis_index("wide")
     out = refs[-1]
     groups, rows, _ = out.shape
-    at = 0
+    heads = []
     for c in range(chunks):
         mine, other, stats = refs[3 * c : 3 * c + 3]
         joined, _, _ = merged(mine[0], other[0], stats[0])
-        for part in joined:
-            for m in range(groups):
-                out[ids[1] ^ m, :, at : at + HEAD_WIDTH] = part[m * rows : (m + 1) * rows].astype(
-                    BF16
-                )
-            at += HEAD_WIDTH
-
-
-def finish(ids, parts, groups):
+        heads += joined
+    whole = jnp.concatenate(heads, axis=1)
+    for m in range(groups):
+        out[me ^ m] = whole[m * rows : (m + 1) * rows].astype(BF16)
+
+
+def finish(parts, groups):
     count = parts[0][0].shape[1]
     columns = sum(part[0].shape[2] for part in parts)
     flat = [array for part in parts for array in part]
     return pl.pallas_call(
         functools.partial(finish_kernel, len(parts)),
         out_shape=jax.ShapeDtypeStruct((groups, count // groups, columns), BF16),
-        in_specs=[smem()] + vmem(len(flat)),
+        in_specs=vmem(len(flat)),
         out_specs=vmem()[0],
         compiler_params=params(*flat),
         name="finish",
-    )(ids, *flat)
+    )(*flat)
 
 
 def reordered(array, flip):
@@ -656,7 +655,7 @@
             bit //= 2
         parts[c] = (keep, swapped(send, "blk", 2), stats)
     parts = [parts[c] for c in range(chunks)]
-    ready = finish(ids, parts, groups)
+    ready = finish(parts, groups)
     ready = lax.all_to_all(ready, "wide", split_axis=0, concat_axis=0, tiled=True)
     return ready.transpose(1, 0, 2).reshape(1, rows, groups * columns)
 

time: 77.2 us -> 76.7 us (level)
  no operation moved by 1% of the time
where the time goes in v4:
time: 76.7 us; the launch traced here: 76.4 us
  waiting for transfers between devices  25.6 us (33%)
  starting transfers between devices  20 us (26%)
  Pallas kernels  14.8 us (19%)
  blocking collectives  9.51 us (12%)
  local copies, waits for them, and re-layouts  3.31 us (4%)
  other arithmetic  2.19 us (3%)
  between operations  0.96 us (1%)
    ppermute x18, waiting for transfers between devices, swapped(): lax.ppermute(block, axis, [(i, i ^ mask) for i in range(lax.axis_size(axi...  25.6 us
    ppermute x18, starting transfers between devices, swapped(): lax.ppermute(block, axis, [(i, i ^ mask) for i in range(lax.axis_size(axi...  20 us
    all_to_all x1, blocking collectives, local(): lax.all_to_all(ready, 'wide', split_axis=0, concat_axis=0, tiled=True)  9.51 us
    pallas_call x2, Pallas kernels, attend(): pl.pallas_call(functools.partial(attend_kernel, together), out_shape=outs...  7.77 us
    pallas_call x1, Pallas kernels, norm(): pl.pallas_call(norm_kernel, out_shape=[jax.ShapeDtypeStruct((rows, size),...  1.76 us
  transfers between devices with their start and end apart: 18, of which 10 were waited for; matrix products, arithmetic and copies ran while one was open for 6% of the time, Pallas kernels for 11%

profile of v4, /device:TPU:0, one launch (start us, length us, event | category | flops | bytes accessed | tf_op | source)
XLA Modules:
  0.0 76.4 jit_solution(13339439614579311885)
XLA Ops:
  0.0 1.8 %norm.1 = (bf16[8,2048]{1,0:T(8,128)(2,1)}, bf16[8,2048]{1,0:T(8,128)(2,1)}, bf16[8,2176]{1,0:T(8,128)(2,1)}, bf16[8,2048]{1,0:T(8,128)(2,1)}) custom-call(bf16[1,8,8192]{2,1,0:T(8,128)(2,1)} %hidden.1, f32[1,8192]{1,0:T(1,128)} %bitcast.15, s32[1,64]{1,0:T(1,128)} %reach.3), custom_call_target="tpu_custom_call" | custom-call | tf_op jit(solution)/shard_map/norm/pallas_call | solution.py:87
  1.8 4.0 %collective-permute-start.1 = (bf16[8,2176]{1,0:T(8,128)(2,1)}, bf16[8,2176]{1,0:T(8,128)(2,1)S(1)}, u32[]{:S(2)}, u32[]{:S(2)}) collective-permute-start(bf16[8,2176]{1,0:T(8,128)(2,1)} %get-tuple-element.31), channel_id=1, source_target_pairs={{0,2},{1,3},{2,0},{3,1},{4,6},{5,7},{6,4},{7,5},{8,10},{9,11},{10,... | collective-permute-start | bytes 104456 | tf_op jit(solution)/shard_map/ppermute | solution.py:50
  5.8 1.6 %collective-permute-start = (bf16[8,2048]{1,0:T(8,128)(2,1)}, bf16[8,2048]{1,0:T(8,128)(2,1)S(1)}, u32[]{:S(2)}, u32[]{:S(2)}) collective-permute-start(bf16[8,2048]{1,0:T(8,128)(2,1)} %get-tuple-element.30), channel_id=1, source_target_pairs={{0,1},{1,0},{2,3},{3,2},{4,5},{5,4},{6,7},{7,6},{8,9},{9,8},{10,11... | collective-permute-start | bytes 98312 | tf_op jit(solution)/shard_map/ppermute | solution.py:50
  7.4 0.0 collective-permute-start.2
  7.4 1.3 %constant_dynamic-slice_fusion = (bf16[2048,128]{1,0:T(8,128)(2,1)S(1)}, bf16[2048,128]{1,0:T(8,128)(2,1)S(1)}) fusion(bf16[2048,1024]{1,0:T(8,128)(2,1)} %param.16, s32[]{:T(128)S(6)} %select_n.41, bf16[2048,1024]{1,0:T(8,128)(2,1)} %param.15), kind=kLoop, calls=%fused_computation.29 | loop fusion | bytes 2097156 | tf_op jit(solution)/shard_map/dynamic_slice | solution.py:577
  8.7 0.0 slice-start
  8.7 1.2 %prepare.1 = (bf16[2,2048,128]{2,1,0:T(8,128)(2,1)S(1)}, bf16[2,1536,128]{2,1,0:T(8,128)(2,1)}) custom-call(bf16[2048,128]{1,0:T(8,128)(2,1)S(1)} %get-tuple-element.66.keys, bf16[2048,128]{1,0:T(8,128)(2,1)S(1)} %get-tuple-element.65.values), custom_call_target="tpu_custom_call" | custom-call | tf_op jit(solution)/shard_map/prepare/pallas_call | solution.py:110
  9.8 0.9 %collective-permute-start.12 = (bf16[2,1536,128]{2,1,0:T(8,128)(2,1)}, bf16[2,1536,128]{2,1,0:T(8,128)(2,1)}, u32[]{:S(2)}, u32[]{:S(2)}) collective-permute-start(bf16[2,1536,128]{2,1,0:T(8,128)(2,1)} %get-tuple-element.43), channel_id=1, source_target_pairs={{0,1},{1,0},{2,3},{3,2},{4,5},{5,4},{6,7},{7,6},{8,9},{9,8},{10,11... | collective-permute-start | bytes 2359304 | tf_op jit(solution)/shard_map/ppermute | solution.py:50
  11.4 0.6 sine_multiply_fusion
  12.1 0.0 collective-permute-done
  12.1 1.3 %collective-permute-done.2 = bf16[8,2048]{1,0:T(8,128)(2,1)S(1)} collective-permute-done((bf16[8,2048]{1,0:T(8,128)(2,1)}, bf16[8,2048]{1,0:T(8,128)(2,1)S(1)}, u32[]{:S(2)}, u32[]{:S(2)}) %collective-permute-start.2) | collective-permute-done | bytes 32800 | tf_op jit(solution)/shard_map/ppermute | solution.py:50
  13.4 0.8 %pad_maximum_fusion.2.refs_0_ = bf16[4,8,2048]{2,1,0:T(8,128)(2,1)S(1)} fusion(bf16[1,8,2048]{2,1,0:T(8,128)(2,1)S(1)} %bitcast.18, bf16[1,8,2048]{2,1,0:T(8,128)(2,1)S(1)} %slice_bitcast_fusion, bf16[1,8,2048]{2,1,0:T(8,128)(2,1)S(1)} %bitcast.17, bf16[1,8,2048]{2,1,0:T(8,128)(2,1)} %bitcast.16), kind=kLoop, calls=%fused_computation.12 | loop fusion | flops 196608 | bytes 262144 | tf_op jit(solution)/shard_map/stack | solution.py:582
  14.2 1.6 %collective-permute-start.4 = (bf16[4,8,2048]{2,1,0:T(8,128)(2,1)S(1)}, bf16[4,8,2048]{2,1,0:T(8,128)(2,1)S(1)}, u32[]{:S(2)}, u32[]{:S(2)}) collective-permute-start(bf16[4,8,2048]{2,1,0:T(8,128)(2,1)S(1)} %pad_maximum_fusion.2.refs_0_), channel_id=1, source_target_pairs={{0,8},{4,12},{8,0},{12,4},{16,24},{20,28},{24,16},{28,20},{1,9},{5... | collective-permute-start | bytes 393224 | tf_op jit(solution)/shard_map/ppermute | solution.py:50
  15.7 1.5 %collective-permute-start.6 = (bf16[4,8,2048]{2,1,0:T(8,128)(2,1)S(1)}, bf16[4,8,2048]{2,1,0:T(8,128)(2,1)S(1)}, u32[]{:S(2)}, u32[]{:S(2)}) collective-permute-start(bf16[4,8,2048]{2,1,0:T(8,128)(2,1)S(1)} %pad_maximum_fusion.2.refs_0_), channel_id=1, source_target_pairs={{0,16},{4,20},{8,24},{12,28},{16,0},{20,4},{24,8},{28,12},{1,17},{... | collective-permute-start | bytes 393224 | tf_op jit(solution)/shard_map/ppermute | solution.py:50
  17.3 0.5 collective-permute-start.8
  17.7 1.3 %constant_dynamic-slice_fusion.2 = (bf16[2048,128]{1,0:T(8,128)(2,1)S(1)}, bf16[2048,128]{1,0:T(8,128)(2,1)S(1)}) fusion(bf16[2048,1024]{1,0:T(8,128)(2,1)} %param.14, s32[]{:T(128)S(6)} %select_n.41, bf16[2048,1024]{1,0:T(8,128)(2,1)} %param.13), kind=kLoop, calls=%fused_computation.31 | loop fusion | bytes 2097156 | tf_op jit(solution)/shard_map/dynamic_slice | solution.py:597
  19.0 1.1 %collective-permute-done.4.refs_2_ = bf16[4,8,2048]{2,1,0:T(8,128)(2,1)S(1)} collective-permute-done((bf16[4,8,2048]{2,1,0:T(8,128)(2,1)S(1)}, bf16[4,8,2048]{2,1,0:T(8,128)(2,1)S(1)}, u32[]{:S(2)}, u32[]{:S(2)}) %collective-permute-start.4) | collective-permute-done | bytes 131104 | tf_op jit(solution)/shard_map/ppermute | solution.py:50
  20.2 0.0 collective-permute-start.5
  20.2 1.3 %collective-permute-done.6.refs_4_ = bf16[4,8,2048]{2,1,0:T(8,128)(2,1)S(1)} collective-permute-done((bf16[4,8,2048]{2,1,0:T(8,128)(2,1)S(1)}, bf16[4,8,2048]{2,1,0:T(8,128)(2,1)S(1)}, u32[]{:S(2)}, u32[]{:S(2)}) %collective-permute-start.6) | collective-permute-done | bytes 131104 | tf_op jit(solution)/shard_map/ppermute | solution.py:50
  21.4 1.7 %collective-permute-done.8.refs_6_ = bf16[4,8,2048]{2,1,0:T(8,128)(2,1)S(1)} collective-permute-done((bf16[4,8,2048]{2,1,0:T(8,128)(2,1)S(1)}, bf16[4,8,2048]{2,1,0:T(8,128)(2,1)S(1)}, u32[]{:S(2)}, u32[]{:S(2)}) %collective-permute-start.8) | collective-permute-done | bytes 131104 | tf_op jit(solution)/shard_map/ppermute | solution.py:50
  23.1 0.3 pad_maximum_fusion.refs_8_
  23.4 1.0 %collective-permute-done.9.refs_7_ = bf16[4,8,2048]{2,1,0:T(8,128)(2,1)S(1)} collective-permute-done((bf16[4,8,2048]{2,1,0:T(8,128)(2,1)S(1)}, bf16[4,8,2048]{2,1,0:T(8,128)(2,1)S(1)}, u32[]{:S(2)}, u32[]{:S(2)}) %collective-permute-start.9) | collective-permute-done | bytes 131104 | tf_op jit(solution)/shard_map/ppermute | solution.py:50
  24.5 1.0 %gather.1 = (bf16[256,2048]{1,0:T(8,128)(2,1)S(1)}, f32[2,64,1024]{2,1,0:T(8,128)S(1)}, f32[2,64,1024]{2,1,0:T(8,128)S(1)}) custom-call(bf16[4,8,2048]{2,1,0:T(8,128)(2,1)S(1)} %pad_maximum_fusion.2.refs_0_, bf16[4,8,2048]{2,1,0:T(8,128)(2,1)S(1)} %collective-permute-done.3.refs_1_, bf16[4,8,2048]{2,1,0:T(8,128)(2,1)S(1)} %collective-permute-done.4.refs_2_, ...), custom_call_target="tpu_custom_call" | custom-call | flops 1073741824 | bytes 2097152 | tf_op jit(solution)/shard_map/gather/pallas_call | solution.py:235
  25.5 0.0 copy-start.1
  25.5 0.0 copy-start.2
  25.5 1.2 %project.1 = (f32[2,64,512]{2,1,0:T(8,128)S(1)}, f32[2,64,512]{2,1,0:T(8,128)S(1)}) custom-call(bf16[256,2048]{1,0:T(8,128)(2,1)S(1)} %get-tuple-element.44.tokens, bf16[2048,1024]{1,0:T(8,128)(2,1)S(1)} %copy-done), custom_call_target="tpu_custom_call" | custom-call | flops 536870912 | bytes 2097152 | tf_op jit(solution)/shard_map/project/pallas_call | solution.py:264
  26.8 0.7 collective-permute-start.13
  27.5 1.5 %collective-permute-start.10 = (f16[2,64,1024]{2,1,0:T(8,128)(2,1)S(1)}, f16[2,64,1024]{2,1,0:T(8,128)(2,1)S(1)}, u32[]{:S(2)}, u32[]{:S(2)}) collective-permute-start(f16[2,64,1024]{2,1,0:T(8,128)(2,1)S(1)} %multiply_convert_fusion), channel_id=1, source_target_pairs={{0,1},{1,0},{2,3},{3,2},{4,5},{5,4},{6,7},{7,6},{8,9},{9,8},{10,11... | collective-permute-start | bytes 786440 | tf_op jit(solution)/shard_map/ppermute | solution.py:50
  29.0 0.1 pad_add_fusion.ids
  29.1 1.5 %mask.1.bias = f32[4224,128]{1,0:T(8,128)S(1)} custom-call(s32[4]{0:T(128)S(1)} %pad_add_fusion.ids, s32[16]{0:T(128)S(1)} %copy-done.2, s32[1,64]{1,0:T(1,128)S(1)} %copy-done.1, bf16[8,128]{1,0:T(8,128)(2,1)S(1)} %slice.80.refs_0_), custom_call_target="tpu_custom_call" | custom-call | tf_op jit(solution)/shard_map/mask/pallas_call | solution.py:195
  30.6 2.6 %collective-permute-done.13 = f16[2,64,512]{2,1,0:T(8,128)(2,1)S(1)} collective-permute-done((f16[2,64,512]{2,1,0:T(8,128)(2,1)S(1)}, f16[2,64,512]{2,1,0:T(8,128)(2,1)S(1)}, u32[]{:S(2)}, u32[]{:S(2)}) %collective-permute-start.13) | collective-permute-done | bytes 131104 | tf_op jit(solution)/shard_map/ppermute | solution.py:50
  33.2 0.1 multiply_convert_fusion.1
  33.2 2.8 %collective-permute-start.16 = (f16[2,64,512]{2,1,0:T(8,128)(2,1)S(1)}, f16[2,64,512]{2,1,0:T(8,128)(2,1)S(1)}, u32[]{:S(2)}, u32[]{:S(2)}) collective-permute-start(f16[2,64,512]{2,1,0:T(8,128)(2,1)S(1)} %get-tuple-element.53), channel_id=1, source_target_pairs={{0,2},{1,3},{2,0},{3,1},{4,6},{5,7},{6,4},{7,5},{8,10},{9,11},{10,... | collective-permute-start | bytes 393224 | tf_op jit(solution)/shard_map/ppermute | solution.py:50
  36.0 0.2 collective-permute-start.14
  36.2 5.3 %collective-permute-done.10 = f16[2,64,1024]{2,1,0:T(8,128)(2,1)S(1)} collective-permute-done((f16[2,64,1024]{2,1,0:T(8,128)(2,1)S(1)}, f16[2,64,1024]{2,1,0:T(8,128)(2,1)S(1)}, u32[]{:S(2)}, u32[]{:S(2)}) %collective-permute-start.10) | collective-permute-done | bytes 262176 | tf_op jit(solution)/shard_map/ppermute | solution.py:50
  41.6 0.1 multiply_add_fusion
  41.8 0.1 pad_maximum_fusion.1
  41.9 1.7 %collective-permute-start.11 = (f16[2,64,768]{2,1,0:T(8,128)(2,1)S(1)}, f16[2,64,768]{2,1,0:T(8,128)(2,1)S(1)}, u32[]{:S(2)}, u32[]{:S(2)}) collective-permute-start(f16[2,64,768]{2,1,0:T(8,128)(2,1)S(1)} %pad_maximum_fusion.1), channel_id=1, source_target_pairs={{0,2},{1,3},{2,0},{3,1},{4,6},{5,7},{6,4},{7,5},{8,10},{9,11},{10,... | collective-permute-start | bytes 589832 | tf_op jit(solution)/shard_map/ppermute | solution.py:50
  43.6 5.8 %collective-permute-done.11 = f16[2,64,768]{2,1,0:T(8,128)(2,1)S(1)} collective-permute-done((f16[2,64,768]{2,1,0:T(8,128)(2,1)S(1)}, f16[2,64,768]{2,1,0:T(8,128)(2,1)S(1)}, u32[]{:S(2)}, u32[]{:S(2)}) %collective-permute-start.11) | collective-permute-done | bytes 196640 | tf_op jit(solution)/shard_map/ppermute | solution.py:50
  49.5 1.3 %collective-permute-done.14.far_last = bf16[2,512,128]{2,1,0:T(8,128)(2,1)S(1)} collective-permute-done((bf16[2,512,128]{2,1,0:T(8,128)(2,1)S(1)}, bf16[2,512,128]{2,1,0:T(8,128)(2,1)S(1)}, u32[]{:S(2)}, u32[]{:S(2)}) %collective-permute-start.14) | collective-permute-done | bytes 262176 | tf_op jit(solution)/shard_map/ppermute | solution.py:50
  50.8 3.9 %attend.3 = (f32[1,64,512]{2,1,0:T(8,128)S(1)}, bf16[1,64,640]{2,1,0:T(8,128)(2,1)S(1)}, f32[1,64,128]{2,1,0:T(8,128)S(1)}) custom-call(f32[2,64,512]{2,1,0:T(8,128)S(1)} %maximum_add_fusion.1.q, f32[2,64,256]{2,1,0:T(8,128)S(1)} %pad_maximum_fusion.3.kv, f32[4,64,128]{2,1,0:T(8,128)S(1)} %get-tuple-element.64.cosine, ...), custom_call_target="tpu_custom_call" | custom-call | flops 4429185024 | bytes 1048576 | tf_op jit(solution)/shard_map/attend/pallas_call | solution.py:401
  54.7 1.8 %collective-permute-start.17 = (bf16[1,64,640]{2,1,0:T(8,128)(2,1)S(1)}, bf16[1,64,640]{2,1,0:T(8,128)(2,1)S(1)}, u32[]{:S(2)}, u32[]{:S(2)}) collective-permute-start(bf16[1,64,640]{2,1,0:T(8,128)(2,1)S(1)} %get-tuple-element.51), channel_id=1, source_target_pairs={{0,2},{1,3},{2,0},{3,1},{4,6},{5,7},{6,4},{7,5},{8,10},{9,11},{10,... | collective-permute-start | bytes 245768 | tf_op jit(solution)/shard_map/ppermute | solution.py:50
  56.5 3.9 %attend.2 = (f32[1,64,512]{2,1,0:T(8,128)S(1)}, bf16[1,64,640]{2,1,0:T(8,128)(2,1)S(1)}, f32[1,64,128]{2,1,0:T(8,128)S(1)}) custom-call(f32[2,64,512]{2,1,0:T(8,128)S(1)} %maximum_add_fusion.q, f32[2,64,256]{2,1,0:T(8,128)S(1)} %pad_maximum_fusion.3.kv, f32[4,64,128]{2,1,0:T(8,128)S(1)} %get-tuple-element.64.cosine, ...), custom_call_target="tpu_custom_call" | custom-call | flops 4429185024 | bytes 1048576 | tf_op jit(solution)/shard_map/attend/pallas_call | solution.py:401
  60.4 1.3 %collective-permute-start.15 = (bf16[1,64,640]{2,1,0:T(8,128)(2,1)S(1)}, bf16[1,64,640]{2,1,0:T(8,128)(2,1)S(1)}, u32[]{:S(2)}, u32[]{:S(2)}) collective-permute-start(bf16[1,64,640]{2,1,0:T(8,128)(2,1)S(1)} %get-tuple-element.48), channel_id=1, source_target_pairs={{0,2},{1,3},{2,0},{3,1},{4,6},{5,7},{6,4},{7,5},{8,10},{9,11},{10,... | collective-permute-start | bytes 245768 | tf_op jit(solution)/shard_map/ppermute | solution.py:50
  61.7 4.1 %collective-permute-done.15.refs_1_ = bf16[1,64,640]{2,1,0:T(8,128)(2,1)S(1)} collective-permute-done((bf16[1,64,640]{2,1,0:T(8,128)(2,1)S(1)}, bf16[1,64,640]{2,1,0:T(8,128)(2,1)S(1)}, u32[]{:S(2)}, u32[]{:S(2)}) %collective-permute-start.15) | collective-permute-done | bytes 81952 | tf_op jit(solution)/shard_map/ppermute | solution.py:50
  65.8 0.4 finish.1
  66.2 9.5 %all_to_all.5 = bf16[8,8,1024]{2,1,0:T(8,128)(2,1)S(1)} all-to-all(bf16[8,8,1024]{2,1,0:T(8,128)(2,1)S(1)} %finish.1), channel_id=1, replica_groups=mesh['wide'=8,'blk'=4] {'wide'}, dimensions={0} | all-to-all | bytes 262144 | tf_op jit(solution)/shard_map/all_to_all | solution.py:659
  75.7 0.7 copy.13
  (36 shorter events, 0.4 us)
Async XLA Ops:
  1.8 10.3 %collective-permute-start.1 = (bf16[8,2176]{1,0:T(8,128)(2,1)}, bf16[8,2176]{1,0:T(8,128)(2,1)S(1)}, u32[]{:S(2)}, u32[]{:S(2)}) collective-permute-start(bf16[8,2176]{1,0:T(8,128)(2,1)} %get-tuple-element.31), channel_id=1, source_target_pairs={{0,2},{1,3},{2,0},{3,1},{4,6},{5,7},{6,4},{7,5},{8,10},{9,11},{10,... | collective-permute-start | bytes 104456 | tf_op jit(solution)/shard_map/ppermute | solution.py:50
  5.8 6.3 %collective-permute-start = (bf16[8,2048]{1,0:T(8,128)(2,1)}, bf16[8,2048]{1,0:T(8,128)(2,1)S(1)}, u32[]{:S(2)}, u32[]{:S(2)}) collective-permute-start(bf16[8,2048]{1,0:T(8,128)(2,1)} %get-tuple-element.30), channel_id=1, source_target_pairs={{0,1},{1,0},{2,3},{3,2},{4,5},{5,4},{6,7},{7,6},{8,9},{9,8},{10,11... | collective-permute-start | bytes 98312 | tf_op jit(solution)/shard_map/ppermute | solution.py:50
  7.4 6.0 %collective-permute-start.2 = (bf16[8,2048]{1,0:T(8,128)(2,1)}, bf16[8,2048]{1,0:T(8,128)(2,1)S(1)}, u32[]{:S(2)}, u32[]{:S(2)}) collective-permute-start(bf16[8,2048]{1,0:T(8,128)(2,1)} %get-tuple-element.32), channel_id=1, source_target_pairs={{0,3},{1,2},{2,1},{3,0},{4,7},{5,6},{6,5},{7,4},{8,11},{9,10},{10,... | collective-permute-start | bytes 98312 | tf_op jit(solution)/shard_map/ppermute | solution.py:50
  8.7 14.5 %slice-start = ((bf16[2048,1024]{1,0:T(8,128)(2,1)}), bf16[2048,512]{1,0:T(8,128)(2,1)S(1)}, s32[]{:S(2)}) async-start(bf16[2048,1024]{1,0:T(8,128)(2,1)} %weights.1), calls=%async_computation.1 | async-start | bytes 4194304 | tf_op jit(solution)/shard_map/slice | solution.py:595
  9.8 41.0 %collective-permute-start.12 = (bf16[2,1536,128]{2,1,0:T(8,128)(2,1)}, bf16[2,1536,128]{2,1,0:T(8,128)(2,1)}, u32[]{:S(2)}, u32[]{:S(2)}) collective-permute-start(bf16[2,1536,128]{2,1,0:T(8,128)(2,1)} %get-tuple-element.43), channel_id=1, source_target_pairs={{0,1},{1,0},{2,3},{3,2},{4,5},{5,4},{6,7},{7,6},{8,9},{9,8},{10,11... | collective-permute-start | bytes 2359304 | tf_op jit(solution)/shard_map/ppermute | solution.py:50
  14.2 6.0 %collective-permute-start.4 = (bf16[4,8,2048]{2,1,0:T(8,128)(2,1)S(1)}, bf16[4,8,2048]{2,1,0:T(8,128)(2,1)S(1)}, u32[]{:S(2)}, u32[]{:S(2)}) collective-permute-start(bf16[4,8,2048]{2,1,0:T(8,128)(2,1)S(1)} %pad_maximum_fusion.2.refs_0_), channel_id=1, source_target_pairs={{0,8},{4,12},{8,0},{12,4},{16,24},{20,28},{24,16},{28,20},{1,9},{5... | collective-permute-start | bytes 393224 | tf_op jit(solution)/shard_map/ppermute | solution.py:50
  15.7 5.7 %collective-permute-start.6 = (bf16[4,8,2048]{2,1,0:T(8,128)(2,1)S(1)}, bf16[4,8,2048]{2,1,0:T(8,128)(2,1)S(1)}, u32[]{:S(2)}, u32[]{:S(2)}) collective-permute-start(bf16[4,8,2048]{2,1,0:T(8,128)(2,1)S(1)} %pad_maximum_fusion.2.refs_0_), channel_id=1, source_target_pairs={{0,16},{4,20},{8,24},{12,28},{16,0},{20,4},{24,8},{28,12},{1,17},{... | collective-permute-start | bytes 393224 | tf_op jit(solution)/shard_map/ppermute | solution.py:50
  17.3 5.9 %collective-permute-start.8 = (bf16[4,8,2048]{2,1,0:T(8,128)(2,1)S(1)}, bf16[4,8,2048]{2,1,0:T(8,128)(2,1)S(1)}, u32[]{:S(2)}, u32[]{:S(2)}) collective-permute-start(bf16[4,8,2048]{2,1,0:T(8,128)(2,1)S(1)} %pad_maximum_fusion.2.refs_0_), channel_id=1, source_target_pairs={{0,24},{4,28},{8,16},{12,20},{16,8},{20,12},{24,0},{28,4},{1,25},{... | collective-permute-start | bytes 393224 | tf_op jit(solution)/shard_map/ppermute | solution.py:50
  17.7 5.7 %collective-permute-start.3 = (bf16[4,8,2048]{2,1,0:T(8,128)(2,1)S(1)}, bf16[4,8,2048]{2,1,0:T(8,128)(2,1)S(1)}, u32[]{:S(2)}, u32[]{:S(2)}) collective-permute-start(bf16[4,8,2048]{2,1,0:T(8,128)(2,1)S(1)} %pad_maximum_fusion.2.refs_0_), channel_id=1, source_target_pairs={{0,4},{4,0},{8,12},{12,8},{16,20},{20,16},{24,28},{28,24},{1,5},{5... | collective-permute-start | bytes 393224 | tf_op jit(solution)/shard_map/ppermute | solution.py:50
  20.2 3.2 %collective-permute-start.5 = (bf16[4,8,2048]{2,1,0:T(8,128)(2,1)S(1)}, bf16[4,8,2048]{2,1,0:T(8,128)(2,1)S(1)}, u32[]{:S(2)}, u32[]{:S(2)}) collective-permute-start(bf16[4,8,2048]{2,1,0:T(8,128)(2,1)S(1)} %collective-permute-done.4.refs_2_), channel_id=1, source_target_pairs={{0,4},{4,0},{8,12},{12,8},{16,20},{20,16},{24,28},{28,24},{1,5},{5... | collective-permute-start | bytes 393224 | tf_op jit(solution)/shard_map/ppermute | solution.py:50
  21.4 2.0 %collective-permute-start.7 = (bf16[4,8,2048]{2,1,0:T(8,128)(2,1)S(1)}, bf16[4,8,2048]{2,1,0:T(8,128)(2,1)S(1)}, u32[]{:S(2)}, u32[]{:S(2)}) collective-permute-start(bf16[4,8,2048]{2,1,0:T(8,128)(2,1)S(1)} %collective-permute-done.6.refs_4_), channel_id=1, source_target_pairs={{0,4},{4,0},{8,12},{12,8},{16,20},{20,16},{24,28},{28,24},{1,5},{5... | collective-permute-start | bytes 393224 | tf_op jit(solution)/shard_map/ppermute | solution.py:50
  23.1 1.3 %collective-permute-start.9 = (bf16[4,8,2048]{2,1,0:T(8,128)(2,1)S(1)}, bf16[4,8,2048]{2,1,0:T(8,128)(2,1)S(1)}, u32[]{:S(2)}, u32[]{:S(2)}) collective-permute-start(bf16[4,8,2048]{2,1,0:T(8,128)(2,1)S(1)} %collective-permute-done.8.refs_6_), channel_id=1, source_target_pairs={{0,4},{4,0},{8,12},{12,8},{16,20},{20,16},{24,28},{28,24},{1,5},{5... | collective-permute-start | bytes 393224 | tf_op jit(solution)/shard_map/ppermute | solution.py:50
  23.1 2.4 %copy-start = (bf16[2048,1024]{1,0:T(8,128)(2,1)S(1)}, bf16[2048,1024]{1,0:T(8,128)(2,1)}, u32[]{:S(2)}) copy-start(bf16[2048,1024]{1,0:T(8,128)(2,1)} %weights.1) | copy-start | bytes 12582916
  25.5 3.6 %copy-start.1 = (s32[1,64]{1,0:T(1,128)S(1)}, s32[1,64]{1,0:T(1,128)}, u32[]{:S(2)}) copy-start(s32[1,64]{1,0:T(1,128)} %reach.3) | copy-start | bytes 772
  25.5 3.6 %copy-start.2 = (s32[16]{0:T(128)S(1)}, s32[16]{0:T(128)}, u32[]{:S(2)}) copy-start(s32[16]{0:T(128)} %passkey.1) | copy-start | bytes 196
  26.8 6.4 %collective-permute-start.13 = (f16[2,64,512]{2,1,0:T(8,128)(2,1)S(1)}, f16[2,64,512]{2,1,0:T(8,128)(2,1)S(1)}, u32[]{:S(2)}, u32[]{:S(2)}) collective-permute-start(f16[2,64,512]{2,1,0:T(8,128)(2,1)S(1)} %multiply_convert_fusion.2), channel_id=1, source_target_pairs={{0,1},{1,0},{2,3},{3,2},{4,5},{5,4},{6,7},{7,6},{8,9},{9,8},{10,11... | collective-permute-start | bytes 393224 | tf_op jit(solution)/shard_map/ppermute | solution.py:50
  27.5 14.1 %collective-permute-start.10 = (f16[2,64,1024]{2,1,0:T(8,128)(2,1)S(1)}, f16[2,64,1024]{2,1,0:T(8,128)(2,1)S(1)}, u32[]{:S(2)}, u32[]{:S(2)}) collective-permute-start(f16[2,64,1024]{2,1,0:T(8,128)(2,1)S(1)} %multiply_convert_fusion), channel_id=1, source_target_pairs={{0,1},{1,0},{2,3},{3,2},{4,5},{5,4},{6,7},{7,6},{8,9},{9,8},{10,11... | collective-permute-start | bytes 786440 | tf_op jit(solution)/shard_map/ppermute | solution.py:50
  33.2 8.5 %collective-permute-start.16 = (f16[2,64,512]{2,1,0:T(8,128)(2,1)S(1)}, f16[2,64,512]{2,1,0:T(8,128)(2,1)S(1)}, u32[]{:S(2)}, u32[]{:S(2)}) collective-permute-start(f16[2,64,512]{2,1,0:T(8,128)(2,1)S(1)} %get-tuple-element.53), channel_id=1, source_target_pairs={{0,2},{1,3},{2,0},{3,1},{4,6},{5,7},{6,4},{7,5},{8,10},{9,11},{10,... | collective-permute-start | bytes 393224 | tf_op jit(solution)/shard_map/ppermute | solution.py:50
  36.0 14.8 %collective-permute-start.14 = (bf16[2,512,128]{2,1,0:T(8,128)(2,1)S(1)}, bf16[2,512,128]{2,1,0:T(8,128)(2,1)S(1)}, u32[]{:S(2)}, u32[]{:S(2)}) collective-permute-start(bf16[2,512,128]{2,1,0:T(8,128)(2,1)S(1)} %rest.1), channel_id=1, source_target_pairs={{0,1},{1,0},{2,3},{3,2},{4,5},{5,4},{6,7},{7,6},{8,9},{9,8},{10,11... | collective-permute-start | bytes 786440 | tf_op jit(solution)/shard_map/ppermute | solution.py:50
  41.9 7.5 %collective-permute-start.11 = (f16[2,64,768]{2,1,0:T(8,128)(2,1)S(1)}, f16[2,64,768]{2,1,0:T(8,128)(2,1)S(1)}, u32[]{:S(2)}, u32[]{:S(2)}) collective-permute-start(f16[2,64,768]{2,1,0:T(8,128)(2,1)S(1)} %pad_maximum_fusion.1), channel_id=1, source_target_pairs={{0,2},{1,3},{2,0},{3,1},{4,6},{5,7},{6,4},{7,5},{8,10},{9,11},{10,... | collective-permute-start | bytes 589832 | tf_op jit(solution)/shard_map/ppermute | solution.py:50
  54.7 6.9 %collective-permute-start.17 = (bf16[1,64,640]{2,1,0:T(8,128)(2,1)S(1)}, bf16[1,64,640]{2,1,0:T(8,128)(2,1)S(1)}, u32[]{:S(2)}, u32[]{:S(2)}) collective-permute-start(bf16[1,64,640]{2,1,0:T(8,128)(2,1)S(1)} %get-tuple-element.51), channel_id=1, source_target_pairs={{0,2},{1,3},{2,0},{3,1},{4,6},{5,7},{6,4},{7,5},{8,10},{9,11},{10,... | collective-permute-start | bytes 245768 | tf_op jit(solution)/shard_map/ppermute | solution.py:50
  60.4 5.4 %collective-permute-start.15 = (bf16[1,64,640]{2,1,0:T(8,128)(2,1)S(1)}, bf16[1,64,640]{2,1,0:T(8,128)(2,1)S(1)}, u32[]{:S(2)}, u32[]{:S(2)}) collective-permute-start(bf16[1,64,640]{2,1,0:T(8,128)(2,1)S(1)} %get-tuple-element.48), channel_id=1, source_target_pairs={{0,2},{1,3},{2,0},{3,1},{4,6},{5,7},{6,4},{7,5},{8,10},{9,11},{10,... | collective-permute-start | bytes 245768 | tf_op jit(solution)/shard_map/ppermute | solution.py:50
